TPU v7x, 1024 devices: a whole 8x8x8 slice. The times are simulated.
1024 devices in a mesh: row: 64 (over y, x), col: 8 (over z), split: 2 (over core).
Axes of the slice: x: 8, y: 8, z: 8, core: 2. Of those that a mesh axis runs over, the one named last changes fastest.
Arguments:
- coefficients: bfloat16 [16384, 6144], P(('row', 'col', 'split')), may hold values from -0.796875 to 0.796875
- row_weight: float32 [16384], P(('row', 'col', 'split')), may hold values from 0.1 to 1
- pattern: int32 [128, 48], replicated, may hold values 0 or 1
- aux_sizes: int32 [48], replicated, may hold values from 32 to 128
Outputs:
- response: float32 [6144, 6144], P(('row', 'split'), 'col')
All inputs are finite; a program needn't handle non-finite values.
Results may differ from a plain program's by a relative error of at most 0.0015.
Values may be sent and summed in bfloat16 or wider, within the bound.
No kernel may reach another device: no remote copies, remote signals or barrier semaphores. Data moves between devices by JAX's collectives and lax.ppermute only.
A program may use at most 64 MiB of HBM per device.

v0:
```python
import jax
import jax.numpy as jnp
from jax import lax
from jax.sharding import PartitionSpec as P

PAIR_ROWS = 128
AUX_PAD = 128


def local_operands(coefficients, row_weight, pattern, aux_sizes):
    rows, width = coefficients.shape
    device = lax.axis_index(("row", "col", "split"))
    global_rows = device * rows + jnp.arange(rows, dtype=jnp.int32)
    blocks = global_rows // PAIR_ROWS
    pat_rows = jnp.take(pattern, blocks, axis=0)
    column = jnp.arange(AUX_PAD, dtype=jnp.int32)
    col_mask = (column[None, :] < aux_sizes[:, None]).astype(jnp.int32)
    valid = (pat_rows[:, :, None] * col_mask[None, :, :]).reshape(rows, width)
    masked = coefficients * valid.astype(coefficients.dtype)
    scaled = (row_weight[:, None] * masked.astype(jnp.float32)).astype(jnp.bfloat16)
    return (masked, scaled)


def contract_rows(first, second):
    return lax.dot_general(
        first, second, (((0,), (0,)), ((), ())), preferred_element_type=jnp.float32
    )


def per_device(coefficients, row_weight, pattern, aux_sizes):
    masked, scaled = local_operands(coefficients, row_weight, pattern, aux_sizes)
    n_row = lax.axis_size("row")
    n_col = lax.axis_size("col")
    local_rows = masked.shape[0]
    right = lax.all_to_all(scaled, "col", split_axis=1, concat_axis=0, tiled=True)
    right = lax.all_gather(right, "row", axis=0, tiled=True)
    right_width = right.shape[1]
    left = lax.all_to_all(masked, "row", split_axis=1, concat_axis=0, tiled=True)
    aligned = right.reshape(n_row, n_col, local_rows, right_width)
    aligned = aligned.transpose(1, 0, 2, 3).reshape(n_col * n_row * local_rows, right_width)
    partial_sum = contract_rows(lax.all_gather(left, "col", axis=0, tiled=True), aligned)
    response = lax.psum_scatter(partial_sum, "split", scatter_dimension=0, tiled=True)
    return response


def solution(mesh):
    placed = (P(("row", "col", "split"), None), P(("row", "col", "split")), P(), P())
    return jax.shard_map(
        per_device,
        mesh=mesh,
        in_specs=placed,
        out_specs=P(("row", "split"), "col"),
        check_vma=False,
    )
```

profile of v0, /device:TPU:1, one launch (start us, length us, event | category | flops | bytes accessed | tf_op | source)
XLA Modules:
  0.0 243.4 jit_solution(18404013522180351944)
XLA Ops:
  6.5 0.0 all-gather.5.cloned.1.call-start
  6.6 0.8 lt.40
  7.4 0.8 copy.13
  8.2 0.6 gather_fusion
  8.8 0.1 broadcast_select_fusion
  8.8 0.2 mul.39
  9.0 1.1 multiply_convert_fusion
  10.1 25.9 %all_to_all.38 = bf16[16,8,768]{2,0,1:T(8,128)(2,1)} all-to-all(bf16[16,8,768]{2,0,1:T(8,128)(2,1)S(1)} %bitcast.37), channel_id=1, replica_groups=mesh['row'=64,'col'=8,'split'=2] {'col'}, dimensions={1} | all-to-all | bytes 393216 | tf_op jit(solution)/shard_map/all_to_all | solution.py:35
  36.1 0.0 all-gather.5.cloned.1.call-update
  36.1 0.0 all-gather.3.cloned.1.call-start
  36.2 0.3 all_to_all.28
  36.4 0.2 copy.14
  36.6 25.7 %all_to_all.39 = bf16[16,64,96]{2,0,1:T(8,128)(2,1)} all-to-all(bf16[16,64,96]{2,0,1:T(8,128)(2,1)S(1)} %copy.14), channel_id=1, replica_groups=mesh['row'=64,'col'=8,'split'=2] {'row'}, dimensions={1} | all-to-all | bytes 393216 | tf_op jit(solution)/shard_map/all_to_all | solution.py:38
  62.3 0.0 all-gather.3.cloned.1.call-update
  62.3 0.0 reduce-scatter.2.cloned.1.call-start
  62.4 96.8 %all-gather.5.cloned.1.call-done = bf16[8192,768]{1,0:T(8,128)(2,1)} async-done(((bf16[128,768]{1,0:T(8,128)(2,1)}), bf16[8192,768]{1,0:T(8,128)(2,1)}) %all-gather.5.cloned.1.call-update) | async-done | bytes 12582928 | tf_op jit(solution)/shard_map/all_gather | solution.py:36
  159.2 10.9 %copy.16 = bf16[64,8,16,768]{3,2,0,1:T(8,128)(2,1)} copy(bf16[64,8,16,768]{3,2,1,0:T(8,128)(2,1)} %bitcast.32) | data formatting | bytes 25165824 | tf_op jit(solution)/shard_map/reshape | solution.py:39
  170.1 35.6 %all-gather.3.cloned.1.call-done = bf16[8192,96]{1,0:T(8,128)(2,1)} async-done(((bf16[1024,96]{1,0:T(8,128)(2,1)}), bf16[8192,96]{1,0:T(8,128)(2,1)}) %all-gather.3.cloned.1.call-update) | async-done | bytes 1572880 | tf_op jit(solution)/shard_map/all_gather | solution.py:41
  205.7 7.8 %fusion.5 = f32[96,768]{1,0:T(8,128)} fusion(bf16[8192,96]{1,0:T(8,128)(2,1)} %all-gather.3.cloned.1.call-done, bf16[8192,768]{1,0:T(8,128)(2,1)} %bitcast.31), kind=kOutput, calls=%fused_computation.22 | convolution fusion | flops 1207959552 | bytes 14450688 | tf_op jit(solution)/shard_map/dot_general | solution.py:25
  213.5 0.0 reduce-scatter.2.cloned.1.call-update
  213.5 23.4 %reduce-scatter.2.cloned.1.call-done = f32[48,768]{1,0:T(8,128)} async-done(((f32[96,768]{1,0:T(8,128)}), f32[48,768]{1,0:T(8,128)}) %reduce-scatter.2.cloned.1.call-update) | async-done | bytes 147472 | tf_op jit(solution)/shard_map/reduce_scatter | solution.py:42
  (5 shorter events, 0.1 us)
Async XLA Ops:
  6.5 152.7 %all-gather.5.cloned.1.call-start = ((), (), s32[]{:S(2)}) async-start(), calls=%async_computation.4 | async-start | bytes 12779520 | tf_op jit(solution)/shard_map/all_gather | solution.py:36
  36.1 169.6 %all-gather.3.cloned.1.call-start = ((), (), s32[]{:S(2)}) async-start(), calls=%async_computation.3 | async-start | bytes 2359296 | tf_op jit(solution)/shard_map/all_gather | solution.py:41
  62.3 174.5 %reduce-scatter.2.cloned.1.call-start = ((), (), s32[]{:S(2)}) async-start(), calls=%async_computation.5 | async-start | bytes 442368 | tf_op jit(solution)/shard_map/reduce_scatter | solution.py:42
Sparse Core Ops, SparseCore 0:
  36.2 122.9 all-gather.4
  161.8 43.8 all-gather.2
  213.6 23.2 reduce-scatter.1
where the time goes:
time: 244 us; the launch traced here: 243 us
  waiting for transfers between devices  156 us (64%)
  blocking collectives  51.6 us (21%)
  local copies, waits for them, and re-layouts  13.7 us (6%)
  between operations  13.2 us (5%)
  matrix products  7.76 us (3%)
    all_gather x1, waiting for transfers between devices, per_device(): right = lax.all_gather(right, 'row', axis=0, tiled=True)  96.8 us
    all_gather x1, waiting for transfers between devices, per_device(): lax.all_gather(left, 'col', axis=0, tiled=True)  35.6 us
    all_to_all x1, blocking collectives, per_device(): lax.all_to_all(scaled, 'col', split_axis=1, concat_axis=0, tiled=True)  25.9 us
    all_to_all x1, blocking collectives, per_device(): lax.all_to_all(masked, 'row', split_axis=1, concat_axis=0, tiled=True)  25.7 us
    reduce_scatter x1, waiting for transfers between devices, per_device(): lax.psum_scatter(partial_sum, 'split', scatter_dimension=0, tiled=True)  23.4 us
    reshape x1, local copies, waits for them, and re-layouts, per_device(): aligned = right.reshape(n_row, n_col, local_rows, right_width)  10.9 us
    dot_general x1, matrix products, contract_rows(): lax.dot_general(first, second, (((0,), (0,)), ((), ())), preferred_elemen...  7.76 us
  transfers between devices with their start and end apart: 3, of which 3 were waited for; matrix products, arithmetic and copies ran while one was open for 5% of the time, Pallas kernels for 0%

commit v1 on v0

v1 whole, which is shorter than its diff:
```python
import functools
import itertools

import jax
import jax.numpy as jnp
from jax import lax
from jax.experimental import pallas as pl
from jax.experimental.pallas import tpu as pltpu
from jax.sharding import Mesh, PartitionSpec as P

PAIR_ROWS = 128
AUX_PAD = 128
N = 8
AXES = ("y", "x", "z", "c")
SMEM = pl.BlockSpec(memory_space=pltpu.SMEM)
VMEM = pl.BlockSpec(memory_space=pltpu.VMEM)


def groups(first, second):
    found = []
    for core, axis in enumerate((first, second)):
        rest = [a for a in "yxz" if a != axis]
        for others in itertools.product(range(N), repeat=2):
            at = dict(zip(rest, others))
            ring = []
            for i in range(N):
                at[axis] = i
                ring.append(((at["y"] * N + at["x"]) * N + at["z"]) * 2 + core)
            found.append(ring)
    return found


def exchange(blocks, first, second):
    return lax.all_to_all(
        blocks, AXES, 0, 0, tiled=True, axis_index_groups=groups(first, second)
    )


def mask_kernel(coef_ref, weight_ref, pattern_ref, sizes_ref, one_ref, two_ref):
    rows, width = coef_ref.shape
    wide = width // N
    core = lax.axis_index("c")
    device = ((lax.axis_index("y") * N + lax.axis_index("x")) * N + lax.axis_index("z")) * 2 + core
    block = device * rows // PAIR_ROWS
    at_row = lax.broadcasted_iota(jnp.int32, (rows, AUX_PAD), 0)
    weight = jnp.zeros((rows, AUX_PAD), jnp.float32)
    for r in range(rows):
        weight = jnp.where(at_row == r, weight_ref[r], weight)
    lane = lax.broadcasted_iota(jnp.int32, (rows, AUX_PAD), 1)
    for atom in range(width // AUX_PAD):
        size = jnp.where(pattern_ref[block, atom] > 0, sizes_ref[atom], 0)
        coef = coef_ref[:, atom * AUX_PAD : (atom + 1) * AUX_PAD].astype(jnp.float32)
        masked = jnp.where(lane < size, coef, 0.0)
        scaled = weight * masked
        to, start = divmod(atom * AUX_PAD, wide)
        columns = slice(start, start + AUX_PAD)
        one_ref[to, :, columns] = jnp.where(core == 0, masked, scaled).astype(jnp.bfloat16)
        two_ref[to, :, columns] = jnp.where(core == 0, scaled, masked).astype(jnp.bfloat16)


def masked_and_scaled(coefficients, row_weight, pattern, aux_sizes):
    rows, width = coefficients.shape
    shape = jax.ShapeDtypeStruct((N, rows, width // N), jnp.bfloat16)
    return pl.pallas_call(
        mask_kernel,
        out_shape=(shape, shape),
        in_specs=[VMEM, SMEM, SMEM, SMEM],
        out_specs=(VMEM, VMEM),
        cost_estimate=pl.CostEstimate(flops=4 * rows * width, bytes_accessed=6 * rows * width, transcendentals=0),
    )(coefficients, row_weight, pattern, aux_sizes)


def contract_kernel(one_ref, two_ref, keep_ref, send_ref):
    wide = one_ref.shape[1]
    tile = 256
    high = wide // 2
    part = keep_ref.shape[1]
    groups_in_tile = high // (2 * part)
    core = lax.axis_index("c")

    def run(left_ref, right_ref, mine, theirs):
        for m in range(2):

            def column_tile(t, carry):
                start = pl.multiple_of(t * tile, tile)
                out = lax.dot_general(
                    left_ref[:, m * high : (m + 1) * high],
                    right_ref[:, pl.ds(start, tile)],
                    (((0,), (0,)), ((), ())),
                    preferred_element_type=jnp.float32,
                ).reshape(groups_in_tile, 2, part, tile)
                at = slice(m * groups_in_tile, (m + 1) * groups_in_tile)
                keep_ref[at, :, pl.ds(start, tile)] = out[:, mine]
                send_ref[at, :, pl.ds(start, tile)] = out[:, theirs]
                return carry

            lax.fori_loop(0, wide // tile, column_tile, 0)

    @pl.when(core == 0)
    def _():
        run(one_ref, two_ref, 0, 1)

    @pl.when(core == 1)
    def _():
        run(two_ref, one_ref, 1, 0)


def contract(one, two):
    depth, wide = one.shape
    shape = jax.ShapeDtypeStruct((N, wide // (2 * N), wide), jnp.float32)
    return pl.pallas_call(
        contract_kernel,
        out_shape=(shape, shape),
        in_specs=[VMEM, VMEM],
        out_specs=(VMEM, VMEM),
        compiler_params=pltpu.CompilerParams(vmem_limit_bytes=40 * 2**20),
        cost_estimate=pl.CostEstimate(
            flops=2 * depth * wide * wide, bytes_accessed=4 * depth * wide + 4 * wide * wide, transcendentals=0
        ),
    )(one, two)


def per_device(coefficients, row_weight, pattern, aux_sizes):
    one, two = masked_and_scaled(coefficients, row_weight, pattern, aux_sizes)
    rows, wide = one.shape[1:]
    one = exchange(one, "y", "z").reshape(N * rows, wide)
    one = lax.all_gather(one, AXES, axis=0, tiled=True, axis_index_groups=groups("z", "y"))
    two = exchange(two, "z", "y").reshape(1, N * rows, wide)
    two = exchange(jnp.broadcast_to(two, (N, N * rows, wide)), "y", "z")
    two = two.reshape(N, N, rows, wide).transpose(1, 0, 2, 3).reshape(N * N * rows, wide)
    keep, send = contract(one, two)
    received = lax.ppermute(send, "c", [(0, 1), (1, 0)])
    partial_sum = (keep + received).astype(jnp.bfloat16)
    parts = lax.all_to_all(partial_sum, "x", 0, 0, tiled=True)
    return jnp.sum(parts.astype(jnp.float32), axis=0)


def solution(mesh):
    grid = Mesh(mesh.devices.reshape(N, N, N, 2), AXES)
    placed = (P(AXES, None), P(AXES), P(), P())
    return jax.shard_map(
        per_device,
        mesh=grid,
        in_specs=placed,
        out_specs=P(("y", "x", "c"), "z"),
        check_vma=False,
    )
```

time: 244 us -> 148 us (0.61)
  waiting for transfers between devices: 156 us -> 47.2 us
  blocking collectives: 51.6 us -> 66.5 us
  starting transfers between devices: 0.09 us -> 9.98 us
  local copies, waits for them, and re-layouts: 13.7 us -> 4.28 us
  matrix products: 7.76 us -> 0 us
  Pallas kernels: 0 us -> 5.28 us
    all_gather x2 -> x1, waiting for transfers between devices: 132 us -> 21.1 us  [per_device(): lax.all_gather(one, AXES, axis=0, tiled=True, axis_index_groups=groups('z...]
    reduce_scatter x1 -> x0, waiting for transfers between devices: 23.4 us -> none  [per_device(): lax.psum_scatter(partial_sum, 'split', scatter_dimension=0, tiled=True)]
    all_to_all x0 -> x1, waiting for transfers between devices: none -> 22.9 us  [exchange(): lax.all_to_all(blocks, AXES, 0, 0, tiled=True, axis_index_groups=groups(f...]
    all_to_all x2 -> x3, blocking collectives: 51.6 us -> 66.5 us  [the longest x2 41.9 us: exchange(): lax.all_to_all(blocks, AXES, 0, 0, tiled=True, axis_index_groups=groups(f...]
    reshape x1 -> x0, local copies, waits for them, and re-layouts: 10.9 us -> none  [per_device(): aligned = right.reshape(n_row, n_col, local_rows, right_width)]
    dot_general x1 -> x0, matrix products: 7.76 us -> none  [contract_rows(): lax.dot_general(first, second, (((0,), (0,)), ((), ())), preferred_elemen...]
    ppermute x0 -> x1, starting transfers between devices: none -> 6.36 us  [per_device(): received = lax.ppermute(send, 'c', [(0, 1), (1, 0)])]
    pallas_call x0 -> x2, Pallas kernels: none -> 5.28 us  [the longest x1 2.77 us: masked_and_scaled(): pl.pallas_call(mask_kernel, out_shape=(shape, shape), in_specs=[VMEM, SME...]
  transfers between devices with their start and end apart: 3 -> 3, of which waited for: 3 -> 3; matrix products, arithmetic and copies ran while one was open for 5% -> 0% of each run, Pallas kernels for 0% -> 0%
where the time goes in v1:
time: 148 us; the launch traced here: 147 us
  blocking collectives  66.5 us (45%)
  waiting for transfers between devices  47.2 us (32%)
  between operations  13.4 us (9%)
  starting transfers between devices  9.98 us (7%)
  Pallas kernels  5.28 us (4%)
  local copies, waits for them, and re-layouts  4.28 us (3%)
    all_to_all x2, blocking collectives, exchange(): lax.all_to_all(blocks, AXES, 0, 0, tiled=True, axis_index_groups=groups(f...  41.9 us
    all_to_all x1, blocking collectives, per_device(): parts = lax.all_to_all(partial_sum, 'x', 0, 0, tiled=True)  24.6 us
    all_to_all x1, waiting for transfers between devices, exchange(): lax.all_to_all(blocks, AXES, 0, 0, tiled=True, axis_index_groups=groups(f...  22.9 us
    all_gather x1, waiting for transfers between devices, per_device(): lax.all_gather(one, AXES, axis=0, tiled=True, axis_index_groups=groups('z...  21.1 us
    ppermute x1, starting transfers between devices, per_device(): received = lax.ppermute(send, 'c', [(0, 1), (1, 0)])  6.36 us
    all_to_all x1, starting transfers between devices, exchange(): lax.all_to_all(blocks, AXES, 0, 0, tiled=True, axis_index_groups=groups(f...  3.58 us
  transfers between devices with their start and end apart: 3, of which 3 were waited for; matrix products, arithmetic and copies ran while one was open for 0% of the time, Pallas kernels for 0%

profile of v1, /device:TPU:1, one launch (start us, length us, event | category | flops | bytes accessed | tf_op | source)
XLA Modules:
  0.0 147.5 jit_solution(4777961651081347243)
XLA Ops:
  6.5 1.5 copy.6.pattern_ref
  8.0 2.8 %shard_map.46 = (bf16[8,16,768]{2,1,0:T(8,128)(2,1)}, bf16[8,16,768]{2,1,0:T(8,128)(2,1)}) custom-call(bf16[16,6144]{1,0:T(8,128)(2,1)} %coef_ref.1, f32[16]{0:T(128)} %weight_ref.1, s32[128,48]{1,0:T(8,128)} %copy.6.pattern_ref, s32[48]{0:T(128)} %sizes_ref.1), custom_call_target="tpu_custom_call" | custom-call | flops 393216 | bytes 589824 | tf_op jit(solution)/shard_map/pallas_call | solution.py:64
  10.8 26.0 %all_to_all.20 = bf16[8,16,768]{2,1,0:T(8,128)(2,1)} all-to-all(bf16[8,16,768]{2,1,0:T(8,128)(2,1)} %get-tuple-element.9), channel_id=1, replica_groups={{0,128,256,384,512,640,768,896},{2,130,258,386,514,642,770,898},{4,132,..., dimensions={0} | all-to-all | bytes 393216 | tf_op jit(solution)/shard_map/all_to_all | solution.py:34
  36.7 15.9 %all_to_all.21 = bf16[8,16,768]{2,1,0:T(8,128)(2,1)S(1)} all-to-all(bf16[8,16,768]{2,1,0:T(8,128)(2,1)} %get-tuple-element.10), channel_id=1, replica_groups={{0,2,4,6,8,10,12,14},{16,18,20,22,24,26,28,30},{32,34,36,38,40,42,44,46..., dimensions={0} | all-to-all | bytes 393216 | tf_op jit(solution)/shard_map/all_to_all | solution.py:34
  52.6 1.3 broadcast_in_dim.8
  53.9 3.6 %all-to-all-start.2 = ((bf16[8,128,768]{2,1,0:T(8,128)(2,1)}), bf16[8,128,768]{2,1,0:T(8,128)(2,1)S(1)}, u32[]{:S(2)}, u32[]{:S(2)}) async-start(bf16[8,128,768]{2,1,0:T(8,128)(2,1)} %broadcast_in_dim.8), calls=%async_computation.2 | async-start | bytes 3145728 | tf_op jit(solution)/shard_map/all_to_all | solution.py:34
  57.5 0.0 all-gather.2.cloned.1.call-start
  57.5 0.7 all-gather.2.cloned.1.call-update
  58.2 22.9 %all-to-all-done.2 = bf16[8,128,768]{2,1,0:T(8,128)(2,1)S(1)} async-done(((bf16[8,128,768]{2,1,0:T(8,128)(2,1)}), bf16[8,128,768]{2,1,0:T(8,128)(2,1)S(1)}, u32[]{:S(2)}, u32[]{:S(2)}) %all-to-all-start.2) | async-done | bytes 1572896 | tf_op jit(solution)/shard_map/all_to_all | solution.py:34
  81.1 0.1 copy.7
  81.3 21.1 %all-gather.2.cloned.1.call-done.one_ref = bf16[1024,768]{1,0:T(8,128)(2,1)} async-done(((bf16[128,768]{1,0:T(8,128)(2,1)}), bf16[1024,768]{1,0:T(8,128)(2,1)}) %all-gather.2.cloned.1.call-update) | async-done | bytes 1572880 | tf_op jit(solution)/shard_map/all_gather | solution.py:127
  102.4 0.0 copy-start
  102.4 1.4 copy-done
  103.8 2.5 %shard_map.47 = (f32[8,48,768]{2,1,0:T(8,128)S(1)}, f32[8,48,768]{2,1,0:T(8,128)S(1)}) custom-call(bf16[1024,768]{1,0:T(8,128)(2,1)S(1)} %copy-done, bf16[1024,768]{1,0:T(8,128)(2,1)S(1)} %bitcast.6), custom_call_target="tpu_custom_call" | custom-call | flops 1207959552 | bytes 5505024 | tf_op jit(solution)/shard_map/pallas_call | solution.py:111
  106.3 6.4 %collective-permute-start = (f32[8,48,768]{2,1,0:T(8,128)S(1)}, f32[8,48,768]{2,1,0:T(8,128)S(1)}, u32[]{:S(2)}, u32[]{:S(2)}) collective-permute-start(f32[8,48,768]{2,1,0:T(8,128)S(1)} %get-tuple-element.12), channel_id=1, source_target_pairs={{0,1},{1,0},{2,3},{3,2},{4,5},{5,4},{6,7},{7,6},{8,9},{9,8},{10,11... | collective-permute-start | bytes 3538952 | tf_op jit(solution)/shard_map/ppermute | solution.py:132
  112.7 2.5 %collective-permute-done = f32[8,48,768]{2,1,0:T(8,128)S(1)} collective-permute-done((f32[8,48,768]{2,1,0:T(8,128)S(1)}, f32[8,48,768]{2,1,0:T(8,128)S(1)}, u32[]{:S(2)}, u32[]{:S(2)}) %collective-permute-start) | collective-permute-done | bytes 1179680 | tf_op jit(solution)/shard_map/ppermute | solution.py:132
  115.2 0.2 add_convert_fusion
  115.3 24.6 %all_to_all.22 = bf16[8,48,768]{2,1,0:T(8,128)(2,1)S(1)} all-to-all(bf16[8,48,768]{2,1,0:T(8,128)(2,1)S(1)} %add_convert_fusion), channel_id=1, replica_groups=mesh['y'=8,'x'=8,'z'=8,'c'=2] {'x'}, dimensions={0} | all-to-all | bytes 1179648 | tf_op jit(solution)/shard_map/all_to_all | solution.py:134
  139.9 0.7 convert_reduce_fusion
Async XLA Ops:
  53.9 27.2 %all-to-all-start.2 = ((bf16[8,128,768]{2,1,0:T(8,128)(2,1)}), bf16[8,128,768]{2,1,0:T(8,128)(2,1)S(1)}, u32[]{:S(2)}, u32[]{:S(2)}) async-start(bf16[8,128,768]{2,1,0:T(8,128)(2,1)} %broadcast_in_dim.8), calls=%async_computation.2 | async-start | bytes 3145728 | tf_op jit(solution)/shard_map/all_to_all | solution.py:34
  57.5 44.9 %all-gather.2.cloned.1.call-start = ((), (), s32[]{:S(2)}) async-start(), calls=%async_computation.4 | async-start | bytes 1769472 | tf_op jit(solution)/shard_map/all_gather | solution.py:127
  102.4 1.4 copy-start
  106.3 8.8 %collective-permute-start = (f32[8,48,768]{2,1,0:T(8,128)S(1)}, f32[8,48,768]{2,1,0:T(8,128)S(1)}, u32[]{:S(2)}, u32[]{:S(2)}) collective-permute-start(f32[8,48,768]{2,1,0:T(8,128)S(1)} %get-tuple-element.12), channel_id=1, source_target_pairs={{0,1},{1,0},{2,3},{3,2},{4,5},{5,4},{6,7},{7,6},{8,9},{9,8},{10,11... | collective-permute-start | bytes 3538952 | tf_op jit(solution)/shard_map/ppermute | solution.py:132
Sparse Core Ops, SparseCore 0:
  61.0 41.3 all-gather.1

commit v2 on v1

v2 whole, which is shorter than its diff:
```python
import itertools

import jax
import jax.numpy as jnp
from jax import lax
from jax.experimental import pallas as pl
from jax.experimental.pallas import tpu as pltpu
from jax.sharding import Mesh, PartitionSpec as P

PAIR_ROWS = 128
AUX_PAD = 128
N = 8
AXES = ("y", "x", "z", "c")
HALF = 384
ROWS = 48
STEPS = 14
SMEM = pl.BlockSpec(memory_space=pltpu.SMEM)
VMEM = pl.BlockSpec(memory_space=pltpu.VMEM)


def groups(first, second):
    found = []
    for core, axis in enumerate((first, second)):
        rest = [a for a in "yxz" if a != axis]
        for others in itertools.product(range(N), repeat=2):
            at = dict(zip(rest, others))
            ring = []
            for i in range(N):
                at[axis] = i
                ring.append(((at["y"] * N + at["x"]) * N + at["z"]) * 2 + core)
            found.append(ring)
    return found


def exchange(blocks, first, second):
    return lax.all_to_all(
        blocks, AXES, 0, 0, tiled=True, axis_index_groups=groups(first, second)
    )


def mask_kernel(coef_ref, weight_ref, pattern_ref, sizes_ref, keep_ref, send_ref):
    rows, width = coef_ref.shape
    wide = width // N
    core = lax.axis_index("c")
    device = ((lax.axis_index("y") * N + lax.axis_index("x")) * N + lax.axis_index("z")) * 2 + core
    block = device * rows // PAIR_ROWS
    at_row = lax.broadcasted_iota(jnp.int32, (rows, AUX_PAD), 0)
    weight = jnp.zeros((rows, AUX_PAD), jnp.float32)
    for r in range(rows):
        weight = jnp.where(at_row == r, weight_ref[r], weight)
    lane = lax.broadcasted_iota(jnp.int32, (rows, AUX_PAD), 1)
    for atom in range(width // AUX_PAD):
        size = jnp.where(pattern_ref[atom, block] > 0, sizes_ref[atom], 0)
        coef = coef_ref[:, atom * AUX_PAD : (atom + 1) * AUX_PAD].astype(jnp.float32)
        masked = jnp.where(lane < size, coef, 0.0)
        scaled = weight * masked
        to, start = divmod(atom * AUX_PAD, wide)
        columns = slice(start, start + AUX_PAD)
        keep_ref[to, :, columns] = jnp.where(core == 0, masked, scaled).astype(jnp.bfloat16)
        send_ref[to, :, columns] = jnp.where(core == 0, scaled, masked).astype(jnp.bfloat16)


def masked_and_scaled(coefficients, row_weight, pattern, aux_sizes):
    rows, width = coefficients.shape
    shape = jax.ShapeDtypeStruct((N, rows, width // N), jnp.bfloat16)
    return pl.pallas_call(
        mask_kernel,
        out_shape=(shape, shape),
        in_specs=[VMEM, SMEM, SMEM, SMEM],
        out_specs=(VMEM, VMEM),
        cost_estimate=pl.CostEstimate(flops=4 * rows * width, bytes_accessed=6 * rows * width, transcendentals=0),
    )(coefficients, row_weight, pattern.T, aux_sizes)


def contract_part(own_ref, other_ref, gathered, part, write):
    steps, inner, two, rows, wide = own_ref.shape
    count = other_ref.shape[0] // (steps * two * rows)
    at = 0
    for k in range(count):
        for i in range(steps):
            for h in range(two):
                gathered[at : at + rows, :] = own_ref[i, part * count + k, 1 - h]
                at += rows
    tile = 256
    core = lax.axis_index("c")

    def run(left_ref, right_ref, columns):
        def row_tile(t, carry):
            start = pl.multiple_of(t * tile, tile)
            write(
                start,
                lax.dot_general(
                    left_ref[:, pl.ds(start, tile)],
                    right_ref[:, columns],
                    (((0,), (0,)), ((), ())),
                    preferred_element_type=jnp.float32,
                ),
            )
            return carry

        lax.fori_loop(0, wide // tile, row_tile, 0)

    @pl.when(core == 0)
    def _():
        run(gathered, other_ref, slice(0, HALF))

    @pl.when(core == 1)
    def _():
        run(other_ref, gathered, slice(HALF, 2 * HALF))


def first_part_kernel(own_ref, other_ref, out_ref, gathered):
    def write(start, value):
        out_ref[pl.ds(start, value.shape[0]), :] = value

    contract_part(own_ref, other_ref, gathered, 0, write)


def second_part_kernel(own_ref, other_ref, first_ref, out_ref, gathered, total):
    def write(start, value):
        rows = pl.ds(start, value.shape[0])
        total[rows, :] = first_ref[rows, :] + value

    contract_part(own_ref, other_ref, gathered, 1, write)

    lanes = out_ref.shape[2]
    tiles = HALF // lanes
    tail = out_ref.shape[1] - tiles * ROWS
    at_row = lax.broadcasted_iota(jnp.int32, (tail, lanes), 0)

    def message(d, carry):
        block = total[pl.ds(pl.multiple_of(d * ROWS, 16), ROWS), :]
        exponents = jnp.zeros((tail, lanes), jnp.int32)
        for t in range(tiles):
            value = block[:, t * lanes : (t + 1) * lanes]
            largest = jnp.max(jnp.abs(value), axis=0, keepdims=True)
            exponent = jnp.floor(jnp.log2(jnp.maximum(largest, 2.0**-110)))
            coded = jnp.floor(value * jnp.exp2(STEPS - exponent) + 0.5)
            coded = jnp.clip(coded, -32767.0, 32767.0).astype(jnp.int32)
            out_ref[d, t * ROWS : (t + 1) * ROWS, :] = coded.astype(jnp.int16)
            exponents = jnp.where(at_row == t, exponent.astype(jnp.int32), exponents)
        out_ref[d, tiles * ROWS :, :] = exponents.astype(jnp.int16)
        return carry

    lax.fori_loop(0, out_ref.shape[0], message, 0)


def sum_kernel(parts_ref, out_ref):
    messages, _, lanes = parts_ref.shape
    tiles = HALF // lanes
    for core in range(2):
        totals = [jnp.zeros((ROWS, lanes), jnp.float32) for _ in range(tiles)]
        for d in range(core, messages, 2):
            exponents = parts_ref[d, tiles * ROWS :, :].astype(jnp.int32).astype(jnp.float32)
            for t in range(tiles):
                scale = jnp.exp2(exponents[t : t + 1, :] - STEPS)
                coded = parts_ref[d, t * ROWS : (t + 1) * ROWS, :].astype(jnp.int32)
                totals[t] = totals[t] + coded.astype(jnp.float32) * scale
        for t in range(tiles):
            start = core * HALF + t * lanes
            out_ref[:, start : start + lanes] = totals[t]


def contract(own, other, first):
    depth, wide = other.shape
    gathered = pltpu.VMEM((depth, wide), jnp.bfloat16)
    total = pltpu.VMEM((wide, HALF), jnp.float32)
    cost = pl.CostEstimate(flops=2 * depth * wide * HALF, bytes_accessed=8 * depth * wide, transcendentals=0)
    params = pltpu.CompilerParams(vmem_limit_bytes=32 * 2**20)
    if first is None:
        return pl.pallas_call(
            first_part_kernel,
            out_shape=jax.ShapeDtypeStruct((wide, HALF), jnp.float32),
            in_specs=[VMEM, VMEM],
            out_specs=VMEM,
            scratch_shapes=[gathered],
            compiler_params=params,
            cost_estimate=cost,
        )(own, other)
    lanes = 128
    return pl.pallas_call(
        second_part_kernel,
        out_shape=jax.ShapeDtypeStruct((wide // ROWS, HALF // lanes * ROWS + 16, lanes), jnp.int16),
        in_specs=[VMEM, VMEM, VMEM],
        out_specs=VMEM,
        scratch_shapes=[gathered, total],
        compiler_params=params,
        cost_estimate=cost,
    )(own, other, first)


def per_device(coefficients, row_weight, pattern, aux_sizes):
    keep, send = masked_and_scaled(coefficients, row_weight, pattern, aux_sizes)
    rows, wide = keep.shape[1:]
    swap = [(0, 1), (1, 0)]
    blocks = jnp.concatenate([keep, lax.ppermute(send, "c", swap)], axis=1)
    blocks = exchange(blocks, "y", "z").reshape(1, N * 2 * rows, wide)
    own = exchange(jnp.broadcast_to(blocks, (N, N * 2 * rows, wide)), "z", "y")
    other = [
        lax.ppermute(own[p * N // 2 : (p + 1) * N // 2], "c", swap).reshape(-1, wide)
        for p in range(2)
    ]
    own = own.reshape(N, N, 2, rows, wide)
    messages = contract(own, other[1], contract(own, other[0], None))
    parts = lax.all_to_all(messages, ("x", "c"), 0, 0, tiled=True)
    return pl.pallas_call(
        sum_kernel,
        out_shape=jax.ShapeDtypeStruct((ROWS, wide), jnp.float32),
        in_specs=[VMEM],
        out_specs=VMEM,
    )(parts)


def solution(mesh):
    grid = Mesh(mesh.devices.reshape(N, N, N, 2), AXES)
    placed = (P(AXES, None), P(AXES), P(), P())
    return jax.shard_map(
        per_device,
        mesh=grid,
        in_specs=placed,
        out_specs=P(("y", "x", "c"), "z"),
        check_vma=False,
    )
```

time: 148 us -> 125 us (0.84)
  waiting for transfers between devices: 47.2 us -> 3.1 us
  blocking collectives: 66.5 us -> 88.8 us
  between operations: 13.4 us -> 0.06 us
  starting transfers between devices: 9.98 us -> 23.1 us
  local copies, waits for them, and re-layouts: 4.28 us -> 0.41 us
  Pallas kernels: 5.28 us -> 7.81 us
    all_to_all x1 -> x0, waiting for transfers between devices: 22.9 us -> none  [exchange(): lax.all_to_all(blocks, AXES, 0, 0, tiled=True, axis_index_groups=groups(f...]
    all_gather x1 -> x0, waiting for transfers between devices: 21.1 us -> none  [per_device(): lax.all_gather(one, AXES, axis=0, tiled=True, axis_index_groups=groups('z...]
    all_to_all x2, blocking collectives: 41.9 us -> 61.6 us  [exchange(): lax.all_to_all(blocks, AXES, 0, 0, tiled=True, axis_index_groups=groups(f...]
    ppermute x1 -> x3, starting transfers between devices: 6.36 us -> 23.1 us  [the longest x1 16.1 us: per_device(): blocks = jnp.concatenate([keep, lax.ppermute(send, 'c', swap)], axis=1)]
    all_to_all x1 -> x0, starting transfers between devices: 3.58 us -> none  [exchange(): lax.all_to_all(blocks, AXES, 0, 0, tiled=True, axis_index_groups=groups(f...]
    pallas_call x1 -> x3, Pallas kernels: 2.51 us -> 5.72 us  [the longest x1 2.28 us: contract(): pl.pallas_call(second_part_kernel, out_shape=jax.ShapeDtypeStruct((wide /...]
    unnamed x3 -> x0, local copies, waits for them, and re-layouts: 2.87 us -> none
    all_to_all x1, blocking collectives: 24.6 us -> 27.2 us  [per_device(): parts = lax.all_to_all(messages, ('x', 'c'), 0, 0, tiled=True)]
  transfers between devices with their start and end apart: 3 -> 3, of which waited for: 3 -> 3; matrix products, arithmetic and copies ran while one was open for 0% -> 0% of each run, Pallas kernels for 0% -> 1%
where the time goes in v2:
time: 125 us; the launch traced here: 124 us
  blocking collectives  88.8 us (71%)
  starting transfers between devices  23.1 us (18%)
  Pallas kernels  7.81 us (6%)
  waiting for transfers between devices  3.1 us (2%)
    all_to_all x2, blocking collectives, exchange(): lax.all_to_all(blocks, AXES, 0, 0, tiled=True, axis_index_groups=groups(f...  61.6 us
    all_to_all x1, blocking collectives, per_device(): parts = lax.all_to_all(messages, ('x', 'c'), 0, 0, tiled=True)  27.2 us
    ppermute x1, starting transfers between devices, per_device(): blocks = jnp.concatenate([keep, lax.ppermute(send, 'c', swap)], axis=1)  16.1 us
    ppermute x2, starting transfers between devices, per_device(): lax.ppermute(own[p * N // 2:(p + 1) * N // 2], 'c', swap).reshape(-1, wide)  7.06 us
  transfers between devices with their start and end apart: 3, of which 3 were waited for; matrix products, arithmetic and copies ran while one was open for 0% of the time, Pallas kernels for 1%

profile of v2, /device:TPU:1, one launch (start us, length us, event | category | flops | bytes accessed | tf_op | source)
XLA Modules:
  0.0 124.3 jit_solution(16668718475755816411)
XLA Ops:
  0.0 2.1 %shard_map.46 = (bf16[8,16,768]{2,1,0:T(8,128)(2,1)}, bf16[8,16,768]{2,1,0:T(8,128)(2,1)}) custom-call(bf16[16,6144]{1,0:T(8,128)(2,1)} %coef_ref.1, f32[16]{0:T(128)} %weight_ref.1, s32[48,128]{1,0:T(8,128)} %bitcast.10, s32[48]{0:T(128)} %sizes_ref.1), custom_call_target="tpu_custom_call" | custom-call | flops 393216 | bytes 589824 | tf_op jit(solution)/shard_map/pallas_call | solution.py:66
  2.1 16.1 %collective-permute-start = (bf16[8,16,768]{2,1,0:T(8,128)(2,1)}, bf16[8,16,768]{2,1,0:T(8,128)(2,1)S(1)}, u32[]{:S(2)}, u32[]{:S(2)}) collective-permute-start(bf16[8,16,768]{2,1,0:T(8,128)(2,1)} %get-tuple-element.8), channel_id=1, source_target_pairs={{0,1},{1,0},{2,3},{3,2},{4,5},{5,4},{6,7},{7,6},{8,9},{9,8},{10,11... | collective-permute-start | bytes 589832 | tf_op jit(solution)/shard_map/ppermute | solution.py:196
  18.1 1.3 %collective-permute-done = bf16[8,16,768]{2,1,0:T(8,128)(2,1)S(1)} collective-permute-done((bf16[8,16,768]{2,1,0:T(8,128)(2,1)}, bf16[8,16,768]{2,1,0:T(8,128)(2,1)S(1)}, u32[]{:S(2)}, u32[]{:S(2)}) %collective-permute-start) | collective-permute-done | bytes 196640 | tf_op jit(solution)/shard_map/ppermute | solution.py:196
  19.4 1.0 pad_maximum_fusion
  20.4 14.3 %all_to_all.15 = bf16[8,32,768]{2,1,0:T(8,128)(2,1)S(1)} all-to-all(bf16[8,32,768]{2,1,0:T(8,128)(2,1)S(1)} %pad_maximum_fusion), channel_id=1, replica_groups={{0,128,256,384,512,640,768,896},{2,130,258,386,514,642,770,898},{4,132,..., dimensions={0} | all-to-all | bytes 786432 | tf_op jit(solution)/shard_map/all_to_all | solution.py:36
  34.7 0.2 broadcast_in_dim.8
  34.9 47.3 %all_to_all.16 = bf16[8,256,768]{2,1,0:T(8,128)(2,1)S(1)} all-to-all(bf16[8,256,768]{2,1,0:T(8,128)(2,1)S(1)} %broadcast_in_dim.8), channel_id=1, replica_groups={{0,2,4,6,8,10,12,14},{16,18,20,22,24,26,28,30},{32,34,36,38,40,42,44,46..., dimensions={0} | all-to-all | bytes 6291456 | tf_op jit(solution)/shard_map/all_to_all | solution.py:36
  82.2 0.2 fusion
  82.4 5.1 %collective-permute-start.2 = (bf16[4,256,768]{2,1,0:T(8,128)(2,1)S(1)}, bf16[4,256,768]{2,1,0:T(8,128)(2,1)S(1)}, u32[]{:S(2)}, u32[]{:S(2)}) collective-permute-start(bf16[4,256,768]{2,1,0:T(8,128)(2,1)S(1)} %get-tuple-element.9), channel_id=1, source_target_pairs={{0,1},{1,0},{2,3},{3,2},{4,5},{5,4},{6,7},{7,6},{8,9},{9,8},{10,11... | collective-permute-start | bytes 4718600 | tf_op jit(solution)/shard_map/ppermute | solution.py:200
  87.5 1.9 %collective-permute-start.1 = (bf16[4,256,768]{2,1,0:T(8,128)(2,1)S(1)}, bf16[4,256,768]{2,1,0:T(8,128)(2,1)S(1)}, u32[]{:S(2)}, u32[]{:S(2)}) collective-permute-start(bf16[4,256,768]{2,1,0:T(8,128)(2,1)S(1)} %get-tuple-element.10), channel_id=1, source_target_pairs={{0,1},{1,0},{2,3},{3,2},{4,5},{5,4},{6,7},{7,6},{8,9},{9,8},{10,11... | collective-permute-start | bytes 4718600 | tf_op jit(solution)/shard_map/ppermute | solution.py:200
  89.5 1.1 collective-permute-done.2
  90.5 1.5 %shard_map.47.first_ref = f32[768,384]{1,0:T(8,128)S(1)} custom-call(bf16[8,8,2,16,768]{4,3,2,1,0:T(8,128)(2,1)S(1)} %bitcast.5, bf16[1024,768]{1,0:T(8,128)(2,1)S(1)} %bitcast.8), custom_call_target="tpu_custom_call" | custom-call | flops 603979776 | bytes 6291456 | tf_op jit(solution)/shard_map/pallas_call | solution.py:171
  92.1 0.8 collective-permute-done.1
  92.8 2.3 %shard_map.48 = s16[16,160,128]{2,1,0:T(8,128)(2,1)S(1)} custom-call(bf16[8,8,2,16,768]{4,3,2,1,0:T(8,128)(2,1)S(1)} %bitcast.6, bf16[1024,768]{1,0:T(8,128)(2,1)S(1)} %bitcast.7, f32[768,384]{1,0:T(8,128)S(1)} %shard_map.47.first_ref), custom_call_target="tpu_custom_call" | custom-call | flops 603979776 | bytes 6291456 | tf_op jit(solution)/shard_map/pallas_call | solution.py:181
  95.1 27.2 %all_to_all.17.parts_ref = s16[16,160,128]{2,1,0:T(8,128)(2,1)} all-to-all(s16[16,160,128]{2,1,0:T(8,128)(2,1)S(1)} %shard_map.48), channel_id=1, replica_groups=mesh['y'=8,'x'=8,'z'=8,'c'=2] {'x','c'}, dimensions={0} | all-to-all | bytes 1310720 | tf_op jit(solution)/shard_map/all_to_all | solution.py:205
  122.3 1.9 %shard_map.49 = f32[48,768]{1,0:T(8,128)} custom-call(s16[16,160,128]{2,1,0:T(8,128)(2,1)} %all_to_all.17.parts_ref), custom_call_target="tpu_custom_call" | custom-call | tf_op jit(solution)/shard_map/pallas_call | solution.py:206
Async XLA Ops:
  2.1 17.3 %collective-permute-start = (bf16[8,16,768]{2,1,0:T(8,128)(2,1)}, bf16[8,16,768]{2,1,0:T(8,128)(2,1)S(1)}, u32[]{:S(2)}, u32[]{:S(2)}) collective-permute-start(bf16[8,16,768]{2,1,0:T(8,128)(2,1)} %get-tuple-element.8), channel_id=1, source_target_pairs={{0,1},{1,0},{2,3},{3,2},{4,5},{5,4},{6,7},{7,6},{8,9},{9,8},{10,11... | collective-permute-start | bytes 589832 | tf_op jit(solution)/shard_map/ppermute | solution.py:196
  82.4 8.2 %collective-permute-start.2 = (bf16[4,256,768]{2,1,0:T(8,128)(2,1)S(1)}, bf16[4,256,768]{2,1,0:T(8,128)(2,1)S(1)}, u32[]{:S(2)}, u32[]{:S(2)}) collective-permute-start(bf16[4,256,768]{2,1,0:T(8,128)(2,1)S(1)} %get-tuple-element.9), channel_id=1, source_target_pairs={{0,1},{1,0},{2,3},{3,2},{4,5},{5,4},{6,7},{7,6},{8,9},{9,8},{10,11... | collective-permute-start | bytes 4718600 | tf_op jit(solution)/shard_map/ppermute | solution.py:200
  87.5 5.3 %collective-permute-start.1 = (bf16[4,256,768]{2,1,0:T(8,128)(2,1)S(1)}, bf16[4,256,768]{2,1,0:T(8,128)(2,1)S(1)}, u32[]{:S(2)}, u32[]{:S(2)}) collective-permute-start(bf16[4,256,768]{2,1,0:T(8,128)(2,1)S(1)} %get-tuple-element.10), channel_id=1, source_target_pairs={{0,1},{1,0},{2,3},{3,2},{4,5},{5,4},{6,7},{7,6},{8,9},{9,8},{10,11... | collective-permute-start | bytes 4718600 | tf_op jit(solution)/shard_map/ppermute | solution.py:200

commit v3 on v2

v3 whole, which is shorter than its diff:
```python
import functools
import itertools

import jax
import jax.numpy as jnp
from jax import lax
from jax.experimental import pallas as pl
from jax.experimental.pallas import tpu as pltpu
from jax.sharding import Mesh, PartitionSpec as P

PAIR_ROWS = 128
AUX_PAD = 128
N = 8
AXES = ("y", "x", "z", "c")
HALF = 384
ROWS = 48
STEPS = 14
SMEM = pl.BlockSpec(memory_space=pltpu.SMEM)
VMEM = pl.BlockSpec(memory_space=pltpu.VMEM)


def groups(first, second):
    found = []
    for core, axis in enumerate((first, second)):
        rest = [a for a in "yxz" if a != axis]
        for others in itertools.product(range(N), repeat=2):
            at = dict(zip(rest, others))
            ring = []
            for i in range(N):
                at[axis] = i
                ring.append(((at["y"] * N + at["x"]) * N + at["z"]) * 2 + core)
            found.append(ring)
    return found


def exchange(blocks, first, second):
    return lax.all_to_all(
        blocks, AXES, 0, 0, tiled=True, axis_index_groups=groups(first, second)
    )


def into_order(tiles):
    lanes = tiles[0].shape[1]
    lane = lax.broadcasted_iota(jnp.int32, tiles[0].shape, 1)
    out = [None] * len(tiles)
    for piece in range(2 * N):
        core, x = divmod(piece, N)
        to, source = piece * ROWS, (2 * x + core) * ROWS
        end = to + ROWS
        while to < end:
            count = min(end - to, lanes - to % lanes, lanes - source % lanes)
            tile, start = divmod(to, lanes)
            rolled = tiles[source // lanes]
            if (to - source) % lanes:
                rolled = pltpu.roll(rolled, (to - source) % lanes, 1)
            out[tile] = rolled if start == 0 else jnp.where(lane >= start, rolled, out[tile])
            to, source = to + count, source + count
    return out


def mask_kernel(of_left, coef_ref, weight_ref, pattern_ref, sizes_ref, out_ref):
    rows, width = coef_ref.shape
    tiles = width // N // AUX_PAD
    core = lax.axis_index("c")
    device = ((lax.axis_index("y") * N + lax.axis_index("x")) * N + lax.axis_index("z")) * 2 + core
    block = device * rows // PAIR_ROWS
    lane = lax.broadcasted_iota(jnp.int32, (rows, AUX_PAD), 1)

    def masked_tiles(to):
        found = []
        for atom in range(to * tiles, (to + 1) * tiles):
            size = jnp.where(pattern_ref[atom, block] > 0, sizes_ref[atom], 0)
            coef = coef_ref[:, atom * AUX_PAD : (atom + 1) * AUX_PAD].astype(jnp.float32)
            found.append(jnp.where(lane < size, coef, 0.0))
        return found

    def store(to, found):
        for t in range(tiles):
            out_ref[to, 0:rows, t * AUX_PAD : (t + 1) * AUX_PAD] = found[t].astype(jnp.bfloat16)

    @pl.when(core == of_left)
    def _():
        for to in range(N):
            store(to, into_order(masked_tiles(to)))

    @pl.when(core != of_left)
    def _():
        at_row = lax.broadcasted_iota(jnp.int32, (rows, AUX_PAD), 0)
        weight = jnp.zeros((rows, AUX_PAD), jnp.float32)
        for r in range(rows):
            weight = jnp.where(at_row == r, weight_ref[r], weight)
        for to in range(N):
            store(to, [weight * m for m in masked_tiles(to)])


def operand(of_left, height, coefficients, row_weight, pattern, aux_sizes):
    rows, width = coefficients.shape
    return pl.pallas_call(
        functools.partial(mask_kernel, of_left),
        out_shape=jax.ShapeDtypeStruct((N, height, width // N), jnp.bfloat16),
        in_specs=[VMEM, SMEM, SMEM, SMEM],
        out_specs=VMEM,
        cost_estimate=pl.CostEstimate(flops=8 * rows * width, bytes_accessed=4 * rows * width, transcendentals=0),
    )(coefficients, row_weight, pattern.T, aux_sizes)


def contract_part(own_ref, other_ref, gathered, part, write):
    steps, inner, two, rows, wide = own_ref.shape
    count = other_ref.shape[0] // (steps * two * rows)
    core = lax.axis_index("c")
    tile = 256

    def gather(columns):
        at = 0
        for k in range(count):
            for i in range(steps):
                for h in range(two):
                    gathered[at : at + rows, columns] = own_ref[i, part * count + k, 1 - h, :, columns]
                    at += rows

    def run(left_ref, right_ref, columns):
        def column_tile(t, carry):
            start = pl.multiple_of(t * tile, tile)
            write(
                start,
                lax.dot_general(
                    left_ref[:, columns],
                    right_ref[:, pl.ds(start, tile)],
                    (((0,), (0,)), ((), ())),
                    preferred_element_type=jnp.float32,
                ),
            )
            return carry

        lax.fori_loop(0, wide // tile, column_tile, 0)

    @pl.when(core == 0)
    def _():
        gather(slice(0, HALF))
        run(gathered, other_ref, slice(0, HALF))

    @pl.when(core == 1)
    def _():
        gather(slice(0, wide))
        run(other_ref, gathered, slice(HALF, 2 * HALF))


def first_part_kernel(own_ref, other_ref, out_ref, gathered):
    def write(start, value):
        out_ref[:, pl.ds(start, value.shape[1])] = value

    contract_part(own_ref, other_ref, gathered, 0, write)


def second_part_kernel(own_ref, other_ref, first_ref, out_ref, gathered, total):
    def write(start, value):
        columns = pl.ds(start, value.shape[1])
        total[:, columns] = first_ref[:, columns] + value

    contract_part(own_ref, other_ref, gathered, 1, write)

    lanes = out_ref.shape[2]
    tiles = total.shape[1] // lanes
    tail = out_ref.shape[1] - tiles * ROWS
    at_row = lax.broadcasted_iota(jnp.int32, (tail, lanes), 0)

    def message(d, carry):
        rows = pl.ds(pl.multiple_of(d * ROWS, 16), ROWS)
        exponents = jnp.zeros((tail, lanes), jnp.int32)
        for t in range(tiles):
            value = total[rows, t * lanes : (t + 1) * lanes]
            largest = jnp.max(jnp.abs(value), axis=0, keepdims=True)
            exponent = jnp.floor(jnp.log2(jnp.maximum(largest, 2.0**-110)))
            coded = jnp.floor(value * jnp.exp2(STEPS - exponent) + 0.5)
            coded = jnp.clip(coded, -32767.0, 32767.0).astype(jnp.int32)
            out_ref[d, t * ROWS : (t + 1) * ROWS, :] = coded.astype(jnp.int16)
            exponents = jnp.where(at_row == t, exponent.astype(jnp.int32), exponents)
        out_ref[d, tiles * ROWS :, :] = exponents.astype(jnp.int16)
        return carry

    lax.fori_loop(0, out_ref.shape[0], message, 0)


def sum_kernel(parts_ref, out_ref):
    messages, _, lanes = parts_ref.shape
    tiles = out_ref.shape[1] // lanes
    scales = [
        jnp.exp2(parts_ref[d, tiles * ROWS :, :].astype(jnp.int32).astype(jnp.float32) - STEPS) for d in range(messages)
    ]
    for t in range(tiles):
        total = jnp.zeros((ROWS, lanes), jnp.float32)
        for d in range(messages):
            coded = parts_ref[d, t * ROWS : (t + 1) * ROWS, :].astype(jnp.int32)
            total = total + coded.astype(jnp.float32) * scales[d][t : t + 1, :]
        out_ref[:, t * lanes : (t + 1) * lanes] = total


def contract(own, other, first):
    depth, wide = other.shape
    gathered = pltpu.VMEM((depth, wide), jnp.bfloat16)
    total = pltpu.VMEM((HALF, wide), jnp.float32)
    cost = pl.CostEstimate(flops=2 * depth * wide * HALF, bytes_accessed=8 * depth * wide, transcendentals=0)
    params = pltpu.CompilerParams(vmem_limit_bytes=32 * 2**20)
    if first is None:
        return pl.pallas_call(
            first_part_kernel,
            out_shape=jax.ShapeDtypeStruct((HALF, wide), jnp.float32),
            in_specs=[VMEM, VMEM],
            out_specs=VMEM,
            scratch_shapes=[gathered],
            compiler_params=params,
            cost_estimate=cost,
        )(own, other)
    lanes = 128
    return pl.pallas_call(
        second_part_kernel,
        out_shape=jax.ShapeDtypeStruct((HALF // ROWS, wide // lanes * ROWS + 16, lanes), jnp.int16),
        in_specs=[VMEM, VMEM, VMEM],
        out_specs=VMEM,
        scratch_shapes=[gathered, total],
        compiler_params=params,
        cost_estimate=cost,
    )(own, other, first)


def per_device(coefficients, row_weight, pattern, aux_sizes):
    given = (coefficients, row_weight, pattern, aux_sizes)
    rows = coefficients.shape[0]
    swap = [(0, 1), (1, 0)]
    received = lax.ppermute(operand(1, rows, *given), "c", swap)
    blocks = lax.dynamic_update_slice(operand(0, 2 * rows, *given), received, (0, rows, 0))
    wide = blocks.shape[2]
    blocks = exchange(blocks, "y", "z").reshape(1, N * 2 * rows, wide)
    own = exchange(jnp.broadcast_to(blocks, (N, N * 2 * rows, wide)), "z", "y")
    other = [
        lax.ppermute(own[p * N // 2 : (p + 1) * N // 2], "c", swap).reshape(-1, wide)
        for p in range(2)
    ]
    own = own.reshape(N, N, 2, rows, wide)
    messages = contract(own, other[1], contract(own, other[0], None))
    parts = lax.all_to_all(messages, "x", 0, 0, tiled=True)
    return pl.pallas_call(
        sum_kernel,
        out_shape=jax.ShapeDtypeStruct((ROWS, wide), jnp.float32),
        in_specs=[VMEM],
        out_specs=VMEM,
    )(parts)


def solution(mesh):
    grid = Mesh(mesh.devices.reshape(N, N, N, 2), AXES)
    placed = (P(AXES, None), P(AXES), P(), P())
    return jax.shard_map(
        per_device,
        mesh=grid,
        in_specs=placed,
        out_specs=P(("y", "x", "c"), "z"),
        check_vma=False,
    )
```

time: 125 us -> 123 us (0.984)
  blocking collectives: 88.8 us -> 87.1 us
  Pallas kernels: 7.81 us -> 9.28 us
    all_to_all x1, blocking collectives: 27.2 us -> 25.3 us  [per_device(): parts = lax.all_to_all(messages, 'x', 0, 0, tiled=True)]
    pallas_call x3 -> x4, Pallas kernels: 5.89 us -> 7.38 us  [the longest x2 4.17 us: operand(): pl.pallas_call(functools.partial(mask_kernel, of_left), out_shape=jax.Sha...]
    ppermute x1, waiting for transfers between devices: 1.26 us -> 0.01 us  [per_device(): received = lax.ppermute(operand(1, rows, *given), 'c', swap)]
  transfers between devices with their start and end apart: 3 -> 3, of which waited for: 3 -> 2; matrix products, arithmetic and copies ran while one was open for 0% -> 0% of each run, Pallas kernels for 1% -> 3%
where the time goes in v3:
time: 123 us; the launch traced here: 122 us
  blocking collectives  87.1 us (71%)
  starting transfers between devices  22.7 us (18%)
  Pallas kernels  9.28 us (8%)
  waiting for transfers between devices  2.02 us (2%)
    all_to_all x2, blocking collectives, exchange(): lax.all_to_all(blocks, AXES, 0, 0, tiled=True, axis_index_groups=groups(f...  61.8 us
    all_to_all x1, blocking collectives, per_device(): parts = lax.all_to_all(messages, 'x', 0, 0, tiled=True)  25.3 us
    ppermute x1, starting transfers between devices, per_device(): received = lax.ppermute(operand(1, rows, *given), 'c', swap)  16 us
    ppermute x2, starting transfers between devices, per_device(): lax.ppermute(own[p * N // 2:(p + 1) * N // 2], 'c', swap).reshape(-1, wide)  6.79 us
    pallas_call x2, Pallas kernels, operand(): pl.pallas_call(functools.partial(mask_kernel, of_left), out_shape=jax.Sha...  4.17 us
  transfers between devices with their start and end apart: 3, of which 2 were waited for; matrix products, arithmetic and copies ran while one was open for 0% of the time, Pallas kernels for 3%

profile of v3, /device:TPU:1, one launch (start us, length us, event | category | flops | bytes accessed | tf_op | source)
XLA Modules:
  0.0 122.3 jit_solution(8494621180416055915)
XLA Ops:
  0.0 2.1 %shard_map.47 = bf16[8,16,768]{2,1,0:T(8,128)(2,1)} custom-call(bf16[16,6144]{1,0:T(8,128)(2,1)} %coef_ref.3, f32[16]{0:T(128)} %weight_ref.3, s32[48,128]{1,0:T(8,128)} %bitcast.10, s32[48]{0:T(128)} %sizes_ref.3), custom_call_target="tpu_custom_call" | custom-call | flops 786432 | bytes 393216 | tf_op jit(solution)/shard_map/pallas_call | solution.py:98
  2.1 16.0 %collective-permute-start = (bf16[8,16,768]{2,1,0:T(8,128)(2,1)}, bf16[8,16,768]{2,1,0:T(8,128)(2,1)S(1)}, u32[]{:S(2)}, u32[]{:S(2)}) collective-permute-start(bf16[8,16,768]{2,1,0:T(8,128)(2,1)} %shard_map.47), channel_id=1, source_target_pairs={{0,1},{1,0},{2,3},{3,2},{4,5},{5,4},{6,7},{7,6},{8,9},{9,8},{10,11... | collective-permute-start | bytes 589832 | tf_op jit(solution)/shard_map/ppermute | solution.py:230
  18.1 2.1 %shard_map.46 = bf16[8,32,768]{2,1,0:T(8,128)(2,1)} custom-call(bf16[16,6144]{1,0:T(8,128)(2,1)} %coef_ref.3, f32[16]{0:T(128)} %weight_ref.3, s32[48,128]{1,0:T(8,128)} %bitcast.11, s32[48]{0:T(128)} %sizes_ref.3), custom_call_target="tpu_custom_call" | custom-call | flops 786432 | bytes 393216 | tf_op jit(solution)/shard_map/pallas_call | solution.py:98
  20.1 0.0 collective-permute-done
  20.1 0.7 constant_dynamic-update-slice_fusion
  20.8 14.8 %all_to_all.15 = bf16[8,32,768]{2,1,0:T(8,128)(2,1)S(1)} all-to-all(bf16[8,32,768]{2,1,0:T(8,128)(2,1)} %constant_dynamic-update-slice_fusion), channel_id=1, replica_groups={{0,128,256,384,512,640,768,896},{2,130,258,386,514,642,770,898},{4,132,..., dimensions={0} | all-to-all | bytes 786432 | tf_op jit(solution)/shard_map/all_to_all | solution.py:37
  35.6 0.2 broadcast_in_dim.8
  35.8 47.0 %all_to_all.16 = bf16[8,256,768]{2,1,0:T(8,128)(2,1)S(1)} all-to-all(bf16[8,256,768]{2,1,0:T(8,128)(2,1)S(1)} %broadcast_in_dim.8), channel_id=1, replica_groups={{0,2,4,6,8,10,12,14},{16,18,20,22,24,26,28,30},{32,34,36,38,40,42,44,46..., dimensions={0} | all-to-all | bytes 6291456 | tf_op jit(solution)/shard_map/all_to_all | solution.py:37
  82.8 0.2 fusion
  83.0 4.9 %collective-permute-start.2 = (bf16[4,256,768]{2,1,0:T(8,128)(2,1)S(1)}, bf16[4,256,768]{2,1,0:T(8,128)(2,1)S(1)}, u32[]{:S(2)}, u32[]{:S(2)}) collective-permute-start(bf16[4,256,768]{2,1,0:T(8,128)(2,1)S(1)} %get-tuple-element.5), channel_id=1, source_target_pairs={{0,1},{1,0},{2,3},{3,2},{4,5},{5,4},{6,7},{7,6},{8,9},{9,8},{10,11... | collective-permute-start | bytes 4718600 | tf_op jit(solution)/shard_map/ppermute | solution.py:236
  87.9 1.9 %collective-permute-start.1 = (bf16[4,256,768]{2,1,0:T(8,128)(2,1)S(1)}, bf16[4,256,768]{2,1,0:T(8,128)(2,1)S(1)}, u32[]{:S(2)}, u32[]{:S(2)}) collective-permute-start(bf16[4,256,768]{2,1,0:T(8,128)(2,1)S(1)} %get-tuple-element.6), channel_id=1, source_target_pairs={{0,1},{1,0},{2,3},{3,2},{4,5},{5,4},{6,7},{7,6},{8,9},{9,8},{10,11... | collective-permute-start | bytes 4718600 | tf_op jit(solution)/shard_map/ppermute | solution.py:236
  89.9 1.1 collective-permute-done.2
  90.9 1.4 %shard_map.48.first_ref = f32[384,768]{1,0:T(8,128)S(1)} custom-call(bf16[8,8,2,16,768]{4,3,2,1,0:T(8,128)(2,1)S(1)} %bitcast.5, bf16[1024,768]{1,0:T(8,128)(2,1)S(1)} %bitcast.8), custom_call_target="tpu_custom_call" | custom-call | flops 603979776 | bytes 6291456 | tf_op jit(solution)/shard_map/pallas_call | solution.py:205
  92.3 0.9 collective-permute-done.1
  93.2 1.9 %shard_map.49 = s16[8,304,128]{2,1,0:T(8,128)(2,1)S(1)} custom-call(bf16[8,8,2,16,768]{4,3,2,1,0:T(8,128)(2,1)S(1)} %bitcast.6, bf16[1024,768]{1,0:T(8,128)(2,1)S(1)} %bitcast.7, f32[384,768]{1,0:T(8,128)S(1)} %shard_map.48.first_ref), custom_call_target="tpu_custom_call" | custom-call | flops 603979776 | bytes 6291456 | tf_op jit(solution)/shard_map/pallas_call | solution.py:215
  95.1 25.3 %all_to_all.17.parts_ref = s16[8,304,128]{2,1,0:T(8,128)(2,1)} all-to-all(s16[8,304,128]{2,1,0:T(8,128)(2,1)S(1)} %shard_map.49), channel_id=1, replica_groups=mesh['y'=8,'x'=8,'z'=8,'c'=2] {'x'}, dimensions={0} | all-to-all | bytes 1245184 | tf_op jit(solution)/shard_map/all_to_all | solution.py:241
  120.4 1.9 %shard_map.50 = f32[48,768]{1,0:T(8,128)} custom-call(s16[8,304,128]{2,1,0:T(8,128)(2,1)} %all_to_all.17.parts_ref), custom_call_target="tpu_custom_call" | custom-call | tf_op jit(solution)/shard_map/pallas_call | solution.py:242
Async XLA Ops:
  2.1 18.0 %collective-permute-start = (bf16[8,16,768]{2,1,0:T(8,128)(2,1)}, bf16[8,16,768]{2,1,0:T(8,128)(2,1)S(1)}, u32[]{:S(2)}, u32[]{:S(2)}) collective-permute-start(bf16[8,16,768]{2,1,0:T(8,128)(2,1)} %shard_map.47), channel_id=1, source_target_pairs={{0,1},{1,0},{2,3},{3,2},{4,5},{5,4},{6,7},{7,6},{8,9},{9,8},{10,11... | collective-permute-start | bytes 589832 | tf_op jit(solution)/shard_map/ppermute | solution.py:230
  83.0 7.9 %collective-permute-start.2 = (bf16[4,256,768]{2,1,0:T(8,128)(2,1)S(1)}, bf16[4,256,768]{2,1,0:T(8,128)(2,1)S(1)}, u32[]{:S(2)}, u32[]{:S(2)}) collective-permute-start(bf16[4,256,768]{2,1,0:T(8,128)(2,1)S(1)} %get-tuple-element.5), channel_id=1, source_target_pairs={{0,1},{1,0},{2,3},{3,2},{4,5},{5,4},{6,7},{7,6},{8,9},{9,8},{10,11... | collective-permute-start | bytes 4718600 | tf_op jit(solution)/shard_map/ppermute | solution.py:236
  87.9 5.3 %collective-permute-start.1 = (bf16[4,256,768]{2,1,0:T(8,128)(2,1)S(1)}, bf16[4,256,768]{2,1,0:T(8,128)(2,1)S(1)}, u32[]{:S(2)}, u32[]{:S(2)}) collective-permute-start(bf16[4,256,768]{2,1,0:T(8,128)(2,1)S(1)} %get-tuple-element.6), channel_id=1, source_target_pairs={{0,1},{1,0},{2,3},{3,2},{4,5},{5,4},{6,7},{7,6},{8,9},{9,8},{10,11... | collective-permute-start | bytes 4718600 | tf_op jit(solution)/shard_map/ppermute | solution.py:236

commit v4 on v3

--- a/solution.py
+++ b/solution.py
@@ -15,8 +15,8 @@
 HALF = 384
 ROWS = 48
 STEPS = 14
-SMEM = pl.BlockSpec(memory_space=pltpu.SMEM)
 VMEM = pl.BlockSpec(memory_space=pltpu.VMEM)
+SMALL = pltpu.CompilerParams(vmem_limit_bytes=8 * 2**20)
 
 
 def groups(first, second):
@@ -58,6 +58,13 @@
     return out
 
 
+def as_column(row):
+    n = row.shape[1]
+    square = (n, n)
+    here = lax.broadcasted_iota(jnp.int32, square, 0) == lax.broadcasted_iota(jnp.int32, square, 1)
+    return jnp.sum(jnp.where(here, jnp.broadcast_to(row, square), 0), axis=1, keepdims=True)
+
+
 def mask_kernel(of_left, coef_ref, weight_ref, pattern_ref, sizes_ref, out_ref):
     rows, width = coef_ref.shape
     tiles = width // N // AUX_PAD
@@ -65,13 +72,15 @@
     device = ((lax.axis_index("y") * N + lax.axis_index("x")) * N + lax.axis_index("z")) * 2 + core
     block = device * rows // PAIR_ROWS
     lane = lax.broadcasted_iota(jnp.int32, (rows, AUX_PAD), 1)
+    at_block = lax.broadcasted_iota(jnp.int32, pattern_ref.shape, 1) == block
+    meets = jnp.sum(jnp.where(at_block, pattern_ref[...], 0), axis=1, keepdims=True)
+    sizes = jnp.broadcast_to(jnp.where(meets > 0, as_column(sizes_ref[...]), 0), pattern_ref.shape)
 
     def masked_tiles(to):
         found = []
         for atom in range(to * tiles, (to + 1) * tiles):
-            size = jnp.where(pattern_ref[atom, block] > 0, sizes_ref[atom], 0)
             coef = coef_ref[:, atom * AUX_PAD : (atom + 1) * AUX_PAD].astype(jnp.float32)
-            found.append(jnp.where(lane < size, coef, 0.0))
+            found.append(jnp.where(lane < sizes[atom : atom + 1, :], coef, 0.0))
         return found
 
     def store(to, found):
@@ -85,10 +94,7 @@
 
     @pl.when(core != of_left)
     def _():
-        at_row = lax.broadcasted_iota(jnp.int32, (rows, AUX_PAD), 0)
-        weight = jnp.zeros((rows, AUX_PAD), jnp.float32)
-        for r in range(rows):
-            weight = jnp.where(at_row == r, weight_ref[r], weight)
+        weight = jnp.broadcast_to(as_column(weight_ref[...]), (rows, AUX_PAD))
         for to in range(N):
             store(to, [weight * m for m in masked_tiles(to)])
 
@@ -98,10 +104,11 @@
     return pl.pallas_call(
         functools.partial(mask_kernel, of_left),
         out_shape=jax.ShapeDtypeStruct((N, height, width // N), jnp.bfloat16),
-        in_specs=[VMEM, SMEM, SMEM, SMEM],
+        in_specs=[VMEM] * 4,
         out_specs=VMEM,
+        compiler_params=SMALL,
         cost_estimate=pl.CostEstimate(flops=8 * rows * width, bytes_accessed=4 * rows * width, transcendentals=0),
-    )(coefficients, row_weight, pattern.T, aux_sizes)
+    )(coefficients, row_weight.reshape(1, -1), pattern.T, aux_sizes.reshape(1, -1))
 
 
 def contract_part(own_ref, other_ref, gathered, part, write):
@@ -244,6 +251,7 @@
         out_shape=jax.ShapeDtypeStruct((ROWS, wide), jnp.float32),
         in_specs=[VMEM],
         out_specs=VMEM,
+        compiler_params=SMALL,
     )(parts)
 
 

time: 123 us -> 121 us (0.984)
  Pallas kernels: 9.28 us -> 4.54 us
  local copies, waits for them, and re-layouts: 1.11 us -> 3.39 us
    pallas_call x2, Pallas kernels: 4.17 us -> 0.51 us  [operand(): pl.pallas_call(functools.partial(mask_kernel, of_left), out_shape=jax.Sha...]
    unnamed x0 -> x8, local copies, waits for them, and re-layouts: none -> 2.97 us
  transfers between devices with their start and end apart: 3 -> 3, of which waited for: 2 -> 3; matrix products, arithmetic and copies ran while one was open for 0% -> 0% of each run, Pallas kernels for 3% -> 1%
where the time goes in v4:
time: 121 us
  blocking collectives  86.7 us (72%)
  starting transfers between devices  23 us (19%)
  Pallas kernels  4.54 us (4%)
  local copies, waits for them, and re-layouts  3.39 us (3%)
  waiting for transfers between devices  2.85 us (2%)
    all_to_all x2, blocking collectives, exchange(): lax.all_to_all(blocks, AXES, 0, 0, tiled=True, axis_index_groups=groups(f...  61.6 us
    all_to_all x1, blocking collectives, per_device(): parts = lax.all_to_all(messages, 'x', 0, 0, tiled=True)  25.1 us
    ppermute x1, starting transfers between devices, per_device(): received = lax.ppermute(operand(1, rows, *given), 'c', swap)  16 us
    ppermute x2, starting transfers between devices, per_device(): lax.ppermute(own[p * N // 2:(p + 1) * N // 2], 'c', swap).reshape(-1, wide)  7.06 us
    unnamed x8, local copies, waits for them, and re-layouts  2.97 us
  transfers between devices with their start and end apart: 3, of which 3 were waited for; matrix products, arithmetic and copies ran while one was open for 0% of the time, Pallas kernels for 1%

profile of v4, /device:TPU:1, one launch (start us, length us, event | category | flops | bytes accessed | tf_op | source)
XLA Modules:
  0.0 120.6 jit_solution(8308593647551816612)
XLA Ops:
  0.0 0.0 copy-start
  0.0 0.9 copy-done
  0.9 0.0 copy-start.1
  0.9 0.7 copy-done.1
  1.7 0.0 copy-start.2
  1.7 0.7 copy-done.2
  2.3 0.0 copy-start.3
  2.3 0.7 copy-done.3
  3.0 0.3 shard_map.47
  3.3 16.0 %collective-permute-start = (bf16[8,16,768]{2,1,0:T(8,128)(2,1)S(1)}, bf16[8,16,768]{2,1,0:T(8,128)(2,1)S(1)}, u32[]{:S(2)}, u32[]{:S(2)}) collective-permute-start(bf16[8,16,768]{2,1,0:T(8,128)(2,1)S(1)} %shard_map.47), channel_id=1, source_target_pairs={{0,1},{1,0},{2,3},{3,2},{4,5},{5,4},{6,7},{7,6},{8,9},{9,8},{10,11... | collective-permute-start | bytes 589832 | tf_op jit(solution)/shard_map/ppermute | solution.py:237
  19.3 0.2 shard_map.46
  19.5 0.8 collective-permute-done
  20.3 14.3 %all_to_all.15 = bf16[8,32,768]{2,1,0:T(8,128)(2,1)S(1)} all-to-all(bf16[8,32,768]{2,1,0:T(8,128)(2,1)S(1)} %constant_dynamic-update-slice_fusion), channel_id=1, replica_groups={{0,128,256,384,512,640,768,896},{2,130,258,386,514,642,770,898},{4,132,..., dimensions={0} | all-to-all | bytes 786432 | tf_op jit(solution)/shard_map/all_to_all | solution.py:37
  34.6 0.2 broadcast_in_dim.8
  34.8 47.3 %all_to_all.16 = bf16[8,256,768]{2,1,0:T(8,128)(2,1)S(1)} all-to-all(bf16[8,256,768]{2,1,0:T(8,128)(2,1)S(1)} %broadcast_in_dim.8), channel_id=1, replica_groups={{0,2,4,6,8,10,12,14},{16,18,20,22,24,26,28,30},{32,34,36,38,40,42,44,46..., dimensions={0} | all-to-all | bytes 6291456 | tf_op jit(solution)/shard_map/all_to_all | solution.py:37
  82.1 0.2 fusion
  82.3 5.1 %collective-permute-start.2 = (bf16[4,256,768]{2,1,0:T(8,128)(2,1)S(1)}, bf16[4,256,768]{2,1,0:T(8,128)(2,1)S(1)}, u32[]{:S(2)}, u32[]{:S(2)}) collective-permute-start(bf16[4,256,768]{2,1,0:T(8,128)(2,1)S(1)} %get-tuple-element.5), channel_id=1, source_target_pairs={{0,1},{1,0},{2,3},{3,2},{4,5},{5,4},{6,7},{7,6},{8,9},{9,8},{10,11... | collective-permute-start | bytes 4718600 | tf_op jit(solution)/shard_map/ppermute | solution.py:243
  87.5 1.9 %collective-permute-start.1 = (bf16[4,256,768]{2,1,0:T(8,128)(2,1)S(1)}, bf16[4,256,768]{2,1,0:T(8,128)(2,1)S(1)}, u32[]{:S(2)}, u32[]{:S(2)}) collective-permute-start(bf16[4,256,768]{2,1,0:T(8,128)(2,1)S(1)} %get-tuple-element.6), channel_id=1, source_target_pairs={{0,1},{1,0},{2,3},{3,2},{4,5},{5,4},{6,7},{7,6},{8,9},{9,8},{10,11... | collective-permute-start | bytes 4718600 | tf_op jit(solution)/shard_map/ppermute | solution.py:243
  89.4 1.1 collective-permute-done.2
  90.5 1.3 %shard_map.48.first_ref = f32[384,768]{1,0:T(8,128)S(1)} custom-call(bf16[8,8,2,16,768]{4,3,2,1,0:T(8,128)(2,1)S(1)} %bitcast.7, bf16[1024,768]{1,0:T(8,128)(2,1)S(1)} %bitcast.10), custom_call_target="tpu_custom_call" | custom-call | flops 603979776 | bytes 6291456 | tf_op jit(solution)/shard_map/pallas_call | solution.py:212
  91.9 0.9 collective-permute-done.1
  92.8 1.9 %shard_map.49 = s16[8,304,128]{2,1,0:T(8,128)(2,1)S(1)} custom-call(bf16[8,8,2,16,768]{4,3,2,1,0:T(8,128)(2,1)S(1)} %bitcast.8, bf16[1024,768]{1,0:T(8,128)(2,1)S(1)} %bitcast.9, f32[384,768]{1,0:T(8,128)S(1)} %shard_map.48.first_ref), custom_call_target="tpu_custom_call" | custom-call | flops 603979776 | bytes 6291456 | tf_op jit(solution)/shard_map/pallas_call | solution.py:222
  94.7 25.1 %all_to_all.17.parts_ref = s16[8,304,128]{2,1,0:T(8,128)(2,1)S(1)} all-to-all(s16[8,304,128]{2,1,0:T(8,128)(2,1)S(1)} %shard_map.49), channel_id=1, replica_groups=mesh['y'=8,'x'=8,'z'=8,'c'=2] {'x'}, dimensions={0} | all-to-all | bytes 1245184 | tf_op jit(solution)/shard_map/all_to_all | solution.py:248
  119.8 0.8 shard_map.50
  (1 shorter events, 0.0 us)
Async XLA Ops:
  0.0 0.9 copy-start
  0.9 0.7 copy-start.1
  1.7 0.7 copy-start.2
  2.3 0.7 copy-start.3
  3.3 17.0 %collective-permute-start = (bf16[8,16,768]{2,1,0:T(8,128)(2,1)S(1)}, bf16[8,16,768]{2,1,0:T(8,128)(2,1)S(1)}, u32[]{:S(2)}, u32[]{:S(2)}) collective-permute-start(bf16[8,16,768]{2,1,0:T(8,128)(2,1)S(1)} %shard_map.47), channel_id=1, source_target_pairs={{0,1},{1,0},{2,3},{3,2},{4,5},{5,4},{6,7},{7,6},{8,9},{9,8},{10,11... | collective-permute-start | bytes 589832 | tf_op jit(solution)/shard_map/ppermute | solution.py:237
  82.3 8.2 %collective-permute-start.2 = (bf16[4,256,768]{2,1,0:T(8,128)(2,1)S(1)}, bf16[4,256,768]{2,1,0:T(8,128)(2,1)S(1)}, u32[]{:S(2)}, u32[]{:S(2)}) collective-permute-start(bf16[4,256,768]{2,1,0:T(8,128)(2,1)S(1)} %get-tuple-element.5), channel_id=1, source_target_pairs={{0,1},{1,0},{2,3},{3,2},{4,5},{5,4},{6,7},{7,6},{8,9},{9,8},{10,11... | collective-permute-start | bytes 4718600 | tf_op jit(solution)/shard_map/ppermute | solution.py:243
  87.5 5.3 %collective-permute-start.1 = (bf16[4,256,768]{2,1,0:T(8,128)(2,1)S(1)}, bf16[4,256,768]{2,1,0:T(8,128)(2,1)S(1)}, u32[]{:S(2)}, u32[]{:S(2)}) collective-permute-start(bf16[4,256,768]{2,1,0:T(8,128)(2,1)S(1)} %get-tuple-element.6), channel_id=1, source_target_pairs={{0,1},{1,0},{2,3},{3,2},{4,5},{5,4},{6,7},{7,6},{8,9},{9,8},{10,11... | collective-permute-start | bytes 4718600 | tf_op jit(solution)/shard_map/ppermute | solution.py:243

commit v5 on v4

--- a/solution.py
+++ b/solution.py
@@ -14,6 +14,7 @@
 AXES = ("y", "x", "z", "c")
 HALF = 384
 ROWS = 48
+ORDER = (0, 1, 7, 2, 6, 3, 5, 4)
 STEPS = 14
 VMEM = pl.BlockSpec(memory_space=pltpu.VMEM)
 SMALL = pltpu.CompilerParams(vmem_limit_bytes=8 * 2**20)
@@ -65,7 +66,17 @@
     return jnp.sum(jnp.where(here, jnp.broadcast_to(row, square), 0), axis=1, keepdims=True)
 
 
-def mask_kernel(of_left, coef_ref, weight_ref, pattern_ref, sizes_ref, out_ref):
+def mask_kernel(coef_at, weight_at, pattern_at, sizes_at, send_ref, keep_ref, coef_ref, weight_ref, pattern_ref, sizes_ref, arrived):
+    copies = [
+        pltpu.make_async_copy(there, here, arrived.at[i])
+        for i, (there, here) in enumerate(
+            ((coef_at, coef_ref), (pattern_at, pattern_ref), (sizes_at, sizes_ref), (weight_at, weight_ref))
+        )
+    ]
+    for copy in copies:
+        copy.start()
+    for copy in copies:
+        copy.wait()
     rows, width = coef_ref.shape
     tiles = width // N // AUX_PAD
     core = lax.axis_index("c")
@@ -75,55 +86,59 @@
     at_block = lax.broadcasted_iota(jnp.int32, pattern_ref.shape, 1) == block
     meets = jnp.sum(jnp.where(at_block, pattern_ref[...], 0), axis=1, keepdims=True)
     sizes = jnp.broadcast_to(jnp.where(meets > 0, as_column(sizes_ref[...]), 0), pattern_ref.shape)
-
-    def masked_tiles(to):
-        found = []
-        for atom in range(to * tiles, (to + 1) * tiles):
-            coef = coef_ref[:, atom * AUX_PAD : (atom + 1) * AUX_PAD].astype(jnp.float32)
-            found.append(jnp.where(lane < sizes[atom : atom + 1, :], coef, 0.0))
-        return found
-
-    def store(to, found):
+    weight = jnp.broadcast_to(as_column(weight_ref[...]), (rows, AUX_PAD))
+
+    def store(ref, to, found):
         for t in range(tiles):
-            out_ref[to, 0:rows, t * AUX_PAD : (t + 1) * AUX_PAD] = found[t].astype(jnp.bfloat16)
-
-    @pl.when(core == of_left)
-    def _():
+            ref[to, 0:rows, t * AUX_PAD : (t + 1) * AUX_PAD] = found[t].astype(jnp.bfloat16)
+
+    def run(left_ref, right_ref):
         for to in range(N):
-            store(to, into_order(masked_tiles(to)))
-
-    @pl.when(core != of_left)
-    def _():
-        weight = jnp.broadcast_to(as_column(weight_ref[...]), (rows, AUX_PAD))
-        for to in range(N):
-            store(to, [weight * m for m in masked_tiles(to)])
-
-
-def operand(of_left, height, coefficients, row_weight, pattern, aux_sizes):
+            masked = []
+            for atom in range(to * tiles, (to + 1) * tiles):
+                coef = coef_ref[:, atom * AUX_PAD : (atom + 1) * AUX_PAD].astype(jnp.float32)
+                masked.append(jnp.where(lane < sizes[atom : atom + 1, :], coef, 0.0))
+            store(left_ref, to, into_order(masked))
+            store(right_ref, to, [weight * m for m in masked])
+
+    @pl.when(core == 0)
+    def _():
+        run(keep_ref, send_ref)
+
+    @pl.when(core == 1)
+    def _():
+        run(send_ref, keep_ref)
+
+
+def operands(coefficients, row_weight, pattern, aux_sizes):
     rows, width = coefficients.shape
+    given = (coefficients, row_weight.reshape(1, -1), pattern.T, aux_sizes.reshape(1, -1))
     return pl.pallas_call(
-        functools.partial(mask_kernel, of_left),
-        out_shape=jax.ShapeDtypeStruct((N, height, width // N), jnp.bfloat16),
-        in_specs=[VMEM] * 4,
-        out_specs=VMEM,
+        mask_kernel,
+        out_shape=[jax.ShapeDtypeStruct((N, height, width // N), jnp.bfloat16) for height in (rows, 2 * rows)],
+        in_specs=[pl.BlockSpec(memory_space=pltpu.HBM)] * 4,
+        out_specs=[VMEM, VMEM],
+        scratch_shapes=[pltpu.VMEM(g.shape, g.dtype) for g in given] + [pltpu.SemaphoreType.DMA((4,))],
         compiler_params=SMALL,
-        cost_estimate=pl.CostEstimate(flops=8 * rows * width, bytes_accessed=4 * rows * width, transcendentals=0),
-    )(coefficients, row_weight.reshape(1, -1), pattern.T, aux_sizes.reshape(1, -1))
-
-
-def contract_part(own_ref, other_ref, gathered, part, write):
-    steps, inner, two, rows, wide = own_ref.shape
-    count = other_ref.shape[0] // (steps * two * rows)
+        cost_estimate=pl.CostEstimate(flops=8 * rows * width, bytes_accessed=6 * rows * width, transcendentals=0),
+    )(*given)
+
+
+def contract_part(own_refs, other_ref, gathered, part, write):
+    slots, places, two, rows, wide = own_refs[0].shape
     core = lax.axis_index("c")
+    mine = jnp.where(core == 0, lax.axis_index("z"), lax.axis_index("y"))
+    theirs = jnp.where(core == 0, lax.axis_index("y"), lax.axis_index("z"))
     tile = 256
 
     def gather(columns):
-        at = 0
-        for k in range(count):
-            for i in range(steps):
+        for k in range(slots):
+            inner = lax.rem(theirs + N - ORDER[part * slots + k], N)
+            for slot in range(len(ORDER)):
+                place = lax.rem(mine + N - ORDER[slot], N)
                 for h in range(two):
-                    gathered[at : at + rows, columns] = own_ref[i, part * count + k, 1 - h, :, columns]
-                    at += rows
+                    at = pl.multiple_of(((k * places + place) * two + h) * rows, rows)
+                    gathered[pl.ds(at, rows), columns] = own_refs[slot // slots][slot % slots, inner, 1 - h, :, columns]
 
     def run(left_ref, right_ref, columns):
         def column_tile(t, carry):
@@ -152,19 +167,19 @@
         run(other_ref, gathered, slice(HALF, 2 * HALF))
 
 
-def first_part_kernel(own_ref, other_ref, out_ref, gathered):
+def first_part_kernel(own_0, own_1, other_ref, out_ref, gathered):
     def write(start, value):
         out_ref[:, pl.ds(start, value.shape[1])] = value
 
-    contract_part(own_ref, other_ref, gathered, 0, write)
-
-
-def second_part_kernel(own_ref, other_ref, first_ref, out_ref, gathered, total):
+    contract_part((own_0, own_1), other_ref, gathered, 0, write)
+
+
+def second_part_kernel(own_0, own_1, other_ref, first_ref, out_ref, gathered, total):
     def write(start, value):
         columns = pl.ds(start, value.shape[1])
         total[:, columns] = first_ref[:, columns] + value
 
-    contract_part(own_ref, other_ref, gathered, 1, write)
+    contract_part((own_0, own_1), other_ref, gathered, 1, write)
 
     lanes = out_ref.shape[2]
     tiles = total.shape[1] // lanes
@@ -212,38 +227,41 @@
         return pl.pallas_call(
             first_part_kernel,
             out_shape=jax.ShapeDtypeStruct((HALF, wide), jnp.float32),
-            in_specs=[VMEM, VMEM],
+            in_specs=[VMEM] * 3,
             out_specs=VMEM,
             scratch_shapes=[gathered],
             compiler_params=params,
             cost_estimate=cost,
-        )(own, other)
+        )(*own, other)
     lanes = 128
     return pl.pallas_call(
         second_part_kernel,
         out_shape=jax.ShapeDtypeStruct((HALF // ROWS, wide // lanes * ROWS + 16, lanes), jnp.int16),
-        in_specs=[VMEM, VMEM, VMEM],
+        in_specs=[VMEM] * 4,
         out_specs=VMEM,
         scratch_shapes=[gathered, total],
         compiler_params=params,
         cost_estimate=cost,
-    )(own, other, first)
+    )(*own, other, first)
+
+
+def along(first, second, distance):
+    pairs = []
+    for ring in groups(first, second):
+        pairs += [(ring[i], ring[(i + distance) % N]) for i in range(N)]
+    return pairs
 
 
 def per_device(coefficients, row_weight, pattern, aux_sizes):
-    given = (coefficients, row_weight, pattern, aux_sizes)
     rows = coefficients.shape[0]
     swap = [(0, 1), (1, 0)]
-    received = lax.ppermute(operand(1, rows, *given), "c", swap)
-    blocks = lax.dynamic_update_slice(operand(0, 2 * rows, *given), received, (0, rows, 0))
+    send, keep = operands(coefficients, row_weight, pattern, aux_sizes)
+    blocks = lax.dynamic_update_slice(keep, lax.ppermute(send, "c", swap), (0, rows, 0))
     wide = blocks.shape[2]
-    blocks = exchange(blocks, "y", "z").reshape(1, N * 2 * rows, wide)
-    own = exchange(jnp.broadcast_to(blocks, (N, N * 2 * rows, wide)), "z", "y")
-    other = [
-        lax.ppermute(own[p * N // 2 : (p + 1) * N // 2], "c", swap).reshape(-1, wide)
-        for p in range(2)
-    ]
-    own = own.reshape(N, N, 2, rows, wide)
+    blocks = exchange(blocks, "y", "z").reshape(N, 2, rows, wide)
+    slots = [blocks if d == 0 else lax.ppermute(blocks, AXES, along("z", "y", d)) for d in ORDER]
+    own = [jnp.stack(slots[p * N // 2 : (p + 1) * N // 2]) for p in range(2)]
+    other = [lax.ppermute(part, "c", swap).reshape(-1, wide) for part in own]
     messages = contract(own, other[1], contract(own, other[0], None))
     parts = lax.all_to_all(messages, "x", 0, 0, tiled=True)
     return pl.pallas_call(

time: 121 us -> 121 us (level)
  blocking collectives: 86.7 us -> 39.3 us
  starting transfers between devices: 23 us -> 55.1 us
  waiting for transfers between devices: 2.85 us -> 17.5 us
    all_to_all x2 -> x1, blocking collectives: 61.6 us -> 14.3 us  [exchange(): lax.all_to_all(blocks, AXES, 0, 0, tiled=True, axis_index_groups=groups(f...]
    ppermute x3 -> x10, starting transfers between devices: 23 us -> 55.1 us  [the longest x7 28.9 us: per_device(): lax.ppermute(blocks, AXES, along('z', 'y', d))]
    ppermute x3 -> x10, waiting for transfers between devices: 2.85 us -> 17.5 us  [the longest x7 14.8 us: per_device(): lax.ppermute(blocks, AXES, along('z', 'y', d))]
  transfers between devices with their start and end apart: 3 -> 10, of which waited for: 3 -> 5; matrix products, arithmetic and copies ran while one was open for 0% -> 0% of each run, Pallas kernels for 1% -> 1%
where the time goes in v5:
time: 121 us; the launch traced here: 120 us
  starting transfers between devices  55.1 us (46%)
  blocking collectives  39.3 us (32%)
  waiting for transfers between devices  17.5 us (14%)
  Pallas kernels  4.67 us (4%)
  local copies, waits for them, and re-layouts  2.99 us (2%)
    ppermute x7, starting transfers between devices, per_device(): lax.ppermute(blocks, AXES, along('z', 'y', d))  28.9 us
    all_to_all x1, blocking collectives, per_device(): parts = lax.all_to_all(messages, 'x', 0, 0, tiled=True)  25.1 us
    ppermute x1, starting transfers between devices, per_device(): lax.ppermute(send, 'c', swap)  16.1 us
    ppermute x7, waiting for transfers between devices, per_device(): lax.ppermute(blocks, AXES, along('z', 'y', d))  14.8 us
    all_to_all x1, blocking collectives, exchange(): lax.all_to_all(blocks, AXES, 0, 0, tiled=True, axis_index_groups=groups(f...  14.3 us
    ppermute x2, starting transfers between devices, per_device(): other = [lax.ppermute(part, 'c', swap).reshape(-1, wide) for part in own]  10.2 us
    unnamed x8, local copies, waits for them, and re-layouts  2.97 us
  transfers between devices with their start and end apart: 10, of which 5 were waited for; matrix products, arithmetic and copies ran while one was open for 0% of the time, Pallas kernels for 1%

profile of v5, /device:TPU:1, one launch (start us, length us, event | category | flops | bytes accessed | tf_op | source)
XLA Modules:
  0.0 120.1 jit_solution(16134976519814993309)
XLA Ops:
  0.0 0.0 copy-start
  0.0 0.9 copy-done
  0.9 0.0 copy-start.1
  0.9 0.7 copy-done.1
  1.7 0.0 copy-start.2
  1.7 0.7 copy-done.2
  2.3 0.0 copy-start.3
  2.3 0.7 copy-done.3
  3.0 0.6 shard_map.46
  3.6 16.1 %collective-permute-start = (bf16[8,16,768]{2,1,0:T(8,128)(2,1)S(1)}, bf16[8,16,768]{2,1,0:T(8,128)(2,1)S(1)}, u32[]{:S(2)}, u32[]{:S(2)}) collective-permute-start(bf16[8,16,768]{2,1,0:T(8,128)(2,1)S(1)} %get-tuple-element.8), channel_id=1, source_target_pairs={{0,1},{1,0},{2,3},{3,2},{4,5},{5,4},{6,7},{7,6},{8,9},{9,8},{10,11... | collective-permute-start | bytes 589832 | tf_op jit(solution)/shard_map/ppermute | solution.py:259
  19.6 1.0 collective-permute-done
  20.7 14.3 %all_to_all.10 = bf16[8,32,768]{2,1,0:T(8,128)(2,1)S(1)} all-to-all(bf16[8,32,768]{2,1,0:T(8,128)(2,1)S(1)} %constant_dynamic-update-slice_fusion), channel_id=1, replica_groups={{0,128,256,384,512,640,768,896},{2,130,258,386,514,642,770,898},{4,132,..., dimensions={0} | all-to-all | bytes 786432 | tf_op jit(solution)/shard_map/all_to_all | solution.py:38
  35.0 4.4 %collective-permute-start.3 = (bf16[8,2,16,768]{3,2,1,0:T(8,128)(2,1)S(1)}, bf16[8,2,16,768]{3,2,1,0:T(8,128)(2,1)S(1)}, u32[]{:S(2)}, u32[]{:S(2)}) collective-permute-start(bf16[8,2,16,768]{3,2,1,0:T(8,128)(2,1)S(1)} %bitcast.19), channel_id=1, source_target_pairs={{0,4},{2,6},{4,8},{6,10},{8,12},{10,14},{12,0},{14,2},{16,20},{18,... | collective-permute-start | bytes 1179656 | tf_op jit(solution)/shard_map/ppermute | solution.py:262
  39.4 3.4 %collective-permute-start.2 = (bf16[8,2,16,768]{3,2,1,0:T(8,128)(2,1)S(1)}, bf16[8,2,16,768]{3,2,1,0:T(8,128)(2,1)S(1)}, u32[]{:S(2)}, u32[]{:S(2)}) collective-permute-start(bf16[8,2,16,768]{3,2,1,0:T(8,128)(2,1)S(1)} %bitcast.20), channel_id=1, source_target_pairs={{0,14},{2,0},{4,2},{6,4},{8,6},{10,8},{12,10},{14,12},{16,30},{18,... | collective-permute-start | bytes 1179656 | tf_op jit(solution)/shard_map/ppermute | solution.py:262
  42.8 1.9 %collective-permute-start.1 = (bf16[8,2,16,768]{3,2,1,0:T(8,128)(2,1)S(1)}, bf16[8,2,16,768]{3,2,1,0:T(8,128)(2,1)S(1)}, u32[]{:S(2)}, u32[]{:S(2)}) collective-permute-start(bf16[8,2,16,768]{3,2,1,0:T(8,128)(2,1)S(1)} %bitcast.21), channel_id=1, source_target_pairs={{0,2},{2,4},{4,6},{6,8},{8,10},{10,12},{12,14},{14,0},{16,18},{18,... | collective-permute-start | bytes 1179656 | tf_op jit(solution)/shard_map/ppermute | solution.py:262
  44.7 6.8 %collective-permute-start.7 = (bf16[8,2,16,768]{3,2,1,0:T(8,128)(2,1)S(1)}, bf16[8,2,16,768]{3,2,1,0:T(8,128)(2,1)S(1)}, u32[]{:S(2)}, u32[]{:S(2)}) collective-permute-start(bf16[8,2,16,768]{3,2,1,0:T(8,128)(2,1)S(1)} %bitcast.22), channel_id=1, source_target_pairs={{0,8},{2,10},{4,12},{6,14},{8,0},{10,2},{12,4},{14,6},{16,24},{18,... | collective-permute-start | bytes 1179656 | tf_op jit(solution)/shard_map/ppermute | solution.py:262
  51.6 3.8 %collective-permute-start.6 = (bf16[8,2,16,768]{3,2,1,0:T(8,128)(2,1)S(1)}, bf16[8,2,16,768]{3,2,1,0:T(8,128)(2,1)S(1)}, u32[]{:S(2)}, u32[]{:S(2)}) collective-permute-start(bf16[8,2,16,768]{3,2,1,0:T(8,128)(2,1)S(1)} %bitcast.23), channel_id=1, source_target_pairs={{0,10},{2,12},{4,14},{6,0},{8,2},{10,4},{12,6},{14,8},{16,26},{18,... | collective-permute-start | bytes 1179656 | tf_op jit(solution)/shard_map/ppermute | solution.py:262
  55.3 0.0 collective-permute-done.3
  55.3 3.3 %collective-permute-start.5 = (bf16[8,2,16,768]{3,2,1,0:T(8,128)(2,1)S(1)}, bf16[8,2,16,768]{3,2,1,0:T(8,128)(2,1)S(1)}, u32[]{:S(2)}, u32[]{:S(2)}) collective-permute-start(bf16[8,2,16,768]{3,2,1,0:T(8,128)(2,1)S(1)} %bitcast.24), channel_id=1, source_target_pairs={{0,6},{2,8},{4,10},{6,12},{8,14},{10,0},{12,2},{14,4},{16,22},{18,... | collective-permute-start | bytes 1179656 | tf_op jit(solution)/shard_map/ppermute | solution.py:262
  58.7 0.0 collective-permute-done.2
  58.7 5.2 %collective-permute-start.4 = (bf16[8,2,16,768]{3,2,1,0:T(8,128)(2,1)S(1)}, bf16[8,2,16,768]{3,2,1,0:T(8,128)(2,1)S(1)}, u32[]{:S(2)}, u32[]{:S(2)}) collective-permute-start(bf16[8,2,16,768]{3,2,1,0:T(8,128)(2,1)S(1)} %bitcast.25), channel_id=1, source_target_pairs={{0,12},{2,14},{4,0},{6,2},{8,4},{10,6},{12,8},{14,10},{16,28},{18,... | collective-permute-start | bytes 1179656 | tf_op jit(solution)/shard_map/ppermute | solution.py:262
  63.9 0.0 collective-permute-done.1
  63.9 0.2 pad_maximum_fusion.own_0
  64.1 4.1 %collective-permute-start.9 = (bf16[4,8,2,16,768]{4,3,2,1,0:T(8,128)(2,1)S(1)}, bf16[4,8,2,16,768]{4,3,2,1,0:T(8,128)(2,1)S(1)}, u32[]{:S(2)}, u32[]{:S(2)}) collective-permute-start(bf16[4,8,2,16,768]{4,3,2,1,0:T(8,128)(2,1)S(1)} %pad_maximum_fusion.own_0), channel_id=1, source_target_pairs={{0,1},{1,0},{2,3},{3,2},{4,5},{5,4},{6,7},{7,6},{8,9},{9,8},{10,11... | collective-permute-start | bytes 4718600 | tf_op jit(solution)/shard_map/ppermute | solution.py:264
  68.3 0.0 collective-permute-done.7
  68.3 4.3 %collective-permute-done.6 = bf16[8,2,16,768]{3,2,1,0:T(8,128)(2,1)S(1)} collective-permute-done((bf16[8,2,16,768]{3,2,1,0:T(8,128)(2,1)S(1)}, bf16[8,2,16,768]{3,2,1,0:T(8,128)(2,1)S(1)}, u32[]{:S(2)}, u32[]{:S(2)}) %collective-permute-start.6) | collective-permute-done | bytes 393248 | tf_op jit(solution)/shard_map/ppermute | solution.py:262
  72.6 4.9 %collective-permute-done.5 = bf16[8,2,16,768]{3,2,1,0:T(8,128)(2,1)S(1)} collective-permute-done((bf16[8,2,16,768]{3,2,1,0:T(8,128)(2,1)S(1)}, bf16[8,2,16,768]{3,2,1,0:T(8,128)(2,1)S(1)}, u32[]{:S(2)}, u32[]{:S(2)}) %collective-permute-start.5) | collective-permute-done | bytes 393248 | tf_op jit(solution)/shard_map/ppermute | solution.py:262
  77.5 5.6 %collective-permute-done.4 = bf16[8,2,16,768]{3,2,1,0:T(8,128)(2,1)S(1)} collective-permute-done((bf16[8,2,16,768]{3,2,1,0:T(8,128)(2,1)S(1)}, bf16[8,2,16,768]{3,2,1,0:T(8,128)(2,1)S(1)}, u32[]{:S(2)}, u32[]{:S(2)}) %collective-permute-start.4) | collective-permute-done | bytes 393248 | tf_op jit(solution)/shard_map/ppermute | solution.py:262
  83.1 0.2 pad_maximum_fusion.1.own_1
  83.3 6.0 %collective-permute-start.8 = (bf16[4,8,2,16,768]{4,3,2,1,0:T(8,128)(2,1)S(1)}, bf16[4,8,2,16,768]{4,3,2,1,0:T(8,128)(2,1)S(1)}, u32[]{:S(2)}, u32[]{:S(2)}) collective-permute-start(bf16[4,8,2,16,768]{4,3,2,1,0:T(8,128)(2,1)S(1)} %pad_maximum_fusion.1.own_1), channel_id=1, source_target_pairs={{0,1},{1,0},{2,3},{3,2},{4,5},{5,4},{6,7},{7,6},{8,9},{9,8},{10,11... | collective-permute-start | bytes 4718600 | tf_op jit(solution)/shard_map/ppermute | solution.py:264
  89.3 0.0 collective-permute-done.9
  89.3 1.4 %shard_map.47.first_ref = f32[384,768]{1,0:T(8,128)S(1)} custom-call(bf16[4,8,2,16,768]{4,3,2,1,0:T(8,128)(2,1)S(1)} %pad_maximum_fusion.own_0, bf16[4,8,2,16,768]{4,3,2,1,0:T(8,128)(2,1)S(1)} %pad_maximum_fusion.1.own_1, bf16[1024,768]{1,0:T(8,128)(2,1)S(1)} %bitcast.14), custom_call_target="tpu_custom_call" | custom-call | flops 603979776 | bytes 6291456 | tf_op jit(solution)/shard_map/pallas_call | solution.py:227
  90.7 1.6 %collective-permute-done.8 = bf16[4,8,2,16,768]{4,3,2,1,0:T(8,128)(2,1)S(1)} collective-permute-done((bf16[4,8,2,16,768]{4,3,2,1,0:T(8,128)(2,1)S(1)}, bf16[4,8,2,16,768]{4,3,2,1,0:T(8,128)(2,1)S(1)}, u32[]{:S(2)}, u32[]{:S(2)}) %collective-permute-start.8) | collective-permute-done | bytes 1572896 | tf_op jit(solution)/shard_map/ppermute | solution.py:264
  92.3 1.9 %shard_map.48 = s16[8,304,128]{2,1,0:T(8,128)(2,1)S(1)} custom-call(bf16[4,8,2,16,768]{4,3,2,1,0:T(8,128)(2,1)S(1)} %pad_maximum_fusion.own_0, bf16[4,8,2,16,768]{4,3,2,1,0:T(8,128)(2,1)S(1)} %pad_maximum_fusion.1.own_1, bf16[1024,768]{1,0:T(8,128)(2,1)S(1)} %bitcast.15, f32[384,768]{1,0:T(8,128)S(1)} %shard_map.47.first_ref), custom_call_target="tpu_custom_call" | custom-call | flops 603979776 | bytes 6291456 | tf_op jit(solution)/shard_map/pallas_call | solution.py:237
  94.2 25.1 %all_to_all.11.parts_ref = s16[8,304,128]{2,1,0:T(8,128)(2,1)S(1)} all-to-all(s16[8,304,128]{2,1,0:T(8,128)(2,1)S(1)} %shard_map.48), channel_id=1, replica_groups=mesh['y'=8,'x'=8,'z'=8,'c'=2] {'x'}, dimensions={0} | all-to-all | bytes 1245184 | tf_op jit(solution)/shard_map/all_to_all | solution.py:266
  119.3 0.8 shard_map.49
  (1 shorter events, 0.0 us)
Async XLA Ops:
  0.0 0.9 copy-start
  0.9 0.7 copy-start.1
  1.7 0.7 copy-start.2
  2.3 0.7 copy-start.3
  3.6 17.1 %collective-permute-start = (bf16[8,16,768]{2,1,0:T(8,128)(2,1)S(1)}, bf16[8,16,768]{2,1,0:T(8,128)(2,1)S(1)}, u32[]{:S(2)}, u32[]{:S(2)}) collective-permute-start(bf16[8,16,768]{2,1,0:T(8,128)(2,1)S(1)} %get-tuple-element.8), channel_id=1, source_target_pairs={{0,1},{1,0},{2,3},{3,2},{4,5},{5,4},{6,7},{7,6},{8,9},{9,8},{10,11... | collective-permute-start | bytes 589832 | tf_op jit(solution)/shard_map/ppermute | solution.py:259
  35.0 20.3 %collective-permute-start.3 = (bf16[8,2,16,768]{3,2,1,0:T(8,128)(2,1)S(1)}, bf16[8,2,16,768]{3,2,1,0:T(8,128)(2,1)S(1)}, u32[]{:S(2)}, u32[]{:S(2)}) collective-permute-start(bf16[8,2,16,768]{3,2,1,0:T(8,128)(2,1)S(1)} %bitcast.19), channel_id=1, source_target_pairs={{0,4},{2,6},{4,8},{6,10},{8,12},{10,14},{12,0},{14,2},{16,20},{18,... | collective-permute-start | bytes 1179656 | tf_op jit(solution)/shard_map/ppermute | solution.py:262
  39.4 19.2 %collective-permute-start.2 = (bf16[8,2,16,768]{3,2,1,0:T(8,128)(2,1)S(1)}, bf16[8,2,16,768]{3,2,1,0:T(8,128)(2,1)S(1)}, u32[]{:S(2)}, u32[]{:S(2)}) collective-permute-start(bf16[8,2,16,768]{3,2,1,0:T(8,128)(2,1)S(1)} %bitcast.20), channel_id=1, source_target_pairs={{0,14},{2,0},{4,2},{6,4},{8,6},{10,8},{12,10},{14,12},{16,30},{18,... | collective-permute-start | bytes 1179656 | tf_op jit(solution)/shard_map/ppermute | solution.py:262
  42.8 21.1 %collective-permute-start.1 = (bf16[8,2,16,768]{3,2,1,0:T(8,128)(2,1)S(1)}, bf16[8,2,16,768]{3,2,1,0:T(8,128)(2,1)S(1)}, u32[]{:S(2)}, u32[]{:S(2)}) collective-permute-start(bf16[8,2,16,768]{3,2,1,0:T(8,128)(2,1)S(1)} %bitcast.21), channel_id=1, source_target_pairs={{0,2},{2,4},{4,6},{6,8},{8,10},{10,12},{12,14},{14,0},{16,18},{18,... | collective-permute-start | bytes 1179656 | tf_op jit(solution)/shard_map/ppermute | solution.py:262
  44.7 23.5 %collective-permute-start.7 = (bf16[8,2,16,768]{3,2,1,0:T(8,128)(2,1)S(1)}, bf16[8,2,16,768]{3,2,1,0:T(8,128)(2,1)S(1)}, u32[]{:S(2)}, u32[]{:S(2)}) collective-permute-start(bf16[8,2,16,768]{3,2,1,0:T(8,128)(2,1)S(1)} %bitcast.22), channel_id=1, source_target_pairs={{0,8},{2,10},{4,12},{6,14},{8,0},{10,2},{12,4},{14,6},{16,24},{18,... | collective-permute-start | bytes 1179656 | tf_op jit(solution)/shard_map/ppermute | solution.py:262
  51.6 21.1 %collective-permute-start.6 = (bf16[8,2,16,768]{3,2,1,0:T(8,128)(2,1)S(1)}, bf16[8,2,16,768]{3,2,1,0:T(8,128)(2,1)S(1)}, u32[]{:S(2)}, u32[]{:S(2)}) collective-permute-start(bf16[8,2,16,768]{3,2,1,0:T(8,128)(2,1)S(1)} %bitcast.23), channel_id=1, source_target_pairs={{0,10},{2,12},{4,14},{6,0},{8,2},{10,4},{12,6},{14,8},{16,26},{18,... | collective-permute-start | bytes 1179656 | tf_op jit(solution)/shard_map/ppermute | solution.py:262
  55.3 22.1 %collective-permute-start.5 = (bf16[8,2,16,768]{3,2,1,0:T(8,128)(2,1)S(1)}, bf16[8,2,16,768]{3,2,1,0:T(8,128)(2,1)S(1)}, u32[]{:S(2)}, u32[]{:S(2)}) collective-permute-start(bf16[8,2,16,768]{3,2,1,0:T(8,128)(2,1)S(1)} %bitcast.24), channel_id=1, source_target_pairs={{0,6},{2,8},{4,10},{6,12},{8,14},{10,0},{12,2},{14,4},{16,22},{18,... | collective-permute-start | bytes 1179656 | tf_op jit(solution)/shard_map/ppermute | solution.py:262
  58.7 24.4 %collective-permute-start.4 = (bf16[8,2,16,768]{3,2,1,0:T(8,128)(2,1)S(1)}, bf16[8,2,16,768]{3,2,1,0:T(8,128)(2,1)S(1)}, u32[]{:S(2)}, u32[]{:S(2)}) collective-permute-start(bf16[8,2,16,768]{3,2,1,0:T(8,128)(2,1)S(1)} %bitcast.25), channel_id=1, source_target_pairs={{0,12},{2,14},{4,0},{6,2},{8,4},{10,6},{12,8},{14,10},{16,28},{18,... | collective-permute-start | bytes 1179656 | tf_op jit(solution)/shard_map/ppermute | solution.py:262
  64.1 25.2 %collective-permute-start.9 = (bf16[4,8,2,16,768]{4,3,2,1,0:T(8,128)(2,1)S(1)}, bf16[4,8,2,16,768]{4,3,2,1,0:T(8,128)(2,1)S(1)}, u32[]{:S(2)}, u32[]{:S(2)}) collective-permute-start(bf16[4,8,2,16,768]{4,3,2,1,0:T(8,128)(2,1)S(1)} %pad_maximum_fusion.own_0), channel_id=1, source_target_pairs={{0,1},{1,0},{2,3},{3,2},{4,5},{5,4},{6,7},{7,6},{8,9},{9,8},{10,11... | collective-permute-start | bytes 4718600 | tf_op jit(solution)/shard_map/ppermute | solution.py:264
  83.3 9.1 %collective-permute-start.8 = (bf16[4,8,2,16,768]{4,3,2,1,0:T(8,128)(2,1)S(1)}, bf16[4,8,2,16,768]{4,3,2,1,0:T(8,128)(2,1)S(1)}, u32[]{:S(2)}, u32[]{:S(2)}) collective-permute-start(bf16[4,8,2,16,768]{4,3,2,1,0:T(8,128)(2,1)S(1)} %pad_maximum_fusion.1.own_1), channel_id=1, source_target_pairs={{0,1},{1,0},{2,3},{3,2},{4,5},{5,4},{6,7},{7,6},{8,9},{9,8},{10,11... | collective-permute-start | bytes 4718600 | tf_op jit(solution)/shard_map/ppermute | solution.py:264

commit v6 on v5

--- a/solution.py
+++ b/solution.py
@@ -63,30 +63,23 @@
     n = row.shape[1]
     square = (n, n)
     here = lax.broadcasted_iota(jnp.int32, square, 0) == lax.broadcasted_iota(jnp.int32, square, 1)
-    return jnp.sum(jnp.where(here, jnp.broadcast_to(row, square), 0), axis=1, keepdims=True)
-
-
-def mask_kernel(coef_at, weight_at, pattern_at, sizes_at, send_ref, keep_ref, coef_ref, weight_ref, pattern_ref, sizes_ref, arrived):
-    copies = [
-        pltpu.make_async_copy(there, here, arrived.at[i])
-        for i, (there, here) in enumerate(
-            ((coef_at, coef_ref), (pattern_at, pattern_ref), (sizes_at, sizes_ref), (weight_at, weight_ref))
-        )
-    ]
-    for copy in copies:
-        copy.start()
-    for copy in copies:
-        copy.wait()
+    return jnp.sum(jnp.where(here, jnp.broadcast_to(row, square), 0.0), axis=1, keepdims=True)
+
+
+def mask_kernel(coef_ref, known_ref, send_ref, keep_ref):
     rows, width = coef_ref.shape
     tiles = width // N // AUX_PAD
     core = lax.axis_index("c")
     device = ((lax.axis_index("y") * N + lax.axis_index("x")) * N + lax.axis_index("z")) * 2 + core
     block = device * rows // PAIR_ROWS
     lane = lax.broadcasted_iota(jnp.int32, (rows, AUX_PAD), 1)
-    at_block = lax.broadcasted_iota(jnp.int32, pattern_ref.shape, 1) == block
-    meets = jnp.sum(jnp.where(at_block, pattern_ref[...], 0), axis=1, keepdims=True)
-    sizes = jnp.broadcast_to(jnp.where(meets > 0, as_column(sizes_ref[...]), 0), pattern_ref.shape)
-    weight = jnp.broadcast_to(as_column(weight_ref[...]), (rows, AUX_PAD))
+    atoms = width // AUX_PAD
+    pattern = known_ref[0:atoms, :]
+    at_block = lax.broadcasted_iota(jnp.int32, pattern.shape, 1) == block
+    meets = jnp.sum(jnp.where(at_block, pattern, 0.0), axis=1, keepdims=True)
+    sizes = jnp.where(meets > 0, as_column(known_ref[atoms : atoms + 1, 0:atoms]), 0.0)
+    sizes = jnp.broadcast_to(sizes, (atoms, AUX_PAD)).astype(jnp.int32)
+    weight = jnp.broadcast_to(as_column(known_ref[atoms + 1 : atoms + 2, 0:rows]), (rows, AUX_PAD))
 
     def store(ref, to, found):
         for t in range(tiles):
@@ -112,16 +105,16 @@
 
 def operands(coefficients, row_weight, pattern, aux_sizes):
     rows, width = coefficients.shape
-    given = (coefficients, row_weight.reshape(1, -1), pattern.T, aux_sizes.reshape(1, -1))
+    as_row = lambda v: jnp.pad(v.astype(jnp.float32).reshape(1, -1), ((0, 0), (0, pattern.shape[0] - v.shape[0])))
+    known = jnp.concatenate([pattern.T.astype(jnp.float32), as_row(aux_sizes), as_row(row_weight)])
     return pl.pallas_call(
         mask_kernel,
         out_shape=[jax.ShapeDtypeStruct((N, height, width // N), jnp.bfloat16) for height in (rows, 2 * rows)],
-        in_specs=[pl.BlockSpec(memory_space=pltpu.HBM)] * 4,
+        in_specs=[VMEM, VMEM],
         out_specs=[VMEM, VMEM],
-        scratch_shapes=[pltpu.VMEM(g.shape, g.dtype) for g in given] + [pltpu.SemaphoreType.DMA((4,))],
         compiler_params=SMALL,
         cost_estimate=pl.CostEstimate(flops=8 * rows * width, bytes_accessed=6 * rows * width, transcendentals=0),
-    )(*given)
+    )(coefficients, known)
 
 
 def contract_part(own_refs, other_ref, gathered, part, write):
@@ -259,8 +252,11 @@
     blocks = lax.dynamic_update_slice(keep, lax.ppermute(send, "c", swap), (0, rows, 0))
     wide = blocks.shape[2]
     blocks = exchange(blocks, "y", "z").reshape(N, 2, rows, wide)
-    slots = [blocks if d == 0 else lax.ppermute(blocks, AXES, along("z", "y", d)) for d in ORDER]
-    own = [jnp.stack(slots[p * N // 2 : (p + 1) * N // 2]) for p in range(2)]
+    move = lambda value, d: lax.ppermute(value, AXES, along("z", "y", d))
+    slot = {0: blocks, 2: move(blocks, 2), 6: move(blocks, -2), 1: move(blocks, 1), 7: move(blocks, -1)}
+    slot[3], slot[5] = move(slot[2], 1), move(slot[6], -1)
+    slot[4] = jnp.concatenate([move(slot[2][: N // 2], 2), move(slot[6][N // 2 :], -2)])
+    own = [jnp.stack([slot[d] for d in ORDER[p * N // 2 : (p + 1) * N // 2]]) for p in range(2)]
     other = [lax.ppermute(part, "c", swap).reshape(-1, wide) for part in own]
     messages = contract(own, other[1], contract(own, other[0], None))
     parts = lax.all_to_all(messages, "x", 0, 0, tiled=True)

time: 121 us -> 111 us (0.917)
  waiting for transfers between devices: 17.5 us -> 4.26 us
  starting transfers between devices: 55.1 us -> 58.8 us
  other arithmetic: 0.4 us -> 2.5 us
  local copies, waits for them, and re-layouts: 2.99 us -> 0.97 us
    ppermute x7 -> x8, waiting for transfers between devices: 14.8 us -> 1.6 us  [per_device(): move = lambda value, d: lax.ppermute(value, AXES, along('z', 'y', d))]
    ppermute x2, starting transfers between devices: 10.2 us -> 14.1 us  [per_device(): other = [lax.ppermute(part, 'c', swap).reshape(-1, wide) for part in own]]
    unnamed x8 -> x2, local copies, waits for them, and re-layouts: 2.97 us -> 0.93 us
    ppermute x7 -> x8, starting transfers between devices: 28.9 us -> 28.6 us  [per_device(): move = lambda value, d: lax.ppermute(value, AXES, along('z', 'y', d))]
  transfers between devices with their start and end apart: 10 -> 11, of which waited for: 5 -> 4; matrix products, arithmetic and copies ran while one was open for 0% -> 0% of each run, Pallas kernels for 1% -> 1%
where the time goes in v6:
time: 111 us; the launch traced here: 110 us
  starting transfers between devices  58.8 us (53%)
  blocking collectives  39.3 us (35%)
  Pallas kernels  4.35 us (4%)
  waiting for transfers between devices  4.26 us (4%)
  other arithmetic  2.5 us (2%)
    ppermute x8, starting transfers between devices, per_device(): move = lambda value, d: lax.ppermute(value, AXES, along('z', 'y', d))  28.6 us
    all_to_all x1, blocking collectives, per_device(): parts = lax.all_to_all(messages, 'x', 0, 0, tiled=True)  25.1 us
    ppermute x1, starting transfers between devices, per_device(): lax.ppermute(send, 'c', swap)  16.1 us
    all_to_all x1, blocking collectives, exchange(): lax.all_to_all(blocks, AXES, 0, 0, tiled=True, axis_index_groups=groups(f...  14.3 us
    ppermute x2, starting transfers between devices, per_device(): other = [lax.ppermute(part, 'c', swap).reshape(-1, wide) for part in own]  14.1 us
  transfers between devices with their start and end apart: 11, of which 4 were waited for; matrix products, arithmetic and copies ran while one was open for 0% of the time, Pallas kernels for 1%

profile of v6, /device:TPU:1, one launch (start us, length us, event | category | flops | bytes accessed | tf_op | source)
XLA Modules:
  0.0 110.4 jit_solution(10585026457754900819)
XLA Ops:
  0.0 0.7 convert_bitcast_fusion.1
  0.7 0.7 convert_bitcast_fusion
  1.4 0.7 select_maximum_fusion.known_ref
  2.1 0.0 copy-start
  2.1 0.9 copy-done
  3.0 0.3 shard_map.46
  3.3 16.1 %collective-permute-start = (bf16[8,16,768]{2,1,0:T(8,128)(2,1)S(1)}, bf16[8,16,768]{2,1,0:T(8,128)(2,1)S(1)}, u32[]{:S(2)}, u32[]{:S(2)}) collective-permute-start(bf16[8,16,768]{2,1,0:T(8,128)(2,1)S(1)} %get-tuple-element.8), channel_id=1, source_target_pairs={{0,1},{1,0},{2,3},{3,2},{4,5},{5,4},{6,7},{7,6},{8,9},{9,8},{10,11... | collective-permute-start | bytes 589832 | tf_op jit(solution)/shard_map/ppermute | solution.py:252
  19.3 1.0 collective-permute-done
  20.4 14.3 %all_to_all.10 = bf16[8,32,768]{2,1,0:T(8,128)(2,1)S(1)} all-to-all(bf16[8,32,768]{2,1,0:T(8,128)(2,1)S(1)} %constant_dynamic-update-slice_fusion), channel_id=1, replica_groups={{0,128,256,384,512,640,768,896},{2,130,258,386,514,642,770,898},{4,132,..., dimensions={0} | all-to-all | bytes 786432 | tf_op jit(solution)/shard_map/all_to_all | solution.py:38
  34.7 6.6 %collective-permute-start.4 = (bf16[8,2,16,768]{3,2,1,0:T(8,128)(2,1)S(1)}, bf16[8,2,16,768]{3,2,1,0:T(8,128)(2,1)S(1)}, u32[]{:S(2)}, u32[]{:S(2)}) collective-permute-start(bf16[8,2,16,768]{3,2,1,0:T(8,128)(2,1)S(1)} %bitcast.19), channel_id=1, source_target_pairs={{0,12},{2,14},{4,0},{6,2},{8,4},{10,6},{12,8},{14,10},{16,28},{18,... | collective-permute-start | bytes 1179656 | tf_op jit(solution)/shard_map/ppermute | solution.py:255
  41.3 1.9 %collective-permute-start.3 = (bf16[8,2,16,768]{3,2,1,0:T(8,128)(2,1)S(1)}, bf16[8,2,16,768]{3,2,1,0:T(8,128)(2,1)S(1)}, u32[]{:S(2)}, u32[]{:S(2)}) collective-permute-start(bf16[8,2,16,768]{3,2,1,0:T(8,128)(2,1)S(1)} %bitcast.20), channel_id=1, source_target_pairs={{0,4},{2,6},{4,8},{6,10},{8,12},{10,14},{12,0},{14,2},{16,20},{18,... | collective-permute-start | bytes 1179656 | tf_op jit(solution)/shard_map/ppermute | solution.py:255
  43.2 4.8 %collective-permute-start.2 = (bf16[8,2,16,768]{3,2,1,0:T(8,128)(2,1)S(1)}, bf16[8,2,16,768]{3,2,1,0:T(8,128)(2,1)S(1)}, u32[]{:S(2)}, u32[]{:S(2)}) collective-permute-start(bf16[8,2,16,768]{3,2,1,0:T(8,128)(2,1)S(1)} %bitcast.21), channel_id=1, source_target_pairs={{0,14},{2,0},{4,2},{6,4},{8,6},{10,8},{12,10},{14,12},{16,30},{18,... | collective-permute-start | bytes 1179656 | tf_op jit(solution)/shard_map/ppermute | solution.py:255
  48.0 1.9 %collective-permute-start.1 = (bf16[8,2,16,768]{3,2,1,0:T(8,128)(2,1)S(1)}, bf16[8,2,16,768]{3,2,1,0:T(8,128)(2,1)S(1)}, u32[]{:S(2)}, u32[]{:S(2)}) collective-permute-start(bf16[8,2,16,768]{3,2,1,0:T(8,128)(2,1)S(1)} %bitcast.22), channel_id=1, source_target_pairs={{0,2},{2,4},{4,6},{6,8},{8,10},{10,12},{12,14},{14,0},{16,18},{18,... | collective-permute-start | bytes 1179656 | tf_op jit(solution)/shard_map/ppermute | solution.py:255
  49.9 0.2 collective-permute-done.4
  50.2 4.4 %collective-permute-start.6 = (bf16[8,2,16,768]{3,2,1,0:T(8,128)(2,1)S(1)}, bf16[8,2,16,768]{3,2,1,0:T(8,128)(2,1)S(1)}, u32[]{:S(2)}, u32[]{:S(2)}) collective-permute-start(bf16[8,2,16,768]{3,2,1,0:T(8,128)(2,1)S(1)} %collective-permute-done.4), channel_id=1, source_target_pairs={{0,14},{2,0},{4,2},{6,4},{8,6},{10,8},{12,10},{14,12},{16,30},{18,... | collective-permute-start | bytes 1179656 | tf_op jit(solution)/shard_map/ppermute | solution.py:255
  54.6 1.3 %collective-permute-done.3 = bf16[8,2,16,768]{3,2,1,0:T(8,128)(2,1)S(1)} collective-permute-done((bf16[8,2,16,768]{3,2,1,0:T(8,128)(2,1)S(1)}, bf16[8,2,16,768]{3,2,1,0:T(8,128)(2,1)S(1)}, u32[]{:S(2)}, u32[]{:S(2)}) %collective-permute-start.3) | collective-permute-done | bytes 393248 | tf_op jit(solution)/shard_map/ppermute | solution.py:255
  55.9 2.9 %collective-permute-start.5 = (bf16[8,2,16,768]{3,2,1,0:T(8,128)(2,1)S(1)}, bf16[8,2,16,768]{3,2,1,0:T(8,128)(2,1)S(1)}, u32[]{:S(2)}, u32[]{:S(2)}) collective-permute-start(bf16[8,2,16,768]{3,2,1,0:T(8,128)(2,1)S(1)} %collective-permute-done.3), channel_id=1, source_target_pairs={{0,2},{2,4},{4,6},{6,8},{8,10},{10,12},{12,14},{14,0},{16,18},{18,... | collective-permute-start | bytes 1179656 | tf_op jit(solution)/shard_map/ppermute | solution.py:255
  58.8 2.9 %collective-permute-start.8 = (bf16[4,2,16,768]{3,2,1,0:T(8,128)(2,1)S(1)}, bf16[4,2,16,768]{3,2,1,0:T(8,128)(2,1)S(1)}, u32[]{:S(2)}, u32[]{:S(2)}) collective-permute-start(bf16[4,2,16,768]{3,2,1,0:T(8,128)(2,1)S(1)} %slice.9), channel_id=1, source_target_pairs={{0,12},{2,14},{4,0},{6,2},{8,4},{10,6},{12,8},{14,10},{16,28},{18,... | collective-permute-start | bytes 589832 | tf_op jit(solution)/shard_map/ppermute | solution.py:255
  61.7 0.0 collective-permute-done.2
  61.7 3.3 %collective-permute-start.7 = (bf16[4,2,16,768]{3,2,1,0:T(8,128)(2,1)S(1)}, bf16[4,2,16,768]{3,2,1,0:T(8,128)(2,1)S(1)}, u32[]{:S(2)}, u32[]{:S(2)}) collective-permute-start(bf16[4,2,16,768]{3,2,1,0:T(8,128)(2,1)S(1)} %slice.8), channel_id=1, source_target_pairs={{0,4},{2,6},{4,8},{6,10},{8,12},{10,14},{12,0},{14,2},{16,20},{18,... | collective-permute-start | bytes 589832 | tf_op jit(solution)/shard_map/ppermute | solution.py:255
  65.0 0.0 collective-permute-done.1
  65.0 0.2 pad_maximum_fusion.own_0
  65.2 5.4 %collective-permute-start.10 = (bf16[4,8,2,16,768]{4,3,2,1,0:T(8,128)(2,1)S(1)}, bf16[4,8,2,16,768]{4,3,2,1,0:T(8,128)(2,1)S(1)}, u32[]{:S(2)}, u32[]{:S(2)}) collective-permute-start(bf16[4,8,2,16,768]{4,3,2,1,0:T(8,128)(2,1)S(1)} %pad_maximum_fusion.own_0), channel_id=1, source_target_pairs={{0,1},{1,0},{2,3},{3,2},{4,5},{5,4},{6,7},{7,6},{8,9},{9,8},{10,11... | collective-permute-start | bytes 4718600 | tf_op jit(solution)/shard_map/ppermute | solution.py:260
  70.6 0.0 collective-permute-done.8
  70.6 0.0 collective-permute-done.7
  70.7 0.0 collective-permute-done.6
  70.7 0.0 collective-permute-done.5
  70.7 0.2 pad_maximum_fusion.1.own_1
  70.9 8.7 %collective-permute-start.9 = (bf16[4,8,2,16,768]{4,3,2,1,0:T(8,128)(2,1)S(1)}, bf16[4,8,2,16,768]{4,3,2,1,0:T(8,128)(2,1)S(1)}, u32[]{:S(2)}, u32[]{:S(2)}) collective-permute-start(bf16[4,8,2,16,768]{4,3,2,1,0:T(8,128)(2,1)S(1)} %pad_maximum_fusion.1.own_1), channel_id=1, source_target_pairs={{0,1},{1,0},{2,3},{3,2},{4,5},{5,4},{6,7},{7,6},{8,9},{9,8},{10,11... | collective-permute-start | bytes 4718600 | tf_op jit(solution)/shard_map/ppermute | solution.py:260
  79.6 0.0 collective-permute-done.10
  79.6 1.4 %shard_map.47.first_ref = f32[384,768]{1,0:T(8,128)S(1)} custom-call(bf16[4,8,2,16,768]{4,3,2,1,0:T(8,128)(2,1)S(1)} %pad_maximum_fusion.own_0, bf16[4,8,2,16,768]{4,3,2,1,0:T(8,128)(2,1)S(1)} %pad_maximum_fusion.1.own_1, bf16[1024,768]{1,0:T(8,128)(2,1)S(1)} %bitcast.17), custom_call_target="tpu_custom_call" | custom-call | flops 603979776 | bytes 6291456 | tf_op jit(solution)/shard_map/pallas_call | solution.py:220
  81.0 1.6 %collective-permute-done.9 = bf16[4,8,2,16,768]{4,3,2,1,0:T(8,128)(2,1)S(1)} collective-permute-done((bf16[4,8,2,16,768]{4,3,2,1,0:T(8,128)(2,1)S(1)}, bf16[4,8,2,16,768]{4,3,2,1,0:T(8,128)(2,1)S(1)}, u32[]{:S(2)}, u32[]{:S(2)}) %collective-permute-start.9) | collective-permute-done | bytes 1572896 | tf_op jit(solution)/shard_map/ppermute | solution.py:260
  82.6 1.9 %shard_map.48 = s16[8,304,128]{2,1,0:T(8,128)(2,1)S(1)} custom-call(bf16[4,8,2,16,768]{4,3,2,1,0:T(8,128)(2,1)S(1)} %pad_maximum_fusion.own_0, bf16[4,8,2,16,768]{4,3,2,1,0:T(8,128)(2,1)S(1)} %pad_maximum_fusion.1.own_1, bf16[1024,768]{1,0:T(8,128)(2,1)S(1)} %bitcast.18, f32[384,768]{1,0:T(8,128)S(1)} %shard_map.47.first_ref), custom_call_target="tpu_custom_call" | custom-call | flops 603979776 | bytes 6291456 | tf_op jit(solution)/shard_map/pallas_call | solution.py:230
  84.5 25.1 %all_to_all.11.parts_ref = s16[8,304,128]{2,1,0:T(8,128)(2,1)S(1)} all-to-all(s16[8,304,128]{2,1,0:T(8,128)(2,1)S(1)} %shard_map.48), channel_id=1, replica_groups=mesh['y'=8,'x'=8,'z'=8,'c'=2] {'x'}, dimensions={0} | all-to-all | bytes 1245184 | tf_op jit(solution)/shard_map/all_to_all | solution.py:262
  109.6 0.8 shard_map.49
  (4 shorter events, 0.1 us)
Async XLA Ops:
  2.1 0.9 copy-start
  3.3 17.1 %collective-permute-start = (bf16[8,16,768]{2,1,0:T(8,128)(2,1)S(1)}, bf16[8,16,768]{2,1,0:T(8,128)(2,1)S(1)}, u32[]{:S(2)}, u32[]{:S(2)}) collective-permute-start(bf16[8,16,768]{2,1,0:T(8,128)(2,1)S(1)} %get-tuple-element.8), channel_id=1, source_target_pairs={{0,1},{1,0},{2,3},{3,2},{4,5},{5,4},{6,7},{7,6},{8,9},{9,8},{10,11... | collective-permute-start | bytes 589832 | tf_op jit(solution)/shard_map/ppermute | solution.py:252
  34.7 15.5 %collective-permute-start.4 = (bf16[8,2,16,768]{3,2,1,0:T(8,128)(2,1)S(1)}, bf16[8,2,16,768]{3,2,1,0:T(8,128)(2,1)S(1)}, u32[]{:S(2)}, u32[]{:S(2)}) collective-permute-start(bf16[8,2,16,768]{3,2,1,0:T(8,128)(2,1)S(1)} %bitcast.19), channel_id=1, source_target_pairs={{0,12},{2,14},{4,0},{6,2},{8,4},{10,6},{12,8},{14,10},{16,28},{18,... | collective-permute-start | bytes 1179656 | tf_op jit(solution)/shard_map/ppermute | solution.py:255
  41.3 14.6 %collective-permute-start.3 = (bf16[8,2,16,768]{3,2,1,0:T(8,128)(2,1)S(1)}, bf16[8,2,16,768]{3,2,1,0:T(8,128)(2,1)S(1)}, u32[]{:S(2)}, u32[]{:S(2)}) collective-permute-start(bf16[8,2,16,768]{3,2,1,0:T(8,128)(2,1)S(1)} %bitcast.20), channel_id=1, source_target_pairs={{0,4},{2,6},{4,8},{6,10},{8,12},{10,14},{12,0},{14,2},{16,20},{18,... | collective-permute-start | bytes 1179656 | tf_op jit(solution)/shard_map/ppermute | solution.py:255
  43.2 18.6 %collective-permute-start.2 = (bf16[8,2,16,768]{3,2,1,0:T(8,128)(2,1)S(1)}, bf16[8,2,16,768]{3,2,1,0:T(8,128)(2,1)S(1)}, u32[]{:S(2)}, u32[]{:S(2)}) collective-permute-start(bf16[8,2,16,768]{3,2,1,0:T(8,128)(2,1)S(1)} %bitcast.21), channel_id=1, source_target_pairs={{0,14},{2,0},{4,2},{6,4},{8,6},{10,8},{12,10},{14,12},{16,30},{18,... | collective-permute-start | bytes 1179656 | tf_op jit(solution)/shard_map/ppermute | solution.py:255
  48.0 17.0 %collective-permute-start.1 = (bf16[8,2,16,768]{3,2,1,0:T(8,128)(2,1)S(1)}, bf16[8,2,16,768]{3,2,1,0:T(8,128)(2,1)S(1)}, u32[]{:S(2)}, u32[]{:S(2)}) collective-permute-start(bf16[8,2,16,768]{3,2,1,0:T(8,128)(2,1)S(1)} %bitcast.22), channel_id=1, source_target_pairs={{0,2},{2,4},{4,6},{6,8},{8,10},{10,12},{12,14},{14,0},{16,18},{18,... | collective-permute-start | bytes 1179656 | tf_op jit(solution)/shard_map/ppermute | solution.py:255
  50.2 20.5 %collective-permute-start.6 = (bf16[8,2,16,768]{3,2,1,0:T(8,128)(2,1)S(1)}, bf16[8,2,16,768]{3,2,1,0:T(8,128)(2,1)S(1)}, u32[]{:S(2)}, u32[]{:S(2)}) collective-permute-start(bf16[8,2,16,768]{3,2,1,0:T(8,128)(2,1)S(1)} %collective-permute-done.4), channel_id=1, source_target_pairs={{0,14},{2,0},{4,2},{6,4},{8,6},{10,8},{12,10},{14,12},{16,30},{18,... | collective-permute-start | bytes 1179656 | tf_op jit(solution)/shard_map/ppermute | solution.py:255
  55.9 14.8 %collective-permute-start.5 = (bf16[8,2,16,768]{3,2,1,0:T(8,128)(2,1)S(1)}, bf16[8,2,16,768]{3,2,1,0:T(8,128)(2,1)S(1)}, u32[]{:S(2)}, u32[]{:S(2)}) collective-permute-start(bf16[8,2,16,768]{3,2,1,0:T(8,128)(2,1)S(1)} %collective-permute-done.3), channel_id=1, source_target_pairs={{0,2},{2,4},{4,6},{6,8},{8,10},{10,12},{12,14},{14,0},{16,18},{18,... | collective-permute-start | bytes 1179656 | tf_op jit(solution)/shard_map/ppermute | solution.py:255
  58.8 11.9 %collective-permute-start.8 = (bf16[4,2,16,768]{3,2,1,0:T(8,128)(2,1)S(1)}, bf16[4,2,16,768]{3,2,1,0:T(8,128)(2,1)S(1)}, u32[]{:S(2)}, u32[]{:S(2)}) collective-permute-start(bf16[4,2,16,768]{3,2,1,0:T(8,128)(2,1)S(1)} %slice.9), channel_id=1, source_target_pairs={{0,12},{2,14},{4,0},{6,2},{8,4},{10,6},{12,8},{14,10},{16,28},{18,... | collective-permute-start | bytes 589832 | tf_op jit(solution)/shard_map/ppermute | solution.py:255
  61.7 8.9 %collective-permute-start.7 = (bf16[4,2,16,768]{3,2,1,0:T(8,128)(2,1)S(1)}, bf16[4,2,16,768]{3,2,1,0:T(8,128)(2,1)S(1)}, u32[]{:S(2)}, u32[]{:S(2)}) collective-permute-start(bf16[4,2,16,768]{3,2,1,0:T(8,128)(2,1)S(1)} %slice.8), channel_id=1, source_target_pairs={{0,4},{2,6},{4,8},{6,10},{8,12},{10,14},{12,0},{14,2},{16,20},{18,... | collective-permute-start | bytes 589832 | tf_op jit(solution)/shard_map/ppermute | solution.py:255
  65.2 14.4 %collective-permute-start.10 = (bf16[4,8,2,16,768]{4,3,2,1,0:T(8,128)(2,1)S(1)}, bf16[4,8,2,16,768]{4,3,2,1,0:T(8,128)(2,1)S(1)}, u32[]{:S(2)}, u32[]{:S(2)}) collective-permute-start(bf16[4,8,2,16,768]{4,3,2,1,0:T(8,128)(2,1)S(1)} %pad_maximum_fusion.own_0), channel_id=1, source_target_pairs={{0,1},{1,0},{2,3},{3,2},{4,5},{5,4},{6,7},{7,6},{8,9},{9,8},{10,11... | collective-permute-start | bytes 4718600 | tf_op jit(solution)/shard_map/ppermute | solution.py:260
  70.9 11.7 %collective-permute-start.9 = (bf16[4,8,2,16,768]{4,3,2,1,0:T(8,128)(2,1)S(1)}, bf16[4,8,2,16,768]{4,3,2,1,0:T(8,128)(2,1)S(1)}, u32[]{:S(2)}, u32[]{:S(2)}) collective-permute-start(bf16[4,8,2,16,768]{4,3,2,1,0:T(8,128)(2,1)S(1)} %pad_maximum_fusion.1.own_1), channel_id=1, source_target_pairs={{0,1},{1,0},{2,3},{3,2},{4,5},{5,4},{6,7},{7,6},{8,9},{9,8},{10,11... | collective-permute-start | bytes 4718600 | tf_op jit(solution)/shard_map/ppermute | solution.py:260

commit v7 on v6

--- a/solution.py
+++ b/solution.py
@@ -15,6 +15,7 @@
 HALF = 384
 ROWS = 48
 ORDER = (0, 1, 7, 2, 6, 3, 5, 4)
+PARTS = ((0, 5), (5, 8))
 STEPS = 14
 VMEM = pl.BlockSpec(memory_space=pltpu.VMEM)
 SMALL = pltpu.CompilerParams(vmem_limit_bytes=8 * 2**20)
@@ -66,20 +67,17 @@
     return jnp.sum(jnp.where(here, jnp.broadcast_to(row, square), 0.0), axis=1, keepdims=True)
 
 
-def mask_kernel(coef_ref, known_ref, send_ref, keep_ref):
+def mask_kernel(coef_ref, limits_ref, weight_ref, send_ref, keep_ref):
     rows, width = coef_ref.shape
     tiles = width // N // AUX_PAD
     core = lax.axis_index("c")
     device = ((lax.axis_index("y") * N + lax.axis_index("x")) * N + lax.axis_index("z")) * 2 + core
     block = device * rows // PAIR_ROWS
     lane = lax.broadcasted_iota(jnp.int32, (rows, AUX_PAD), 1)
-    atoms = width // AUX_PAD
-    pattern = known_ref[0:atoms, :]
-    at_block = lax.broadcasted_iota(jnp.int32, pattern.shape, 1) == block
-    meets = jnp.sum(jnp.where(at_block, pattern, 0.0), axis=1, keepdims=True)
-    sizes = jnp.where(meets > 0, as_column(known_ref[atoms : atoms + 1, 0:atoms]), 0.0)
-    sizes = jnp.broadcast_to(sizes, (atoms, AUX_PAD)).astype(jnp.int32)
-    weight = jnp.broadcast_to(as_column(known_ref[atoms + 1 : atoms + 2, 0:rows]), (rows, AUX_PAD))
+    at_block = lax.broadcasted_iota(jnp.int32, limits_ref.shape, 1) == block
+    limits = jnp.sum(jnp.where(at_block, limits_ref[...], 0), axis=1, keepdims=True)
+    limits = jnp.broadcast_to(limits, limits_ref.shape)
+    weight = jnp.broadcast_to(as_column(weight_ref[...]), (rows, AUX_PAD))
 
     def store(ref, to, found):
         for t in range(tiles):
@@ -90,7 +88,7 @@
             masked = []
             for atom in range(to * tiles, (to + 1) * tiles):
                 coef = coef_ref[:, atom * AUX_PAD : (atom + 1) * AUX_PAD].astype(jnp.float32)
-                masked.append(jnp.where(lane < sizes[atom : atom + 1, :], coef, 0.0))
+                masked.append(jnp.where(lane < limits[atom : atom + 1, :], coef, 0.0))
             store(left_ref, to, into_order(masked))
             store(right_ref, to, [weight * m for m in masked])
 
@@ -105,33 +103,33 @@
 
 def operands(coefficients, row_weight, pattern, aux_sizes):
     rows, width = coefficients.shape
-    as_row = lambda v: jnp.pad(v.astype(jnp.float32).reshape(1, -1), ((0, 0), (0, pattern.shape[0] - v.shape[0])))
-    known = jnp.concatenate([pattern.T.astype(jnp.float32), as_row(aux_sizes), as_row(row_weight)])
+    limits = pattern.T * aux_sizes[:, None]
     return pl.pallas_call(
         mask_kernel,
         out_shape=[jax.ShapeDtypeStruct((N, height, width // N), jnp.bfloat16) for height in (rows, 2 * rows)],
-        in_specs=[VMEM, VMEM],
-        out_specs=[VMEM, VMEM],
+        in_specs=[VMEM] * 3,
+        out_specs=[VMEM] * 2,
         compiler_params=SMALL,
         cost_estimate=pl.CostEstimate(flops=8 * rows * width, bytes_accessed=6 * rows * width, transcendentals=0),
-    )(coefficients, known)
+    )(coefficients, limits, row_weight.reshape(1, -1))
 
 
 def contract_part(own_refs, other_ref, gathered, part, write):
-    slots, places, two, rows, wide = own_refs[0].shape
+    places, two, rows, wide = own_refs[0].shape[1:]
     core = lax.axis_index("c")
     mine = jnp.where(core == 0, lax.axis_index("z"), lax.axis_index("y"))
     theirs = jnp.where(core == 0, lax.axis_index("y"), lax.axis_index("z"))
     tile = 256
 
     def gather(columns):
-        for k in range(slots):
-            inner = lax.rem(theirs + N - ORDER[part * slots + k], N)
-            for slot in range(len(ORDER)):
-                place = lax.rem(mine + N - ORDER[slot], N)
-                for h in range(two):
-                    at = pl.multiple_of(((k * places + place) * two + h) * rows, rows)
-                    gathered[pl.ds(at, rows), columns] = own_refs[slot // slots][slot % slots, inner, 1 - h, :, columns]
+        for k, distance in enumerate(ORDER[slice(*PARTS[part])]):
+            inner = lax.rem(theirs + N - distance, N)
+            for own_ref, (first, last) in zip(own_refs, PARTS):
+                for slot in range(first, last):
+                    place = lax.rem(mine + N - ORDER[slot], N)
+                    for h in range(two):
+                        at = pl.multiple_of(((k * places + place) * two + h) * rows, rows)
+                        gathered[pl.ds(at, rows), columns] = own_ref[slot - first, inner, 1 - h, :, columns]
 
     def run(left_ref, right_ref, columns):
         def column_tile(t, carry):
@@ -256,7 +254,7 @@
     slot = {0: blocks, 2: move(blocks, 2), 6: move(blocks, -2), 1: move(blocks, 1), 7: move(blocks, -1)}
     slot[3], slot[5] = move(slot[2], 1), move(slot[6], -1)
     slot[4] = jnp.concatenate([move(slot[2][: N // 2], 2), move(slot[6][N // 2 :], -2)])
-    own = [jnp.stack([slot[d] for d in ORDER[p * N // 2 : (p + 1) * N // 2]]) for p in range(2)]
+    own = [jnp.stack([slot[d] for d in ORDER[slice(*part)]]) for part in PARTS]
     other = [lax.ppermute(part, "c", swap).reshape(-1, wide) for part in own]
     messages = contract(own, other[1], contract(own, other[0], None))
     parts = lax.all_to_all(messages, "x", 0, 0, tiled=True)

time: 111 us -> 118 us (1.063)
  waiting for transfers between devices: 4.26 us -> 16.3 us
  starting transfers between devices: 58.8 us -> 54.6 us
  other arithmetic: 2.5 us -> 0.98 us
    ppermute x8, waiting for transfers between devices: 1.6 us -> 14.4 us  [per_device(): move = lambda value, d: lax.ppermute(value, AXES, along('z', 'y', d))]
    ppermute x2, starting transfers between devices: 14.1 us -> 9.43 us  [per_device(): other = [lax.ppermute(part, 'c', swap).reshape(-1, wide) for part in own]]
  transfers between devices with their start and end apart: 11 -> 11, of which waited for: 4 -> 6; matrix products, arithmetic and copies ran while one was open for 0% -> 0% of each run, Pallas kernels for 1% -> 1%
where the time goes in v7:
time: 118 us
  starting transfers between devices  54.6 us (46%)
  blocking collectives  39.3 us (33%)
  waiting for transfers between devices  16.3 us (14%)
  Pallas kernels  4.34 us (4%)
  local copies, waits for them, and re-layouts  1.76 us (1%)
    ppermute x8, starting transfers between devices, per_device(): move = lambda value, d: lax.ppermute(value, AXES, along('z', 'y', d))  29.1 us
    all_to_all x1, blocking collectives, per_device(): parts = lax.all_to_all(messages, 'x', 0, 0, tiled=True)  25 us
    ppermute x1, starting transfers between devices, per_device(): lax.ppermute(send, 'c', swap)  16.1 us
    ppermute x8, waiting for transfers between devices, per_device(): move = lambda value, d: lax.ppermute(value, AXES, along('z', 'y', d))  14.4 us
    all_to_all x1, blocking collectives, exchange(): lax.all_to_all(blocks, AXES, 0, 0, tiled=True, axis_index_groups=groups(f...  14.3 us
    ppermute x2, starting transfers between devices, per_device(): other = [lax.ppermute(part, 'c', swap).reshape(-1, wide) for part in own]  9.43 us
  transfers between devices with their start and end apart: 11, of which 6 were waited for; matrix products, arithmetic and copies ran while one was open for 0% of the time, Pallas kernels for 1%

profile of v7, /device:TPU:1, one launch (start us, length us, event | category | flops | bytes accessed | tf_op | source)
XLA Modules:
  0.0 117.5 jit_solution(12322549780372189751)
XLA Ops:
  0.0 0.8 multiply_bitcast_fusion.limits_ref
  0.8 0.0 copy-start
  0.8 0.9 copy-done
  1.7 0.0 copy-start.1
  1.7 0.7 copy-done.1
  2.4 0.3 shard_map.46
  2.7 16.1 %collective-permute-start = (bf16[8,16,768]{2,1,0:T(8,128)(2,1)S(1)}, bf16[8,16,768]{2,1,0:T(8,128)(2,1)S(1)}, u32[]{:S(2)}, u32[]{:S(2)}) collective-permute-start(bf16[8,16,768]{2,1,0:T(8,128)(2,1)S(1)} %get-tuple-element.8), channel_id=1, source_target_pairs={{0,1},{1,0},{2,3},{3,2},{4,5},{5,4},{6,7},{7,6},{8,9},{9,8},{10,11... | collective-permute-start | bytes 589832 | tf_op jit(solution)/shard_map/ppermute | solution.py:250
  18.7 1.0 collective-permute-done
  19.8 14.3 %all_to_all.10 = bf16[8,32,768]{2,1,0:T(8,128)(2,1)S(1)} all-to-all(bf16[8,32,768]{2,1,0:T(8,128)(2,1)S(1)} %constant_dynamic-update-slice_fusion.1), channel_id=1, replica_groups={{0,128,256,384,512,640,768,896},{2,130,258,386,514,642,770,898},{4,132,..., dimensions={0} | all-to-all | bytes 786432 | tf_op jit(solution)/shard_map/all_to_all | solution.py:39
  34.1 3.3 %collective-permute-start.1 = (bf16[8,2,16,768]{3,2,1,0:T(8,128)(2,1)S(1)}, bf16[8,2,16,768]{3,2,1,0:T(8,128)(2,1)S(1)}, u32[]{:S(2)}, u32[]{:S(2)}) collective-permute-start(bf16[8,2,16,768]{3,2,1,0:T(8,128)(2,1)S(1)} %bitcast.22), channel_id=1, source_target_pairs={{0,2},{2,4},{4,6},{6,8},{8,10},{10,12},{12,14},{14,0},{16,18},{18,... | collective-permute-start | bytes 1179656 | tf_op jit(solution)/shard_map/ppermute | solution.py:253
  37.4 4.5 %collective-permute-start.2 = (bf16[8,2,16,768]{3,2,1,0:T(8,128)(2,1)S(1)}, bf16[8,2,16,768]{3,2,1,0:T(8,128)(2,1)S(1)}, u32[]{:S(2)}, u32[]{:S(2)}) collective-permute-start(bf16[8,2,16,768]{3,2,1,0:T(8,128)(2,1)S(1)} %bitcast.23), channel_id=1, source_target_pairs={{0,14},{2,0},{4,2},{6,4},{8,6},{10,8},{12,10},{14,12},{16,30},{18,... | collective-permute-start | bytes 1179656 | tf_op jit(solution)/shard_map/ppermute | solution.py:253
  41.9 1.9 %collective-permute-start.3 = (bf16[8,2,16,768]{3,2,1,0:T(8,128)(2,1)S(1)}, bf16[8,2,16,768]{3,2,1,0:T(8,128)(2,1)S(1)}, u32[]{:S(2)}, u32[]{:S(2)}) collective-permute-start(bf16[8,2,16,768]{3,2,1,0:T(8,128)(2,1)S(1)} %bitcast.24), channel_id=1, source_target_pairs={{0,4},{2,6},{4,8},{6,10},{8,12},{10,14},{12,0},{14,2},{16,20},{18,... | collective-permute-start | bytes 1179656 | tf_op jit(solution)/shard_map/ppermute | solution.py:253
  43.8 5.5 %collective-permute-start.4 = (bf16[8,2,16,768]{3,2,1,0:T(8,128)(2,1)S(1)}, bf16[8,2,16,768]{3,2,1,0:T(8,128)(2,1)S(1)}, u32[]{:S(2)}, u32[]{:S(2)}) collective-permute-start(bf16[8,2,16,768]{3,2,1,0:T(8,128)(2,1)S(1)} %bitcast.25), channel_id=1, source_target_pairs={{0,12},{2,14},{4,0},{6,2},{8,4},{10,6},{12,8},{14,10},{16,28},{18,... | collective-permute-start | bytes 1179656 | tf_op jit(solution)/shard_map/ppermute | solution.py:253
  49.4 0.0 collective-permute-done.1
  49.4 0.0 collective-permute-done.2
  49.5 7.6 %collective-permute-done.3 = bf16[8,2,16,768]{3,2,1,0:T(8,128)(2,1)S(1)} collective-permute-done((bf16[8,2,16,768]{3,2,1,0:T(8,128)(2,1)S(1)}, bf16[8,2,16,768]{3,2,1,0:T(8,128)(2,1)S(1)}, u32[]{:S(2)}, u32[]{:S(2)}) %collective-permute-start.3) | collective-permute-done | bytes 393248 | tf_op jit(solution)/shard_map/ppermute | solution.py:253
  57.1 3.0 %collective-permute-done.4 = bf16[8,2,16,768]{3,2,1,0:T(8,128)(2,1)S(1)} collective-permute-done((bf16[8,2,16,768]{3,2,1,0:T(8,128)(2,1)S(1)}, bf16[8,2,16,768]{3,2,1,0:T(8,128)(2,1)S(1)}, u32[]{:S(2)}, u32[]{:S(2)}) %collective-permute-start.4) | collective-permute-done | bytes 393248 | tf_op jit(solution)/shard_map/ppermute | solution.py:253
  60.1 3.8 %collective-permute-start.10 = (bf16[5,8,2,16,768]{4,3,2,1,0:T(8,128)(2,1)S(1)}, bf16[5,8,2,16,768]{4,3,2,1,0:T(8,128)(2,1)S(1)}, u32[]{:S(2)}, u32[]{:S(2)}) collective-permute-start(bf16[5,8,2,16,768]{4,3,2,1,0:T(8,128)(2,1)S(1)} %bitcast_dynamic-update-slice_fusion.own_0), channel_id=1, source_target_pairs={{0,1},{1,0},{2,3},{3,2},{4,5},{5,4},{6,7},{7,6},{8,9},{9,8},{10,11... | collective-permute-start | bytes 5898248 | tf_op jit(solution)/shard_map/ppermute | solution.py:258
  63.9 2.3 %collective-permute-start.5 = (bf16[8,2,16,768]{3,2,1,0:T(8,128)(2,1)S(1)}, bf16[8,2,16,768]{3,2,1,0:T(8,128)(2,1)S(1)}, u32[]{:S(2)}, u32[]{:S(2)}) collective-permute-start(bf16[8,2,16,768]{3,2,1,0:T(8,128)(2,1)S(1)} %collective-permute-done.3), channel_id=1, source_target_pairs={{0,2},{2,4},{4,6},{6,8},{8,10},{10,12},{12,14},{14,0},{16,18},{18,... | collective-permute-start | bytes 1179656 | tf_op jit(solution)/shard_map/ppermute | solution.py:253
  66.2 4.2 %collective-permute-start.6 = (bf16[8,2,16,768]{3,2,1,0:T(8,128)(2,1)S(1)}, bf16[8,2,16,768]{3,2,1,0:T(8,128)(2,1)S(1)}, u32[]{:S(2)}, u32[]{:S(2)}) collective-permute-start(bf16[8,2,16,768]{3,2,1,0:T(8,128)(2,1)S(1)} %collective-permute-done.4), channel_id=1, source_target_pairs={{0,14},{2,0},{4,2},{6,4},{8,6},{10,8},{12,10},{14,12},{16,30},{18,... | collective-permute-start | bytes 1179656 | tf_op jit(solution)/shard_map/ppermute | solution.py:253
  70.5 1.9 %collective-permute-start.7 = (bf16[4,2,16,768]{3,2,1,0:T(8,128)(2,1)S(1)}, bf16[4,2,16,768]{3,2,1,0:T(8,128)(2,1)S(1)}, u32[]{:S(2)}, u32[]{:S(2)}) collective-permute-start(bf16[4,2,16,768]{3,2,1,0:T(8,128)(2,1)S(1)} %slice.8), channel_id=1, source_target_pairs={{0,4},{2,6},{4,8},{6,10},{8,12},{10,14},{12,0},{14,2},{16,20},{18,... | collective-permute-start | bytes 589832 | tf_op jit(solution)/shard_map/ppermute | solution.py:253
  72.4 5.5 %collective-permute-start.8 = (bf16[4,2,16,768]{3,2,1,0:T(8,128)(2,1)S(1)}, bf16[4,2,16,768]{3,2,1,0:T(8,128)(2,1)S(1)}, u32[]{:S(2)}, u32[]{:S(2)}) collective-permute-start(bf16[4,2,16,768]{3,2,1,0:T(8,128)(2,1)S(1)} %slice.9), channel_id=1, source_target_pairs={{0,12},{2,14},{4,0},{6,2},{8,4},{10,6},{12,8},{14,10},{16,28},{18,... | collective-permute-start | bytes 589832 | tf_op jit(solution)/shard_map/ppermute | solution.py:253
  77.9 2.5 %collective-permute-done.7 = bf16[4,2,16,768]{3,2,1,0:T(8,128)(2,1)S(1)} collective-permute-done((bf16[4,2,16,768]{3,2,1,0:T(8,128)(2,1)S(1)}, bf16[4,2,16,768]{3,2,1,0:T(8,128)(2,1)S(1)}, u32[]{:S(2)}, u32[]{:S(2)}) %collective-permute-start.7) | collective-permute-done | bytes 196640 | tf_op jit(solution)/shard_map/ppermute | solution.py:253
  80.4 1.3 %collective-permute-done.8 = bf16[4,2,16,768]{3,2,1,0:T(8,128)(2,1)S(1)} collective-permute-done((bf16[4,2,16,768]{3,2,1,0:T(8,128)(2,1)S(1)}, bf16[4,2,16,768]{3,2,1,0:T(8,128)(2,1)S(1)}, u32[]{:S(2)}, u32[]{:S(2)}) %collective-permute-start.8) | collective-permute-done | bytes 196640 | tf_op jit(solution)/shard_map/ppermute | solution.py:253
  81.7 0.0 collective-permute-done.5
  81.7 0.0 collective-permute-done.6
  81.8 0.1 pad_maximum_fusion.own_1
  81.9 5.6 %collective-permute-start.9 = (bf16[3,8,2,16,768]{4,3,2,1,0:T(8,128)(2,1)S(1)}, bf16[3,8,2,16,768]{4,3,2,1,0:T(8,128)(2,1)S(1)}, u32[]{:S(2)}, u32[]{:S(2)}) collective-permute-start(bf16[3,8,2,16,768]{4,3,2,1,0:T(8,128)(2,1)S(1)} %pad_maximum_fusion.own_1), channel_id=1, source_target_pairs={{0,1},{1,0},{2,3},{3,2},{4,5},{5,4},{6,7},{7,6},{8,9},{9,8},{10,11... | collective-permute-start | bytes 3538952 | tf_op jit(solution)/shard_map/ppermute | solution.py:258
  87.5 0.0 collective-permute-done.10
  87.5 1.6 %shard_map.47.first_ref = f32[384,768]{1,0:T(8,128)S(1)} custom-call(bf16[5,8,2,16,768]{4,3,2,1,0:T(8,128)(2,1)S(1)} %bitcast_dynamic-update-slice_fusion.own_0, bf16[3,8,2,16,768]{4,3,2,1,0:T(8,128)(2,1)S(1)} %pad_maximum_fusion.own_1, bf16[1280,768]{1,0:T(8,128)(2,1)S(1)} %bitcast.19), custom_call_target="tpu_custom_call" | custom-call | flops 754974720 | bytes 7864320 | tf_op jit(solution)/shard_map/pallas_call | solution.py:218
  89.1 0.9 collective-permute-done.9
  90.0 1.7 %shard_map.48 = s16[8,304,128]{2,1,0:T(8,128)(2,1)S(1)} custom-call(bf16[5,8,2,16,768]{4,3,2,1,0:T(8,128)(2,1)S(1)} %bitcast_dynamic-update-slice_fusion.own_0, bf16[3,8,2,16,768]{4,3,2,1,0:T(8,128)(2,1)S(1)} %pad_maximum_fusion.own_1, bf16[768,768]{1,0:T(8,128)(2,1)S(1)} %bitcast.20, f32[384,768]{1,0:T(8,128)S(1)} %shard_map.47.first_ref), custom_call_target="tpu_custom_call" | custom-call | flops 452984832 | bytes 4718592 | tf_op jit(solution)/shard_map/pallas_call | solution.py:228
  91.7 25.0 %all_to_all.11.parts_ref = s16[8,304,128]{2,1,0:T(8,128)(2,1)S(1)} all-to-all(s16[8,304,128]{2,1,0:T(8,128)(2,1)S(1)} %shard_map.48), channel_id=1, replica_groups=mesh['y'=8,'x'=8,'z'=8,'c'=2] {'x'}, dimensions={0} | all-to-all | bytes 1245184 | tf_op jit(solution)/shard_map/all_to_all | solution.py:260
  116.7 0.8 shard_map.49
  (9 shorter events, 0.2 us)
Async XLA Ops:
  0.8 0.9 copy-start
  1.7 0.7 copy-start.1
  2.7 17.1 %collective-permute-start = (bf16[8,16,768]{2,1,0:T(8,128)(2,1)S(1)}, bf16[8,16,768]{2,1,0:T(8,128)(2,1)S(1)}, u32[]{:S(2)}, u32[]{:S(2)}) collective-permute-start(bf16[8,16,768]{2,1,0:T(8,128)(2,1)S(1)} %get-tuple-element.8), channel_id=1, source_target_pairs={{0,1},{1,0},{2,3},{3,2},{4,5},{5,4},{6,7},{7,6},{8,9},{9,8},{10,11... | collective-permute-start | bytes 589832 | tf_op jit(solution)/shard_map/ppermute | solution.py:250
  34.1 15.3 %collective-permute-start.1 = (bf16[8,2,16,768]{3,2,1,0:T(8,128)(2,1)S(1)}, bf16[8,2,16,768]{3,2,1,0:T(8,128)(2,1)S(1)}, u32[]{:S(2)}, u32[]{:S(2)}) collective-permute-start(bf16[8,2,16,768]{3,2,1,0:T(8,128)(2,1)S(1)} %bitcast.22), channel_id=1, source_target_pairs={{0,2},{2,4},{4,6},{6,8},{8,10},{10,12},{12,14},{14,0},{16,18},{18,... | collective-permute-start | bytes 1179656 | tf_op jit(solution)/shard_map/ppermute | solution.py:253
  37.4 12.0 %collective-permute-start.2 = (bf16[8,2,16,768]{3,2,1,0:T(8,128)(2,1)S(1)}, bf16[8,2,16,768]{3,2,1,0:T(8,128)(2,1)S(1)}, u32[]{:S(2)}, u32[]{:S(2)}) collective-permute-start(bf16[8,2,16,768]{3,2,1,0:T(8,128)(2,1)S(1)} %bitcast.23), channel_id=1, source_target_pairs={{0,14},{2,0},{4,2},{6,4},{8,6},{10,8},{12,10},{14,12},{16,30},{18,... | collective-permute-start | bytes 1179656 | tf_op jit(solution)/shard_map/ppermute | solution.py:253
  41.9 15.1 %collective-permute-start.3 = (bf16[8,2,16,768]{3,2,1,0:T(8,128)(2,1)S(1)}, bf16[8,2,16,768]{3,2,1,0:T(8,128)(2,1)S(1)}, u32[]{:S(2)}, u32[]{:S(2)}) collective-permute-start(bf16[8,2,16,768]{3,2,1,0:T(8,128)(2,1)S(1)} %bitcast.24), channel_id=1, source_target_pairs={{0,4},{2,6},{4,8},{6,10},{8,12},{10,14},{12,0},{14,2},{16,20},{18,... | collective-permute-start | bytes 1179656 | tf_op jit(solution)/shard_map/ppermute | solution.py:253
  43.8 16.2 %collective-permute-start.4 = (bf16[8,2,16,768]{3,2,1,0:T(8,128)(2,1)S(1)}, bf16[8,2,16,768]{3,2,1,0:T(8,128)(2,1)S(1)}, u32[]{:S(2)}, u32[]{:S(2)}) collective-permute-start(bf16[8,2,16,768]{3,2,1,0:T(8,128)(2,1)S(1)} %bitcast.25), channel_id=1, source_target_pairs={{0,12},{2,14},{4,0},{6,2},{8,4},{10,6},{12,8},{14,10},{16,28},{18,... | collective-permute-start | bytes 1179656 | tf_op jit(solution)/shard_map/ppermute | solution.py:253
  60.1 27.4 %collective-permute-start.10 = (bf16[5,8,2,16,768]{4,3,2,1,0:T(8,128)(2,1)S(1)}, bf16[5,8,2,16,768]{4,3,2,1,0:T(8,128)(2,1)S(1)}, u32[]{:S(2)}, u32[]{:S(2)}) collective-permute-start(bf16[5,8,2,16,768]{4,3,2,1,0:T(8,128)(2,1)S(1)} %bitcast_dynamic-update-slice_fusion.own_0), channel_id=1, source_target_pairs={{0,1},{1,0},{2,3},{3,2},{4,5},{5,4},{6,7},{7,6},{8,9},{9,8},{10,11... | collective-permute-start | bytes 5898248 | tf_op jit(solution)/shard_map/ppermute | solution.py:258
  63.9 17.8 %collective-permute-start.5 = (bf16[8,2,16,768]{3,2,1,0:T(8,128)(2,1)S(1)}, bf16[8,2,16,768]{3,2,1,0:T(8,128)(2,1)S(1)}, u32[]{:S(2)}, u32[]{:S(2)}) collective-permute-start(bf16[8,2,16,768]{3,2,1,0:T(8,128)(2,1)S(1)} %collective-permute-done.3), channel_id=1, source_target_pairs={{0,2},{2,4},{4,6},{6,8},{8,10},{10,12},{12,14},{14,0},{16,18},{18,... | collective-permute-start | bytes 1179656 | tf_op jit(solution)/shard_map/ppermute | solution.py:253
  66.2 15.5 %collective-permute-start.6 = (bf16[8,2,16,768]{3,2,1,0:T(8,128)(2,1)S(1)}, bf16[8,2,16,768]{3,2,1,0:T(8,128)(2,1)S(1)}, u32[]{:S(2)}, u32[]{:S(2)}) collective-permute-start(bf16[8,2,16,768]{3,2,1,0:T(8,128)(2,1)S(1)} %collective-permute-done.4), channel_id=1, source_target_pairs={{0,14},{2,0},{4,2},{6,4},{8,6},{10,8},{12,10},{14,12},{16,30},{18,... | collective-permute-start | bytes 1179656 | tf_op jit(solution)/shard_map/ppermute | solution.py:253
  70.5 9.9 %collective-permute-start.7 = (bf16[4,2,16,768]{3,2,1,0:T(8,128)(2,1)S(1)}, bf16[4,2,16,768]{3,2,1,0:T(8,128)(2,1)S(1)}, u32[]{:S(2)}, u32[]{:S(2)}) collective-permute-start(bf16[4,2,16,768]{3,2,1,0:T(8,128)(2,1)S(1)} %slice.8), channel_id=1, source_target_pairs={{0,4},{2,6},{4,8},{6,10},{8,12},{10,14},{12,0},{14,2},{16,20},{18,... | collective-permute-start | bytes 589832 | tf_op jit(solution)/shard_map/ppermute | solution.py:253
  72.4 9.3 %collective-permute-start.8 = (bf16[4,2,16,768]{3,2,1,0:T(8,128)(2,1)S(1)}, bf16[4,2,16,768]{3,2,1,0:T(8,128)(2,1)S(1)}, u32[]{:S(2)}, u32[]{:S(2)}) collective-permute-start(bf16[4,2,16,768]{3,2,1,0:T(8,128)(2,1)S(1)} %slice.9), channel_id=1, source_target_pairs={{0,12},{2,14},{4,0},{6,2},{8,4},{10,6},{12,8},{14,10},{16,28},{18,... | collective-permute-start | bytes 589832 | tf_op jit(solution)/shard_map/ppermute | solution.py:253
  81.9 8.1 %collective-permute-start.9 = (bf16[3,8,2,16,768]{4,3,2,1,0:T(8,128)(2,1)S(1)}, bf16[3,8,2,16,768]{4,3,2,1,0:T(8,128)(2,1)S(1)}, u32[]{:S(2)}, u32[]{:S(2)}) collective-permute-start(bf16[3,8,2,16,768]{4,3,2,1,0:T(8,128)(2,1)S(1)} %pad_maximum_fusion.own_1), channel_id=1, source_target_pairs={{0,1},{1,0},{2,3},{3,2},{4,5},{5,4},{6,7},{7,6},{8,9},{9,8},{10,11... | collective-permute-start | bytes 3538952 | tf_op jit(solution)/shard_map/ppermute | solution.py:258

commit v8 on v7

--- a/solution.py
+++ b/solution.py
@@ -14,8 +14,8 @@
 AXES = ("y", "x", "z", "c")
 HALF = 384
 ROWS = 48
-ORDER = (0, 1, 7, 2, 6, 3, 5, 4)
-PARTS = ((0, 5), (5, 8))
+ORDER = (0, 2, 6, 1, 7, 3, 5, 4)
+PARTS = ((0, 4), (4, 8))
 STEPS = 14
 VMEM = pl.BlockSpec(memory_space=pltpu.VMEM)
 SMALL = pltpu.CompilerParams(vmem_limit_bytes=8 * 2**20)
@@ -131,14 +131,16 @@
                         at = pl.multiple_of(((k * places + place) * two + h) * rows, rows)
                         gathered[pl.ds(at, rows), columns] = own_ref[slot - first, inner, 1 - h, :, columns]
 
+    depth = other_ref.shape[0]
+
     def run(left_ref, right_ref, columns):
         def column_tile(t, carry):
             start = pl.multiple_of(t * tile, tile)
             write(
                 start,
                 lax.dot_general(
-                    left_ref[:, columns],
-                    right_ref[:, pl.ds(start, tile)],
+                    left_ref[0:depth, columns],
+                    right_ref[0:depth, pl.ds(start, tile)],
                     (((0,), (0,)), ((), ())),
                     preferred_element_type=jnp.float32,
                 ),
@@ -158,19 +160,25 @@
         run(other_ref, gathered, slice(HALF, 2 * HALF))
 
 
-def first_part_kernel(own_0, own_1, other_ref, out_ref, gathered):
-    def write(start, value):
-        out_ref[:, pl.ds(start, value.shape[1])] = value
-
-    contract_part((own_0, own_1), other_ref, gathered, 0, write)
-
-
-def second_part_kernel(own_0, own_1, other_ref, first_ref, out_ref, gathered, total):
-    def write(start, value):
-        columns = pl.ds(start, value.shape[1])
-        total[:, columns] = first_ref[:, columns] + value
-
-    contract_part((own_0, own_1), other_ref, gathered, 1, write)
+def contract_parts(parts, own_refs, other_refs, sum_ref, out_ref, gathered):
+    for part, other_ref in zip(parts, other_refs):
+
+        def write(start, value, before=sum_ref):
+            columns = pl.ds(start, value.shape[1])
+            out_ref[:, columns] = value if before is None else before[:, columns] + value
+
+        contract_part(own_refs, other_ref, gathered, part, write)
+        sum_ref = out_ref
+
+
+def first_parts_kernel(parts, *refs):
+    own, other, (out_ref, gathered) = refs[: len(PARTS)], refs[len(PARTS) : -2], refs[-2:]
+    contract_parts(parts, own, other, None, out_ref, gathered)
+
+
+def last_part_kernel(parts, *refs):
+    own, other, (first_ref, out_ref, gathered, total) = refs[: len(PARTS)], refs[len(PARTS) : -4], refs[-4:]
+    contract_parts(parts, own, other, first_ref, total, gathered)
 
     lanes = out_ref.shape[2]
     tiles = total.shape[1] // lanes
@@ -208,32 +216,36 @@
         out_ref[:, t * lanes : (t + 1) * lanes] = total
 
 
-def contract(own, other, first):
-    depth, wide = other.shape
-    gathered = pltpu.VMEM((depth, wide), jnp.bfloat16)
-    total = pltpu.VMEM((HALF, wide), jnp.float32)
-    cost = pl.CostEstimate(flops=2 * depth * wide * HALF, bytes_accessed=8 * depth * wide, transcendentals=0)
+def contract(own, other):
+    wide = own[0].shape[-1]
+    *early, last = range(len(PARTS))
+    depths = [o.shape[0] for o in other]
+    gathered = lambda parts: pltpu.VMEM((max(depths[p] for p in parts), wide), jnp.bfloat16)
+    cost = lambda parts: pl.CostEstimate(
+        flops=2 * sum(depths[p] for p in parts) * wide * HALF,
+        bytes_accessed=8 * sum(depths[p] for p in parts) * wide,
+        transcendentals=0,
+    )
     params = pltpu.CompilerParams(vmem_limit_bytes=32 * 2**20)
-    if first is None:
-        return pl.pallas_call(
-            first_part_kernel,
-            out_shape=jax.ShapeDtypeStruct((HALF, wide), jnp.float32),
-            in_specs=[VMEM] * 3,
-            out_specs=VMEM,
-            scratch_shapes=[gathered],
-            compiler_params=params,
-            cost_estimate=cost,
-        )(*own, other)
+    first = pl.pallas_call(
+        functools.partial(first_parts_kernel, early),
+        out_shape=jax.ShapeDtypeStruct((HALF, wide), jnp.float32),
+        in_specs=[VMEM] * (len(PARTS) + len(early)),
+        out_specs=VMEM,
+        scratch_shapes=[gathered(early)],
+        compiler_params=params,
+        cost_estimate=cost(early),
+    )(*own, *[other[p] for p in early])
     lanes = 128
     return pl.pallas_call(
-        second_part_kernel,
+        functools.partial(last_part_kernel, [last]),
         out_shape=jax.ShapeDtypeStruct((HALF // ROWS, wide // lanes * ROWS + 16, lanes), jnp.int16),
-        in_specs=[VMEM] * 4,
+        in_specs=[VMEM] * (len(PARTS) + 2),
         out_specs=VMEM,
-        scratch_shapes=[gathered, total],
+        scratch_shapes=[gathered([last]), pltpu.VMEM((HALF, wide), jnp.float32)],
         compiler_params=params,
-        cost_estimate=cost,
-    )(*own, other, first)
+        cost_estimate=cost([last]),
+    )(*own, other[last], first)
 
 
 def along(first, second, distance):
@@ -256,7 +268,7 @@
     slot[4] = jnp.concatenate([move(slot[2][: N // 2], 2), move(slot[6][N // 2 :], -2)])
     own = [jnp.stack([slot[d] for d in ORDER[slice(*part)]]) for part in PARTS]
     other = [lax.ppermute(part, "c", swap).reshape(-1, wide) for part in own]
-    messages = contract(own, other[1], contract(own, other[0], None))
+    messages = contract(own, other)
     parts = lax.all_to_all(messages, "x", 0, 0, tiled=True)
     return pl.pallas_call(
         sum_kernel,

time: 118 us -> 109 us (0.924)
  waiting for transfers between devices: 16.3 us -> 6.87 us
    ppermute x8, waiting for transfers between devices: 14.4 us -> 4.17 us  [per_device(): move = lambda value, d: lax.ppermute(value, AXES, along('z', 'y', d))]
  transfers between devices with their start and end apart: 11 -> 11, of which waited for: 6 -> 5; matrix products, arithmetic and copies ran while one was open for 0% -> 0% of each run, Pallas kernels for 1% -> 1%
where the time goes in v8:
time: 109 us; the launch traced here: 108 us
  starting transfers between devices  53.9 us (49%)
  blocking collectives  40.2 us (37%)
  waiting for transfers between devices  6.87 us (6%)
  Pallas kernels  4.33 us (4%)
  local copies, waits for them, and re-layouts  1.63 us (1%)
  other arithmetic  1.25 us (1%)
    ppermute x8, starting transfers between devices, per_device(): move = lambda value, d: lax.ppermute(value, AXES, along('z', 'y', d))  28 us
    all_to_all x1, blocking collectives, per_device(): parts = lax.all_to_all(messages, 'x', 0, 0, tiled=True)  25.9 us
    ppermute x1, starting transfers between devices, per_device(): lax.ppermute(send, 'c', swap)  16.1 us
    all_to_all x1, blocking collectives, exchange(): lax.all_to_all(blocks, AXES, 0, 0, tiled=True, axis_index_groups=groups(f...  14.3 us
    ppermute x2, starting transfers between devices, per_device(): other = [lax.ppermute(part, 'c', swap).reshape(-1, wide) for part in own]  9.84 us
    ppermute x8, waiting for transfers between devices, per_device(): move = lambda value, d: lax.ppermute(value, AXES, along('z', 'y', d))  4.17 us
  transfers between devices with their start and end apart: 11, of which 5 were waited for; matrix products, arithmetic and copies ran while one was open for 0% of the time, Pallas kernels for 1%

profile of v8, /device:TPU:1, one launch (start us, length us, event | category | flops | bytes accessed | tf_op | source)
XLA Modules:
  0.0 108.4 jit_solution(4063208648371194191)
XLA Ops:
  0.0 0.8 multiply_bitcast_fusion.limits_ref
  0.8 0.0 copy-start
  0.8 0.9 copy-done
  1.7 0.0 copy-start.1
  1.7 0.7 copy-done.1
  2.4 0.3 shard_map.46
  2.7 16.1 %collective-permute-start = (bf16[8,16,768]{2,1,0:T(8,128)(2,1)S(1)}, bf16[8,16,768]{2,1,0:T(8,128)(2,1)S(1)}, u32[]{:S(2)}, u32[]{:S(2)}) collective-permute-start(bf16[8,16,768]{2,1,0:T(8,128)(2,1)S(1)} %get-tuple-element.8), channel_id=1, source_target_pairs={{0,1},{1,0},{2,3},{3,2},{4,5},{5,4},{6,7},{7,6},{8,9},{9,8},{10,11... | collective-permute-start | bytes 589832 | tf_op jit(solution)/shard_map/ppermute | solution.py:262
  18.7 1.0 collective-permute-done
  19.8 14.3 %all_to_all.10 = bf16[8,32,768]{2,1,0:T(8,128)(2,1)S(1)} all-to-all(bf16[8,32,768]{2,1,0:T(8,128)(2,1)S(1)} %constant_dynamic-update-slice_fusion), channel_id=1, replica_groups={{0,128,256,384,512,640,768,896},{2,130,258,386,514,642,770,898},{4,132,..., dimensions={0} | all-to-all | bytes 786432 | tf_op jit(solution)/shard_map/all_to_all | solution.py:39
  34.1 4.4 %collective-permute-start.1 = (bf16[8,2,16,768]{3,2,1,0:T(8,128)(2,1)S(1)}, bf16[8,2,16,768]{3,2,1,0:T(8,128)(2,1)S(1)}, u32[]{:S(2)}, u32[]{:S(2)}) collective-permute-start(bf16[8,2,16,768]{3,2,1,0:T(8,128)(2,1)S(1)} %bitcast.18), channel_id=1, source_target_pairs={{0,4},{2,6},{4,8},{6,10},{8,12},{10,14},{12,0},{14,2},{16,20},{18,... | collective-permute-start | bytes 1179656 | tf_op jit(solution)/shard_map/ppermute | solution.py:265
  38.5 4.0 %collective-permute-start.2 = (bf16[8,2,16,768]{3,2,1,0:T(8,128)(2,1)S(1)}, bf16[8,2,16,768]{3,2,1,0:T(8,128)(2,1)S(1)}, u32[]{:S(2)}, u32[]{:S(2)}) collective-permute-start(bf16[8,2,16,768]{3,2,1,0:T(8,128)(2,1)S(1)} %bitcast.19), channel_id=1, source_target_pairs={{0,12},{2,14},{4,0},{6,2},{8,4},{10,6},{12,8},{14,10},{16,28},{18,... | collective-permute-start | bytes 1179656 | tf_op jit(solution)/shard_map/ppermute | solution.py:265
  42.6 2.4 %collective-permute-start.3 = (bf16[8,2,16,768]{3,2,1,0:T(8,128)(2,1)S(1)}, bf16[8,2,16,768]{3,2,1,0:T(8,128)(2,1)S(1)}, u32[]{:S(2)}, u32[]{:S(2)}) collective-permute-start(bf16[8,2,16,768]{3,2,1,0:T(8,128)(2,1)S(1)} %bitcast.20), channel_id=1, source_target_pairs={{0,2},{2,4},{4,6},{6,8},{8,10},{10,12},{12,14},{14,0},{16,18},{18,... | collective-permute-start | bytes 1179656 | tf_op jit(solution)/shard_map/ppermute | solution.py:265
  45.0 4.1 %collective-permute-start.4 = (bf16[8,2,16,768]{3,2,1,0:T(8,128)(2,1)S(1)}, bf16[8,2,16,768]{3,2,1,0:T(8,128)(2,1)S(1)}, u32[]{:S(2)}, u32[]{:S(2)}) collective-permute-start(bf16[8,2,16,768]{3,2,1,0:T(8,128)(2,1)S(1)} %bitcast.21), channel_id=1, source_target_pairs={{0,14},{2,0},{4,2},{6,4},{8,6},{10,8},{12,10},{14,12},{16,30},{18,... | collective-permute-start | bytes 1179656 | tf_op jit(solution)/shard_map/ppermute | solution.py:265
  49.1 0.0 collective-permute-done.1
  49.1 3.6 %collective-permute-start.5 = (bf16[8,2,16,768]{3,2,1,0:T(8,128)(2,1)S(1)}, bf16[8,2,16,768]{3,2,1,0:T(8,128)(2,1)S(1)}, u32[]{:S(2)}, u32[]{:S(2)}) collective-permute-start(bf16[8,2,16,768]{3,2,1,0:T(8,128)(2,1)S(1)} %collective-permute-done.1), channel_id=1, source_target_pairs={{0,2},{2,4},{4,6},{6,8},{8,10},{10,12},{12,14},{14,0},{16,18},{18,... | collective-permute-start | bytes 1179656 | tf_op jit(solution)/shard_map/ppermute | solution.py:265
  52.7 1.2 %collective-permute-done.2 = bf16[8,2,16,768]{3,2,1,0:T(8,128)(2,1)S(1)} collective-permute-done((bf16[8,2,16,768]{3,2,1,0:T(8,128)(2,1)S(1)}, bf16[8,2,16,768]{3,2,1,0:T(8,128)(2,1)S(1)}, u32[]{:S(2)}, u32[]{:S(2)}) %collective-permute-start.2) | collective-permute-done | bytes 393248 | tf_op jit(solution)/shard_map/ppermute | solution.py:265
  53.9 2.0 %collective-permute-start.6 = (bf16[8,2,16,768]{3,2,1,0:T(8,128)(2,1)S(1)}, bf16[8,2,16,768]{3,2,1,0:T(8,128)(2,1)S(1)}, u32[]{:S(2)}, u32[]{:S(2)}) collective-permute-start(bf16[8,2,16,768]{3,2,1,0:T(8,128)(2,1)S(1)} %collective-permute-done.2), channel_id=1, source_target_pairs={{0,14},{2,0},{4,2},{6,4},{8,6},{10,8},{12,10},{14,12},{16,30},{18,... | collective-permute-start | bytes 1179656 | tf_op jit(solution)/shard_map/ppermute | solution.py:265
  56.0 4.5 %collective-permute-start.7 = (bf16[4,2,16,768]{3,2,1,0:T(8,128)(2,1)S(1)}, bf16[4,2,16,768]{3,2,1,0:T(8,128)(2,1)S(1)}, u32[]{:S(2)}, u32[]{:S(2)}) collective-permute-start(bf16[4,2,16,768]{3,2,1,0:T(8,128)(2,1)S(1)} %slice.8), channel_id=1, source_target_pairs={{0,4},{2,6},{4,8},{6,10},{8,12},{10,14},{12,0},{14,2},{16,20},{18,... | collective-permute-start | bytes 589832 | tf_op jit(solution)/shard_map/ppermute | solution.py:265
  60.5 0.0 collective-permute-done.3
  60.5 2.9 %collective-permute-start.8 = (bf16[4,2,16,768]{3,2,1,0:T(8,128)(2,1)S(1)}, bf16[4,2,16,768]{3,2,1,0:T(8,128)(2,1)S(1)}, u32[]{:S(2)}, u32[]{:S(2)}) collective-permute-start(bf16[4,2,16,768]{3,2,1,0:T(8,128)(2,1)S(1)} %slice.9), channel_id=1, source_target_pairs={{0,12},{2,14},{4,0},{6,2},{8,4},{10,6},{12,8},{14,10},{16,28},{18,... | collective-permute-start | bytes 589832 | tf_op jit(solution)/shard_map/ppermute | solution.py:265
  63.4 0.2 pad_maximum_fusion.refs_0_
  63.6 3.0 %collective-permute-done.7 = bf16[4,2,16,768]{3,2,1,0:T(8,128)(2,1)S(1)} collective-permute-done((bf16[4,2,16,768]{3,2,1,0:T(8,128)(2,1)S(1)}, bf16[4,2,16,768]{3,2,1,0:T(8,128)(2,1)S(1)}, u32[]{:S(2)}, u32[]{:S(2)}) %collective-permute-start.7) | collective-permute-done | bytes 196640 | tf_op jit(solution)/shard_map/ppermute | solution.py:265
  66.6 7.5 %collective-permute-start.10 = (bf16[4,8,2,16,768]{4,3,2,1,0:T(8,128)(2,1)S(1)}, bf16[4,8,2,16,768]{4,3,2,1,0:T(8,128)(2,1)S(1)}, u32[]{:S(2)}, u32[]{:S(2)}) collective-permute-start(bf16[4,8,2,16,768]{4,3,2,1,0:T(8,128)(2,1)S(1)} %pad_maximum_fusion.refs_0_), channel_id=1, source_target_pairs={{0,1},{1,0},{2,3},{3,2},{4,5},{5,4},{6,7},{7,6},{8,9},{9,8},{10,11... | collective-permute-start | bytes 4718600 | tf_op jit(solution)/shard_map/ppermute | solution.py:270
  74.1 0.0 collective-permute-done.8
  74.2 0.0 collective-permute-done.4
  74.2 0.0 collective-permute-done.5
  74.2 0.0 collective-permute-done.6
  74.2 0.2 pad_maximum_fusion.1.refs_1_
  74.4 2.3 %collective-permute-start.9 = (bf16[4,8,2,16,768]{4,3,2,1,0:T(8,128)(2,1)S(1)}, bf16[4,8,2,16,768]{4,3,2,1,0:T(8,128)(2,1)S(1)}, u32[]{:S(2)}, u32[]{:S(2)}) collective-permute-start(bf16[4,8,2,16,768]{4,3,2,1,0:T(8,128)(2,1)S(1)} %pad_maximum_fusion.1.refs_1_), channel_id=1, source_target_pairs={{0,1},{1,0},{2,3},{3,2},{4,5},{5,4},{6,7},{7,6},{8,9},{9,8},{10,11... | collective-permute-start | bytes 4718600 | tf_op jit(solution)/shard_map/ppermute | solution.py:270
  76.7 0.4 collective-permute-done.10
  77.1 1.4 %shard_map.47.refs_3_ = f32[384,768]{1,0:T(8,128)S(1)} custom-call(bf16[4,8,2,16,768]{4,3,2,1,0:T(8,128)(2,1)S(1)} %pad_maximum_fusion.refs_0_, bf16[4,8,2,16,768]{4,3,2,1,0:T(8,128)(2,1)S(1)} %pad_maximum_fusion.1.refs_1_, bf16[1024,768]{1,0:T(8,128)(2,1)S(1)} %bitcast.15), custom_call_target="tpu_custom_call" | custom-call | flops 603979776 | bytes 6291456 | tf_op jit(solution)/shard_map/pallas_call | solution.py:230
  78.5 1.2 %collective-permute-done.9 = bf16[4,8,2,16,768]{4,3,2,1,0:T(8,128)(2,1)S(1)} collective-permute-done((bf16[4,8,2,16,768]{4,3,2,1,0:T(8,128)(2,1)S(1)}, bf16[4,8,2,16,768]{4,3,2,1,0:T(8,128)(2,1)S(1)}, u32[]{:S(2)}, u32[]{:S(2)}) %collective-permute-start.9) | collective-permute-done | bytes 1572896 | tf_op jit(solution)/shard_map/ppermute | solution.py:270
  79.8 1.9 %shard_map.48 = s16[8,304,128]{2,1,0:T(8,128)(2,1)S(1)} custom-call(bf16[4,8,2,16,768]{4,3,2,1,0:T(8,128)(2,1)S(1)} %pad_maximum_fusion.refs_0_, bf16[4,8,2,16,768]{4,3,2,1,0:T(8,128)(2,1)S(1)} %pad_maximum_fusion.1.refs_1_, bf16[1024,768]{1,0:T(8,128)(2,1)S(1)} %bitcast.16, f32[384,768]{1,0:T(8,128)S(1)} %shard_map.47.refs_3_), custom_call_target="tpu_custom_call" | custom-call | flops 603979776 | bytes 6291456 | tf_op jit(solution)/shard_map/pallas_call | solution.py:240
  81.6 25.9 %all_to_all.11.parts_ref = s16[8,304,128]{2,1,0:T(8,128)(2,1)S(1)} all-to-all(s16[8,304,128]{2,1,0:T(8,128)(2,1)S(1)} %shard_map.48), channel_id=1, replica_groups=mesh['y'=8,'x'=8,'z'=8,'c'=2] {'x'}, dimensions={0} | all-to-all | bytes 1245184 | tf_op jit(solution)/shard_map/all_to_all | solution.py:272
  107.5 0.8 shard_map.49
  (4 shorter events, 0.1 us)
Async XLA Ops:
  0.8 0.9 copy-start
  1.7 0.7 copy-start.1
  2.7 17.1 %collective-permute-start = (bf16[8,16,768]{2,1,0:T(8,128)(2,1)S(1)}, bf16[8,16,768]{2,1,0:T(8,128)(2,1)S(1)}, u32[]{:S(2)}, u32[]{:S(2)}) collective-permute-start(bf16[8,16,768]{2,1,0:T(8,128)(2,1)S(1)} %get-tuple-element.8), channel_id=1, source_target_pairs={{0,1},{1,0},{2,3},{3,2},{4,5},{5,4},{6,7},{7,6},{8,9},{9,8},{10,11... | collective-permute-start | bytes 589832 | tf_op jit(solution)/shard_map/ppermute | solution.py:262
  34.1 15.0 %collective-permute-start.1 = (bf16[8,2,16,768]{3,2,1,0:T(8,128)(2,1)S(1)}, bf16[8,2,16,768]{3,2,1,0:T(8,128)(2,1)S(1)}, u32[]{:S(2)}, u32[]{:S(2)}) collective-permute-start(bf16[8,2,16,768]{3,2,1,0:T(8,128)(2,1)S(1)} %bitcast.18), channel_id=1, source_target_pairs={{0,4},{2,6},{4,8},{6,10},{8,12},{10,14},{12,0},{14,2},{16,20},{18,... | collective-permute-start | bytes 1179656 | tf_op jit(solution)/shard_map/ppermute | solution.py:265
  38.5 15.4 %collective-permute-start.2 = (bf16[8,2,16,768]{3,2,1,0:T(8,128)(2,1)S(1)}, bf16[8,2,16,768]{3,2,1,0:T(8,128)(2,1)S(1)}, u32[]{:S(2)}, u32[]{:S(2)}) collective-permute-start(bf16[8,2,16,768]{3,2,1,0:T(8,128)(2,1)S(1)} %bitcast.19), channel_id=1, source_target_pairs={{0,12},{2,14},{4,0},{6,2},{8,4},{10,6},{12,8},{14,10},{16,28},{18,... | collective-permute-start | bytes 1179656 | tf_op jit(solution)/shard_map/ppermute | solution.py:265
  42.6 17.9 %collective-permute-start.3 = (bf16[8,2,16,768]{3,2,1,0:T(8,128)(2,1)S(1)}, bf16[8,2,16,768]{3,2,1,0:T(8,128)(2,1)S(1)}, u32[]{:S(2)}, u32[]{:S(2)}) collective-permute-start(bf16[8,2,16,768]{3,2,1,0:T(8,128)(2,1)S(1)} %bitcast.20), channel_id=1, source_target_pairs={{0,2},{2,4},{4,6},{6,8},{8,10},{10,12},{12,14},{14,0},{16,18},{18,... | collective-permute-start | bytes 1179656 | tf_op jit(solution)/shard_map/ppermute | solution.py:265
  45.0 29.2 %collective-permute-start.4 = (bf16[8,2,16,768]{3,2,1,0:T(8,128)(2,1)S(1)}, bf16[8,2,16,768]{3,2,1,0:T(8,128)(2,1)S(1)}, u32[]{:S(2)}, u32[]{:S(2)}) collective-permute-start(bf16[8,2,16,768]{3,2,1,0:T(8,128)(2,1)S(1)} %bitcast.21), channel_id=1, source_target_pairs={{0,14},{2,0},{4,2},{6,4},{8,6},{10,8},{12,10},{14,12},{16,30},{18,... | collective-permute-start | bytes 1179656 | tf_op jit(solution)/shard_map/ppermute | solution.py:265
  49.1 25.1 %collective-permute-start.5 = (bf16[8,2,16,768]{3,2,1,0:T(8,128)(2,1)S(1)}, bf16[8,2,16,768]{3,2,1,0:T(8,128)(2,1)S(1)}, u32[]{:S(2)}, u32[]{:S(2)}) collective-permute-start(bf16[8,2,16,768]{3,2,1,0:T(8,128)(2,1)S(1)} %collective-permute-done.1), channel_id=1, source_target_pairs={{0,2},{2,4},{4,6},{6,8},{8,10},{10,12},{12,14},{14,0},{16,18},{18,... | collective-permute-start | bytes 1179656 | tf_op jit(solution)/shard_map/ppermute | solution.py:265
  53.9 20.3 %collective-permute-start.6 = (bf16[8,2,16,768]{3,2,1,0:T(8,128)(2,1)S(1)}, bf16[8,2,16,768]{3,2,1,0:T(8,128)(2,1)S(1)}, u32[]{:S(2)}, u32[]{:S(2)}) collective-permute-start(bf16[8,2,16,768]{3,2,1,0:T(8,128)(2,1)S(1)} %collective-permute-done.2), channel_id=1, source_target_pairs={{0,14},{2,0},{4,2},{6,4},{8,6},{10,8},{12,10},{14,12},{16,30},{18,... | collective-permute-start | bytes 1179656 | tf_op jit(solution)/shard_map/ppermute | solution.py:265
  56.0 10.6 %collective-permute-start.7 = (bf16[4,2,16,768]{3,2,1,0:T(8,128)(2,1)S(1)}, bf16[4,2,16,768]{3,2,1,0:T(8,128)(2,1)S(1)}, u32[]{:S(2)}, u32[]{:S(2)}) collective-permute-start(bf16[4,2,16,768]{3,2,1,0:T(8,128)(2,1)S(1)} %slice.8), channel_id=1, source_target_pairs={{0,4},{2,6},{4,8},{6,10},{8,12},{10,14},{12,0},{14,2},{16,20},{18,... | collective-permute-start | bytes 589832 | tf_op jit(solution)/shard_map/ppermute | solution.py:265
  60.5 13.6 %collective-permute-start.8 = (bf16[4,2,16,768]{3,2,1,0:T(8,128)(2,1)S(1)}, bf16[4,2,16,768]{3,2,1,0:T(8,128)(2,1)S(1)}, u32[]{:S(2)}, u32[]{:S(2)}) collective-permute-start(bf16[4,2,16,768]{3,2,1,0:T(8,128)(2,1)S(1)} %slice.9), channel_id=1, source_target_pairs={{0,12},{2,14},{4,0},{6,2},{8,4},{10,6},{12,8},{14,10},{16,28},{18,... | collective-permute-start | bytes 589832 | tf_op jit(solution)/shard_map/ppermute | solution.py:265
  66.6 10.6 %collective-permute-start.10 = (bf16[4,8,2,16,768]{4,3,2,1,0:T(8,128)(2,1)S(1)}, bf16[4,8,2,16,768]{4,3,2,1,0:T(8,128)(2,1)S(1)}, u32[]{:S(2)}, u32[]{:S(2)}) collective-permute-start(bf16[4,8,2,16,768]{4,3,2,1,0:T(8,128)(2,1)S(1)} %pad_maximum_fusion.refs_0_), channel_id=1, source_target_pairs={{0,1},{1,0},{2,3},{3,2},{4,5},{5,4},{6,7},{7,6},{8,9},{9,8},{10,11... | collective-permute-start | bytes 4718600 | tf_op jit(solution)/shard_map/ppermute | solution.py:270
  74.4 5.3 %collective-permute-start.9 = (bf16[4,8,2,16,768]{4,3,2,1,0:T(8,128)(2,1)S(1)}, bf16[4,8,2,16,768]{4,3,2,1,0:T(8,128)(2,1)S(1)}, u32[]{:S(2)}, u32[]{:S(2)}) collective-permute-start(bf16[4,8,2,16,768]{4,3,2,1,0:T(8,128)(2,1)S(1)} %pad_maximum_fusion.1.refs_1_), channel_id=1, source_target_pairs={{0,1},{1,0},{2,3},{3,2},{4,5},{5,4},{6,7},{7,6},{8,9},{9,8},{10,11... | collective-permute-start | bytes 4718600 | tf_op jit(solution)/shard_map/ppermute | solution.py:270

commit v9 on v8

--- a/solution.py
+++ b/solution.py
@@ -14,7 +14,7 @@
 AXES = ("y", "x", "z", "c")
 HALF = 384
 ROWS = 48
-ORDER = (0, 2, 6, 1, 7, 3, 5, 4)
+ORDER = (0, 2, 6, 4, 1, 7, 3, 5)
 PARTS = ((0, 4), (4, 8))
 STEPS = 14
 VMEM = pl.BlockSpec(memory_space=pltpu.VMEM)

time: 109 us -> 116 us (1.064)
  starting transfers between devices: 53.9 us -> 59 us
  waiting for transfers between devices: 6.87 us -> 9.04 us
    ppermute x2, starting transfers between devices: 9.84 us -> 14.3 us  [per_device(): other = [lax.ppermute(part, 'c', swap).reshape(-1, wide) for part in own]]
    ppermute x8, waiting for transfers between devices: 4.17 us -> 6.39 us  [per_device(): move = lambda value, d: lax.ppermute(value, AXES, along('z', 'y', d))]
  transfers between devices with their start and end apart: 11 -> 11, of which waited for: 5 -> 4; matrix products, arithmetic and copies ran while one was open for 0% -> 0% of each run, Pallas kernels for 1% -> 1%
where the time goes in v9:
time: 116 us; the launch traced here: 115 us
  starting transfers between devices  59 us (51%)
  blocking collectives  39.7 us (34%)
  waiting for transfers between devices  9.04 us (8%)
  Pallas kernels  4.36 us (4%)
  local copies, waits for them, and re-layouts  1.63 us (1%)
  other arithmetic  1.25 us (1%)
    ppermute x8, starting transfers between devices, per_device(): move = lambda value, d: lax.ppermute(value, AXES, along('z', 'y', d))  28.7 us
    all_to_all x1, blocking collectives, per_device(): parts = lax.all_to_all(messages, 'x', 0, 0, tiled=True)  25.4 us
    ppermute x1, starting transfers between devices, per_device(): lax.ppermute(send, 'c', swap)  16.1 us
    all_to_all x1, blocking collectives, exchange(): lax.all_to_all(blocks, AXES, 0, 0, tiled=True, axis_index_groups=groups(f...  14.3 us
    ppermute x2, starting transfers between devices, per_device(): other = [lax.ppermute(part, 'c', swap).reshape(-1, wide) for part in own]  14.3 us
    ppermute x8, waiting for transfers between devices, per_device(): move = lambda value, d: lax.ppermute(value, AXES, along('z', 'y', d))  6.39 us
  transfers between devices with their start and end apart: 11, of which 4 were waited for; matrix products, arithmetic and copies ran while one was open for 0% of the time, Pallas kernels for 1%

profile of v9, /device:TPU:1, one launch (start us, length us, event | category | flops | bytes accessed | tf_op | source)
XLA Modules:
  0.0 115.2 jit_solution(13275592001758947460)
XLA Ops:
  0.0 0.8 multiply_bitcast_fusion.limits_ref
  0.8 0.0 copy-start
  0.8 0.9 copy-done
  1.7 0.0 copy-start.1
  1.7 0.7 copy-done.1
  2.4 0.3 shard_map.46
  2.7 16.1 %collective-permute-start = (bf16[8,16,768]{2,1,0:T(8,128)(2,1)S(1)}, bf16[8,16,768]{2,1,0:T(8,128)(2,1)S(1)}, u32[]{:S(2)}, u32[]{:S(2)}) collective-permute-start(bf16[8,16,768]{2,1,0:T(8,128)(2,1)S(1)} %get-tuple-element.8), channel_id=1, source_target_pairs={{0,1},{1,0},{2,3},{3,2},{4,5},{5,4},{6,7},{7,6},{8,9},{9,8},{10,11... | collective-permute-start | bytes 589832 | tf_op jit(solution)/shard_map/ppermute | solution.py:262
  18.7 1.0 collective-permute-done
  19.8 14.3 %all_to_all.10 = bf16[8,32,768]{2,1,0:T(8,128)(2,1)S(1)} all-to-all(bf16[8,32,768]{2,1,0:T(8,128)(2,1)S(1)} %constant_dynamic-update-slice_fusion), channel_id=1, replica_groups={{0,128,256,384,512,640,768,896},{2,130,258,386,514,642,770,898},{4,132,..., dimensions={0} | all-to-all | bytes 786432 | tf_op jit(solution)/shard_map/all_to_all | solution.py:39
  34.1 4.4 %collective-permute-start.1 = (bf16[8,2,16,768]{3,2,1,0:T(8,128)(2,1)S(1)}, bf16[8,2,16,768]{3,2,1,0:T(8,128)(2,1)S(1)}, u32[]{:S(2)}, u32[]{:S(2)}) collective-permute-start(bf16[8,2,16,768]{3,2,1,0:T(8,128)(2,1)S(1)} %bitcast.18), channel_id=1, source_target_pairs={{0,4},{2,6},{4,8},{6,10},{8,12},{10,14},{12,0},{14,2},{16,20},{18,... | collective-permute-start | bytes 1179656 | tf_op jit(solution)/shard_map/ppermute | solution.py:265
  38.5 4.0 %collective-permute-start.2 = (bf16[8,2,16,768]{3,2,1,0:T(8,128)(2,1)S(1)}, bf16[8,2,16,768]{3,2,1,0:T(8,128)(2,1)S(1)}, u32[]{:S(2)}, u32[]{:S(2)}) collective-permute-start(bf16[8,2,16,768]{3,2,1,0:T(8,128)(2,1)S(1)} %bitcast.19), channel_id=1, source_target_pairs={{0,12},{2,14},{4,0},{6,2},{8,4},{10,6},{12,8},{14,10},{16,28},{18,... | collective-permute-start | bytes 1179656 | tf_op jit(solution)/shard_map/ppermute | solution.py:265
  42.6 5.6 %collective-permute-done.1 = bf16[8,2,16,768]{3,2,1,0:T(8,128)(2,1)S(1)} collective-permute-done((bf16[8,2,16,768]{3,2,1,0:T(8,128)(2,1)S(1)}, bf16[8,2,16,768]{3,2,1,0:T(8,128)(2,1)S(1)}, u32[]{:S(2)}, u32[]{:S(2)}) %collective-permute-start.1) | collective-permute-done | bytes 393248 | tf_op jit(solution)/shard_map/ppermute | solution.py:265
  48.2 4.6 %collective-permute-start.3 = (bf16[4,2,16,768]{3,2,1,0:T(8,128)(2,1)S(1)}, bf16[4,2,16,768]{3,2,1,0:T(8,128)(2,1)S(1)}, u32[]{:S(2)}, u32[]{:S(2)}) collective-permute-start(bf16[4,2,16,768]{3,2,1,0:T(8,128)(2,1)S(1)} %slice.8), channel_id=1, source_target_pairs={{0,4},{2,6},{4,8},{6,10},{8,12},{10,14},{12,0},{14,2},{16,20},{18,... | collective-permute-start | bytes 589832 | tf_op jit(solution)/shard_map/ppermute | solution.py:265
  52.8 0.8 collective-permute-done.2
  53.6 3.9 %collective-permute-start.4 = (bf16[4,2,16,768]{3,2,1,0:T(8,128)(2,1)S(1)}, bf16[4,2,16,768]{3,2,1,0:T(8,128)(2,1)S(1)}, u32[]{:S(2)}, u32[]{:S(2)}) collective-permute-start(bf16[4,2,16,768]{3,2,1,0:T(8,128)(2,1)S(1)} %slice.9), channel_id=1, source_target_pairs={{0,12},{2,14},{4,0},{6,2},{8,4},{10,6},{12,8},{14,10},{16,28},{18,... | collective-permute-start | bytes 589832 | tf_op jit(solution)/shard_map/ppermute | solution.py:265
  57.5 2.7 %collective-permute-start.5 = (bf16[8,2,16,768]{3,2,1,0:T(8,128)(2,1)S(1)}, bf16[8,2,16,768]{3,2,1,0:T(8,128)(2,1)S(1)}, u32[]{:S(2)}, u32[]{:S(2)}) collective-permute-start(bf16[8,2,16,768]{3,2,1,0:T(8,128)(2,1)S(1)} %bitcast.20), channel_id=1, source_target_pairs={{0,2},{2,4},{4,6},{6,8},{8,10},{10,12},{12,14},{14,0},{16,18},{18,... | collective-permute-start | bytes 1179656 | tf_op jit(solution)/shard_map/ppermute | solution.py:265
  60.2 3.7 %collective-permute-start.6 = (bf16[8,2,16,768]{3,2,1,0:T(8,128)(2,1)S(1)}, bf16[8,2,16,768]{3,2,1,0:T(8,128)(2,1)S(1)}, u32[]{:S(2)}, u32[]{:S(2)}) collective-permute-start(bf16[8,2,16,768]{3,2,1,0:T(8,128)(2,1)S(1)} %bitcast.21), channel_id=1, source_target_pairs={{0,14},{2,0},{4,2},{6,4},{8,6},{10,8},{12,10},{14,12},{16,30},{18,... | collective-permute-start | bytes 1179656 | tf_op jit(solution)/shard_map/ppermute | solution.py:265
  64.0 1.9 %collective-permute-start.8 = (bf16[8,2,16,768]{3,2,1,0:T(8,128)(2,1)S(1)}, bf16[8,2,16,768]{3,2,1,0:T(8,128)(2,1)S(1)}, u32[]{:S(2)}, u32[]{:S(2)}) collective-permute-start(bf16[8,2,16,768]{3,2,1,0:T(8,128)(2,1)S(1)} %collective-permute-done.2), channel_id=1, source_target_pairs={{0,14},{2,0},{4,2},{6,4},{8,6},{10,8},{12,10},{14,12},{16,30},{18,... | collective-permute-start | bytes 1179656 | tf_op jit(solution)/shard_map/ppermute | solution.py:265
  65.9 0.0 collective-permute-done.3
  65.9 3.4 %collective-permute-start.7 = (bf16[8,2,16,768]{3,2,1,0:T(8,128)(2,1)S(1)}, bf16[8,2,16,768]{3,2,1,0:T(8,128)(2,1)S(1)}, u32[]{:S(2)}, u32[]{:S(2)}) collective-permute-start(bf16[8,2,16,768]{3,2,1,0:T(8,128)(2,1)S(1)} %collective-permute-done.1), channel_id=1, source_target_pairs={{0,2},{2,4},{4,6},{6,8},{8,10},{10,12},{12,14},{14,0},{16,18},{18,... | collective-permute-start | bytes 1179656 | tf_op jit(solution)/shard_map/ppermute | solution.py:265
  69.3 0.0 collective-permute-done.4
  69.3 0.2 pad_maximum_fusion.refs_0_
  69.5 6.5 %collective-permute-start.10 = (bf16[4,8,2,16,768]{4,3,2,1,0:T(8,128)(2,1)S(1)}, bf16[4,8,2,16,768]{4,3,2,1,0:T(8,128)(2,1)S(1)}, u32[]{:S(2)}, u32[]{:S(2)}) collective-permute-start(bf16[4,8,2,16,768]{4,3,2,1,0:T(8,128)(2,1)S(1)} %pad_maximum_fusion.refs_0_), channel_id=1, source_target_pairs={{0,1},{1,0},{2,3},{3,2},{4,5},{5,4},{6,7},{7,6},{8,9},{9,8},{10,11... | collective-permute-start | bytes 4718600 | tf_op jit(solution)/shard_map/ppermute | solution.py:270
  76.0 0.0 collective-permute-done.5
  76.0 0.0 collective-permute-done.6
  76.0 0.0 collective-permute-done.8
  76.1 0.0 collective-permute-done.7
  76.1 0.2 pad_maximum_fusion.1.refs_1_
  76.3 7.8 %collective-permute-start.9 = (bf16[4,8,2,16,768]{4,3,2,1,0:T(8,128)(2,1)S(1)}, bf16[4,8,2,16,768]{4,3,2,1,0:T(8,128)(2,1)S(1)}, u32[]{:S(2)}, u32[]{:S(2)}) collective-permute-start(bf16[4,8,2,16,768]{4,3,2,1,0:T(8,128)(2,1)S(1)} %pad_maximum_fusion.1.refs_1_), channel_id=1, source_target_pairs={{0,1},{1,0},{2,3},{3,2},{4,5},{5,4},{6,7},{7,6},{8,9},{9,8},{10,11... | collective-permute-start | bytes 4718600 | tf_op jit(solution)/shard_map/ppermute | solution.py:270
  84.1 0.0 collective-permute-done.10
  84.1 1.4 %shard_map.47.refs_3_ = f32[384,768]{1,0:T(8,128)S(1)} custom-call(bf16[4,8,2,16,768]{4,3,2,1,0:T(8,128)(2,1)S(1)} %pad_maximum_fusion.refs_0_, bf16[4,8,2,16,768]{4,3,2,1,0:T(8,128)(2,1)S(1)} %pad_maximum_fusion.1.refs_1_, bf16[1024,768]{1,0:T(8,128)(2,1)S(1)} %bitcast.15), custom_call_target="tpu_custom_call" | custom-call | flops 603979776 | bytes 6291456 | tf_op jit(solution)/shard_map/pallas_call | solution.py:230
  85.5 1.6 %collective-permute-done.9 = bf16[4,8,2,16,768]{4,3,2,1,0:T(8,128)(2,1)S(1)} collective-permute-done((bf16[4,8,2,16,768]{4,3,2,1,0:T(8,128)(2,1)S(1)}, bf16[4,8,2,16,768]{4,3,2,1,0:T(8,128)(2,1)S(1)}, u32[]{:S(2)}, u32[]{:S(2)}) %collective-permute-start.9) | collective-permute-done | bytes 1572896 | tf_op jit(solution)/shard_map/ppermute | solution.py:270
  87.1 1.9 %shard_map.48 = s16[8,304,128]{2,1,0:T(8,128)(2,1)S(1)} custom-call(bf16[4,8,2,16,768]{4,3,2,1,0:T(8,128)(2,1)S(1)} %pad_maximum_fusion.refs_0_, bf16[4,8,2,16,768]{4,3,2,1,0:T(8,128)(2,1)S(1)} %pad_maximum_fusion.1.refs_1_, bf16[1024,768]{1,0:T(8,128)(2,1)S(1)} %bitcast.16, f32[384,768]{1,0:T(8,128)S(1)} %shard_map.47.refs_3_), custom_call_target="tpu_custom_call" | custom-call | flops 603979776 | bytes 6291456 | tf_op jit(solution)/shard_map/pallas_call | solution.py:240
  89.0 25.4 %all_to_all.11.parts_ref = s16[8,304,128]{2,1,0:T(8,128)(2,1)S(1)} all-to-all(s16[8,304,128]{2,1,0:T(8,128)(2,1)S(1)} %shard_map.48), channel_id=1, replica_groups=mesh['y'=8,'x'=8,'z'=8,'c'=2] {'x'}, dimensions={0} | all-to-all | bytes 1245184 | tf_op jit(solution)/shard_map/all_to_all | solution.py:272
  114.4 0.8 shard_map.49
  (4 shorter events, 0.1 us)
Async XLA Ops:
  0.8 0.9 copy-start
  1.7 0.7 copy-start.1
  2.7 17.1 %collective-permute-start = (bf16[8,16,768]{2,1,0:T(8,128)(2,1)S(1)}, bf16[8,16,768]{2,1,0:T(8,128)(2,1)S(1)}, u32[]{:S(2)}, u32[]{:S(2)}) collective-permute-start(bf16[8,16,768]{2,1,0:T(8,128)(2,1)S(1)} %get-tuple-element.8), channel_id=1, source_target_pairs={{0,1},{1,0},{2,3},{3,2},{4,5},{5,4},{6,7},{7,6},{8,9},{9,8},{10,11... | collective-permute-start | bytes 589832 | tf_op jit(solution)/shard_map/ppermute | solution.py:262
  34.1 14.1 %collective-permute-start.1 = (bf16[8,2,16,768]{3,2,1,0:T(8,128)(2,1)S(1)}, bf16[8,2,16,768]{3,2,1,0:T(8,128)(2,1)S(1)}, u32[]{:S(2)}, u32[]{:S(2)}) collective-permute-start(bf16[8,2,16,768]{3,2,1,0:T(8,128)(2,1)S(1)} %bitcast.18), channel_id=1, source_target_pairs={{0,4},{2,6},{4,8},{6,10},{8,12},{10,14},{12,0},{14,2},{16,20},{18,... | collective-permute-start | bytes 1179656 | tf_op jit(solution)/shard_map/ppermute | solution.py:265
  38.5 15.0 %collective-permute-start.2 = (bf16[8,2,16,768]{3,2,1,0:T(8,128)(2,1)S(1)}, bf16[8,2,16,768]{3,2,1,0:T(8,128)(2,1)S(1)}, u32[]{:S(2)}, u32[]{:S(2)}) collective-permute-start(bf16[8,2,16,768]{3,2,1,0:T(8,128)(2,1)S(1)} %bitcast.19), channel_id=1, source_target_pairs={{0,12},{2,14},{4,0},{6,2},{8,4},{10,6},{12,8},{14,10},{16,28},{18,... | collective-permute-start | bytes 1179656 | tf_op jit(solution)/shard_map/ppermute | solution.py:265
  48.2 17.7 %collective-permute-start.3 = (bf16[4,2,16,768]{3,2,1,0:T(8,128)(2,1)S(1)}, bf16[4,2,16,768]{3,2,1,0:T(8,128)(2,1)S(1)}, u32[]{:S(2)}, u32[]{:S(2)}) collective-permute-start(bf16[4,2,16,768]{3,2,1,0:T(8,128)(2,1)S(1)} %slice.8), channel_id=1, source_target_pairs={{0,4},{2,6},{4,8},{6,10},{8,12},{10,14},{12,0},{14,2},{16,20},{18,... | collective-permute-start | bytes 589832 | tf_op jit(solution)/shard_map/ppermute | solution.py:265
  53.6 15.7 %collective-permute-start.4 = (bf16[4,2,16,768]{3,2,1,0:T(8,128)(2,1)S(1)}, bf16[4,2,16,768]{3,2,1,0:T(8,128)(2,1)S(1)}, u32[]{:S(2)}, u32[]{:S(2)}) collective-permute-start(bf16[4,2,16,768]{3,2,1,0:T(8,128)(2,1)S(1)} %slice.9), channel_id=1, source_target_pairs={{0,12},{2,14},{4,0},{6,2},{8,4},{10,6},{12,8},{14,10},{16,28},{18,... | collective-permute-start | bytes 589832 | tf_op jit(solution)/shard_map/ppermute | solution.py:265
  57.5 18.6 %collective-permute-start.5 = (bf16[8,2,16,768]{3,2,1,0:T(8,128)(2,1)S(1)}, bf16[8,2,16,768]{3,2,1,0:T(8,128)(2,1)S(1)}, u32[]{:S(2)}, u32[]{:S(2)}) collective-permute-start(bf16[8,2,16,768]{3,2,1,0:T(8,128)(2,1)S(1)} %bitcast.20), channel_id=1, source_target_pairs={{0,2},{2,4},{4,6},{6,8},{8,10},{10,12},{12,14},{14,0},{16,18},{18,... | collective-permute-start | bytes 1179656 | tf_op jit(solution)/shard_map/ppermute | solution.py:265
  60.2 15.8 %collective-permute-start.6 = (bf16[8,2,16,768]{3,2,1,0:T(8,128)(2,1)S(1)}, bf16[8,2,16,768]{3,2,1,0:T(8,128)(2,1)S(1)}, u32[]{:S(2)}, u32[]{:S(2)}) collective-permute-start(bf16[8,2,16,768]{3,2,1,0:T(8,128)(2,1)S(1)} %bitcast.21), channel_id=1, source_target_pairs={{0,14},{2,0},{4,2},{6,4},{8,6},{10,8},{12,10},{14,12},{16,30},{18,... | collective-permute-start | bytes 1179656 | tf_op jit(solution)/shard_map/ppermute | solution.py:265
  64.0 12.1 %collective-permute-start.8 = (bf16[8,2,16,768]{3,2,1,0:T(8,128)(2,1)S(1)}, bf16[8,2,16,768]{3,2,1,0:T(8,128)(2,1)S(1)}, u32[]{:S(2)}, u32[]{:S(2)}) collective-permute-start(bf16[8,2,16,768]{3,2,1,0:T(8,128)(2,1)S(1)} %collective-permute-done.2), channel_id=1, source_target_pairs={{0,14},{2,0},{4,2},{6,4},{8,6},{10,8},{12,10},{14,12},{16,30},{18,... | collective-permute-start | bytes 1179656 | tf_op jit(solution)/shard_map/ppermute | solution.py:265
  65.9 10.2 %collective-permute-start.7 = (bf16[8,2,16,768]{3,2,1,0:T(8,128)(2,1)S(1)}, bf16[8,2,16,768]{3,2,1,0:T(8,128)(2,1)S(1)}, u32[]{:S(2)}, u32[]{:S(2)}) collective-permute-start(bf16[8,2,16,768]{3,2,1,0:T(8,128)(2,1)S(1)} %collective-permute-done.1), channel_id=1, source_target_pairs={{0,2},{2,4},{4,6},{6,8},{8,10},{10,12},{12,14},{14,0},{16,18},{18,... | collective-permute-start | bytes 1179656 | tf_op jit(solution)/shard_map/ppermute | solution.py:265
  69.5 14.5 %collective-permute-start.10 = (bf16[4,8,2,16,768]{4,3,2,1,0:T(8,128)(2,1)S(1)}, bf16[4,8,2,16,768]{4,3,2,1,0:T(8,128)(2,1)S(1)}, u32[]{:S(2)}, u32[]{:S(2)}) collective-permute-start(bf16[4,8,2,16,768]{4,3,2,1,0:T(8,128)(2,1)S(1)} %pad_maximum_fusion.refs_0_), channel_id=1, source_target_pairs={{0,1},{1,0},{2,3},{3,2},{4,5},{5,4},{6,7},{7,6},{8,9},{9,8},{10,11... | collective-permute-start | bytes 4718600 | tf_op jit(solution)/shard_map/ppermute | solution.py:270
  76.3 10.8 %collective-permute-start.9 = (bf16[4,8,2,16,768]{4,3,2,1,0:T(8,128)(2,1)S(1)}, bf16[4,8,2,16,768]{4,3,2,1,0:T(8,128)(2,1)S(1)}, u32[]{:S(2)}, u32[]{:S(2)}) collective-permute-start(bf16[4,8,2,16,768]{4,3,2,1,0:T(8,128)(2,1)S(1)} %pad_maximum_fusion.1.refs_1_), channel_id=1, source_target_pairs={{0,1},{1,0},{2,3},{3,2},{4,5},{5,4},{6,7},{7,6},{8,9},{9,8},{10,11... | collective-permute-start | bytes 4718600 | tf_op jit(solution)/shard_map/ppermute | solution.py:270

commit v10 on v9

--- a/solution.py
+++ b/solution.py
@@ -14,7 +14,7 @@
 AXES = ("y", "x", "z", "c")
 HALF = 384
 ROWS = 48
-ORDER = (0, 2, 6, 4, 1, 7, 3, 5)
+OFFSETS = (0, -2, 2, 1, -1, 3, -3, 4)
 PARTS = ((0, 4), (4, 8))
 STEPS = 14
 VMEM = pl.BlockSpec(memory_space=pltpu.VMEM)
@@ -114,6 +114,10 @@
     )(coefficients, limits, row_weight.reshape(1, -1))
 
 
+def away(place, offset):
+    return lax.rem(place + (1 - 2 * lax.rem(place, 2)) * offset + N, N)
+
+
 def contract_part(own_refs, other_ref, gathered, part, write):
     places, two, rows, wide = own_refs[0].shape[1:]
     core = lax.axis_index("c")
@@ -122,11 +126,11 @@
     tile = 256
 
     def gather(columns):
-        for k, distance in enumerate(ORDER[slice(*PARTS[part])]):
-            inner = lax.rem(theirs + N - distance, N)
+        for k, offset in enumerate(OFFSETS[slice(*PARTS[part])]):
+            inner = away(theirs, offset)
             for own_ref, (first, last) in zip(own_refs, PARTS):
                 for slot in range(first, last):
-                    place = lax.rem(mine + N - ORDER[slot], N)
+                    place = away(mine, OFFSETS[slot])
                     for h in range(two):
                         at = pl.multiple_of(((k * places + place) * two + h) * rows, rows)
                         gathered[pl.ds(at, rows), columns] = own_ref[slot - first, inner, 1 - h, :, columns]
@@ -248,10 +252,10 @@
     )(*own, other[last], first)
 
 
-def along(first, second, distance):
+def along(first, second, step):
     pairs = []
     for ring in groups(first, second):
-        pairs += [(ring[i], ring[(i + distance) % N]) for i in range(N)]
+        pairs += [(ring[i], ring[(i + (step if i % 2 == 0 else -step)) % N]) for i in range(N)]
     return pairs
 
 
@@ -262,11 +266,10 @@
     blocks = lax.dynamic_update_slice(keep, lax.ppermute(send, "c", swap), (0, rows, 0))
     wide = blocks.shape[2]
     blocks = exchange(blocks, "y", "z").reshape(N, 2, rows, wide)
-    move = lambda value, d: lax.ppermute(value, AXES, along("z", "y", d))
-    slot = {0: blocks, 2: move(blocks, 2), 6: move(blocks, -2), 1: move(blocks, 1), 7: move(blocks, -1)}
-    slot[3], slot[5] = move(slot[2], 1), move(slot[6], -1)
-    slot[4] = jnp.concatenate([move(slot[2][: N // 2], 2), move(slot[6][N // 2 :], -2)])
-    own = [jnp.stack([slot[d] for d in ORDER[slice(*part)]]) for part in PARTS]
+    move = lambda value, step: lax.ppermute(value, AXES, along("z", "y", step))
+    slot = {0: blocks, -2: move(blocks, 2), 2: move(blocks, -2), 1: move(blocks, 1), -1: move(blocks, -1)}
+    slot[4], slot[3], slot[-3] = move(slot[-2], 2), move(slot[-2], 1), move(slot[2], -1)
+    own = [jnp.stack([slot[k] for k in OFFSETS[slice(*part)]]) for part in PARTS]
     other = [lax.ppermute(part, "c", swap).reshape(-1, wide) for part in own]
     messages = contract(own, other)
     parts = lax.all_to_all(messages, "x", 0, 0, tiled=True)

time: 116 us -> 106 us (0.914)
  waiting for transfers between devices: 9.04 us -> 3.66 us
  starting transfers between devices: 59 us -> 55.3 us
    ppermute x8 -> x7, waiting for transfers between devices: 6.39 us -> 1.01 us  [per_device(): move = lambda value, step: lax.ppermute(value, AXES, along('z', 'y', step))]
    ppermute x8 -> x7, starting transfers between devices: 28.7 us -> 25.7 us  [per_device(): move = lambda value, step: lax.ppermute(value, AXES, along('z', 'y', step))]
  transfers between devices with their start and end apart: 11 -> 10, of which waited for: 4 -> 3; matrix products, arithmetic and copies ran while one was open for 0% -> 0% of each run, Pallas kernels for 1% -> 1%
where the time goes in v10:
time: 106 us
  starting transfers between devices  55.3 us (52%)
  blocking collectives  39.3 us (37%)
  Pallas kernels  4.37 us (4%)
  waiting for transfers between devices  3.66 us (3%)
  local copies, waits for them, and re-layouts  1.6 us (2%)
  other arithmetic  1.21 us (1%)
    ppermute x7, starting transfers between devices, per_device(): move = lambda value, step: lax.ppermute(value, AXES, along('z', 'y', step))  25.7 us
    all_to_all x1, blocking collectives, per_device(): parts = lax.all_to_all(messages, 'x', 0, 0, tiled=True)  25 us
    ppermute x1, starting transfers between devices, per_device(): lax.ppermute(send, 'c', swap)  16.1 us
    all_to_all x1, blocking collectives, exchange(): lax.all_to_all(blocks, AXES, 0, 0, tiled=True, axis_index_groups=groups(f...  14.3 us
    ppermute x2, starting transfers between devices, per_device(): other = [lax.ppermute(part, 'c', swap).reshape(-1, wide) for part in own]  13.5 us
  transfers between devices with their start and end apart: 10, of which 3 were waited for; matrix products, arithmetic and copies ran while one was open for 0% of the time, Pallas kernels for 1%

profile of v10, /device:TPU:1, one launch (start us, length us, event | category | flops | bytes accessed | tf_op | source)
XLA Modules:
  0.0 105.6 jit_solution(12377580939321205498)
XLA Ops:
  0.0 0.8 multiply_bitcast_fusion.limits_ref
  0.8 0.0 copy-start
  0.8 0.9 copy-done
  1.7 0.0 copy-start.1
  1.7 0.7 copy-done.1
  2.4 0.3 shard_map.46
  2.7 16.1 %collective-permute-start = (bf16[8,16,768]{2,1,0:T(8,128)(2,1)S(1)}, bf16[8,16,768]{2,1,0:T(8,128)(2,1)S(1)}, u32[]{:S(2)}, u32[]{:S(2)}) collective-permute-start(bf16[8,16,768]{2,1,0:T(8,128)(2,1)S(1)} %get-tuple-element.8), channel_id=1, source_target_pairs={{0,1},{1,0},{2,3},{3,2},{4,5},{5,4},{6,7},{7,6},{8,9},{9,8},{10,11... | collective-permute-start | bytes 589832 | tf_op jit(solution)/shard_map/ppermute | solution.py:266
  18.7 1.0 collective-permute-done
  19.8 14.3 %all_to_all.10 = bf16[8,32,768]{2,1,0:T(8,128)(2,1)S(1)} all-to-all(bf16[8,32,768]{2,1,0:T(8,128)(2,1)S(1)} %constant_dynamic-update-slice_fusion), channel_id=1, replica_groups={{0,128,256,384,512,640,768,896},{2,130,258,386,514,642,770,898},{4,132,..., dimensions={0} | all-to-all | bytes 786432 | tf_op jit(solution)/shard_map/all_to_all | solution.py:39
  34.1 4.4 %collective-permute-start.1 = (bf16[8,2,16,768]{3,2,1,0:T(8,128)(2,1)S(1)}, bf16[8,2,16,768]{3,2,1,0:T(8,128)(2,1)S(1)}, u32[]{:S(2)}, u32[]{:S(2)}) collective-permute-start(bf16[8,2,16,768]{3,2,1,0:T(8,128)(2,1)S(1)} %bitcast.17), channel_id=1, source_target_pairs={{0,4},{2,14},{4,8},{6,2},{8,12},{10,6},{12,0},{14,10},{16,20},{18,... | collective-permute-start | bytes 1179656 | tf_op jit(solution)/shard_map/ppermute | solution.py:269
  38.5 4.0 %collective-permute-start.2 = (bf16[8,2,16,768]{3,2,1,0:T(8,128)(2,1)S(1)}, bf16[8,2,16,768]{3,2,1,0:T(8,128)(2,1)S(1)}, u32[]{:S(2)}, u32[]{:S(2)}) collective-permute-start(bf16[8,2,16,768]{3,2,1,0:T(8,128)(2,1)S(1)} %bitcast.18), channel_id=1, source_target_pairs={{0,12},{2,6},{4,0},{6,10},{8,4},{10,14},{12,8},{14,2},{16,28},{18,... | collective-permute-start | bytes 1179656 | tf_op jit(solution)/shard_map/ppermute | solution.py:269
  42.6 2.4 %collective-permute-start.3 = (bf16[8,2,16,768]{3,2,1,0:T(8,128)(2,1)S(1)}, bf16[8,2,16,768]{3,2,1,0:T(8,128)(2,1)S(1)}, u32[]{:S(2)}, u32[]{:S(2)}) collective-permute-start(bf16[8,2,16,768]{3,2,1,0:T(8,128)(2,1)S(1)} %bitcast.19), channel_id=1, source_target_pairs={{0,2},{2,0},{4,6},{6,4},{8,10},{10,8},{12,14},{14,12},{16,18},{18,... | collective-permute-start | bytes 1179656 | tf_op jit(solution)/shard_map/ppermute | solution.py:269
  45.0 4.3 %collective-permute-start.4 = (bf16[8,2,16,768]{3,2,1,0:T(8,128)(2,1)S(1)}, bf16[8,2,16,768]{3,2,1,0:T(8,128)(2,1)S(1)}, u32[]{:S(2)}, u32[]{:S(2)}) collective-permute-start(bf16[8,2,16,768]{3,2,1,0:T(8,128)(2,1)S(1)} %bitcast.20), channel_id=1, source_target_pairs={{0,14},{2,4},{4,2},{6,8},{8,6},{10,12},{12,10},{14,0},{16,30},{18,... | collective-permute-start | bytes 1179656 | tf_op jit(solution)/shard_map/ppermute | solution.py:269
  49.3 0.0 collective-permute-done.1
  49.3 3.8 %collective-permute-start.7 = (bf16[8,2,16,768]{3,2,1,0:T(8,128)(2,1)S(1)}, bf16[8,2,16,768]{3,2,1,0:T(8,128)(2,1)S(1)}, u32[]{:S(2)}, u32[]{:S(2)}) collective-permute-start(bf16[8,2,16,768]{3,2,1,0:T(8,128)(2,1)S(1)} %collective-permute-done.1), channel_id=1, source_target_pairs={{0,4},{2,14},{4,8},{6,2},{8,12},{10,6},{12,0},{14,10},{16,20},{18,... | collective-permute-start | bytes 1179656 | tf_op jit(solution)/shard_map/ppermute | solution.py:269
  53.1 4.8 %collective-permute-start.5 = (bf16[8,2,16,768]{3,2,1,0:T(8,128)(2,1)S(1)}, bf16[8,2,16,768]{3,2,1,0:T(8,128)(2,1)S(1)}, u32[]{:S(2)}, u32[]{:S(2)}) collective-permute-start(bf16[8,2,16,768]{3,2,1,0:T(8,128)(2,1)S(1)} %collective-permute-done.1), channel_id=1, source_target_pairs={{0,2},{2,0},{4,6},{6,4},{8,10},{10,8},{12,14},{14,12},{16,18},{18,... | collective-permute-start | bytes 1179656 | tf_op jit(solution)/shard_map/ppermute | solution.py:269
  58.0 0.0 collective-permute-done.2
  58.0 1.9 %collective-permute-start.6 = (bf16[8,2,16,768]{3,2,1,0:T(8,128)(2,1)S(1)}, bf16[8,2,16,768]{3,2,1,0:T(8,128)(2,1)S(1)}, u32[]{:S(2)}, u32[]{:S(2)}) collective-permute-start(bf16[8,2,16,768]{3,2,1,0:T(8,128)(2,1)S(1)} %collective-permute-done.2), channel_id=1, source_target_pairs={{0,14},{2,4},{4,2},{6,8},{8,6},{10,12},{12,10},{14,0},{16,30},{18,... | collective-permute-start | bytes 1179656 | tf_op jit(solution)/shard_map/ppermute | solution.py:269
  59.9 0.0 collective-permute-done.3
  59.9 0.2 pad_maximum_fusion.refs_0_
  60.1 6.6 %collective-permute-start.9 = (bf16[4,8,2,16,768]{4,3,2,1,0:T(8,128)(2,1)S(1)}, bf16[4,8,2,16,768]{4,3,2,1,0:T(8,128)(2,1)S(1)}, u32[]{:S(2)}, u32[]{:S(2)}) collective-permute-start(bf16[4,8,2,16,768]{4,3,2,1,0:T(8,128)(2,1)S(1)} %pad_maximum_fusion.refs_0_), channel_id=1, source_target_pairs={{0,1},{1,0},{2,3},{3,2},{4,5},{5,4},{6,7},{7,6},{8,9},{9,8},{10,11... | collective-permute-start | bytes 4718600 | tf_op jit(solution)/shard_map/ppermute | solution.py:273
  66.7 0.0 collective-permute-done.4
  66.7 0.0 collective-permute-done.7
  66.7 0.0 collective-permute-done.5
  66.7 1.0 collective-permute-done.6
  67.7 0.2 pad_maximum_fusion.1.refs_1_
  67.9 6.9 %collective-permute-start.8 = (bf16[4,8,2,16,768]{4,3,2,1,0:T(8,128)(2,1)S(1)}, bf16[4,8,2,16,768]{4,3,2,1,0:T(8,128)(2,1)S(1)}, u32[]{:S(2)}, u32[]{:S(2)}) collective-permute-start(bf16[4,8,2,16,768]{4,3,2,1,0:T(8,128)(2,1)S(1)} %pad_maximum_fusion.1.refs_1_), channel_id=1, source_target_pairs={{0,1},{1,0},{2,3},{3,2},{4,5},{5,4},{6,7},{7,6},{8,9},{9,8},{10,11... | collective-permute-start | bytes 4718600 | tf_op jit(solution)/shard_map/ppermute | solution.py:273
  74.8 0.0 collective-permute-done.9
  74.8 1.4 %shard_map.47.refs_3_ = f32[384,768]{1,0:T(8,128)S(1)} custom-call(bf16[4,8,2,16,768]{4,3,2,1,0:T(8,128)(2,1)S(1)} %pad_maximum_fusion.refs_0_, bf16[4,8,2,16,768]{4,3,2,1,0:T(8,128)(2,1)S(1)} %pad_maximum_fusion.1.refs_1_, bf16[1024,768]{1,0:T(8,128)(2,1)S(1)} %bitcast.14), custom_call_target="tpu_custom_call" | custom-call | flops 603979776 | bytes 6291456 | tf_op jit(solution)/shard_map/pallas_call | solution.py:234
  76.2 1.6 %collective-permute-done.8 = bf16[4,8,2,16,768]{4,3,2,1,0:T(8,128)(2,1)S(1)} collective-permute-done((bf16[4,8,2,16,768]{4,3,2,1,0:T(8,128)(2,1)S(1)}, bf16[4,8,2,16,768]{4,3,2,1,0:T(8,128)(2,1)S(1)}, u32[]{:S(2)}, u32[]{:S(2)}) %collective-permute-start.8) | collective-permute-done | bytes 1572896 | tf_op jit(solution)/shard_map/ppermute | solution.py:273
  77.8 1.9 %shard_map.48 = s16[8,304,128]{2,1,0:T(8,128)(2,1)S(1)} custom-call(bf16[4,8,2,16,768]{4,3,2,1,0:T(8,128)(2,1)S(1)} %pad_maximum_fusion.refs_0_, bf16[4,8,2,16,768]{4,3,2,1,0:T(8,128)(2,1)S(1)} %pad_maximum_fusion.1.refs_1_, bf16[1024,768]{1,0:T(8,128)(2,1)S(1)} %bitcast.15, f32[384,768]{1,0:T(8,128)S(1)} %shard_map.47.refs_3_), custom_call_target="tpu_custom_call" | custom-call | flops 603979776 | bytes 6291456 | tf_op jit(solution)/shard_map/pallas_call | solution.py:244
  79.7 25.0 %all_to_all.11.parts_ref = s16[8,304,128]{2,1,0:T(8,128)(2,1)S(1)} all-to-all(s16[8,304,128]{2,1,0:T(8,128)(2,1)S(1)} %shard_map.48), channel_id=1, replica_groups=mesh['y'=8,'x'=8,'z'=8,'c'=2] {'x'}, dimensions={0} | all-to-all | bytes 1245184 | tf_op jit(solution)/shard_map/all_to_all | solution.py:275
  104.7 0.8 shard_map.49
  (1 shorter events, 0.0 us)
Async XLA Ops:
  0.8 0.9 copy-start
  1.7 0.7 copy-start.1
  2.7 17.1 %collective-permute-start = (bf16[8,16,768]{2,1,0:T(8,128)(2,1)S(1)}, bf16[8,16,768]{2,1,0:T(8,128)(2,1)S(1)}, u32[]{:S(2)}, u32[]{:S(2)}) collective-permute-start(bf16[8,16,768]{2,1,0:T(8,128)(2,1)S(1)} %get-tuple-element.8), channel_id=1, source_target_pairs={{0,1},{1,0},{2,3},{3,2},{4,5},{5,4},{6,7},{7,6},{8,9},{9,8},{10,11... | collective-permute-start | bytes 589832 | tf_op jit(solution)/shard_map/ppermute | solution.py:266
  34.1 15.2 %collective-permute-start.1 = (bf16[8,2,16,768]{3,2,1,0:T(8,128)(2,1)S(1)}, bf16[8,2,16,768]{3,2,1,0:T(8,128)(2,1)S(1)}, u32[]{:S(2)}, u32[]{:S(2)}) collective-permute-start(bf16[8,2,16,768]{3,2,1,0:T(8,128)(2,1)S(1)} %bitcast.17), channel_id=1, source_target_pairs={{0,4},{2,14},{4,8},{6,2},{8,12},{10,6},{12,0},{14,10},{16,20},{18,... | collective-permute-start | bytes 1179656 | tf_op jit(solution)/shard_map/ppermute | solution.py:269
  38.5 19.4 %collective-permute-start.2 = (bf16[8,2,16,768]{3,2,1,0:T(8,128)(2,1)S(1)}, bf16[8,2,16,768]{3,2,1,0:T(8,128)(2,1)S(1)}, u32[]{:S(2)}, u32[]{:S(2)}) collective-permute-start(bf16[8,2,16,768]{3,2,1,0:T(8,128)(2,1)S(1)} %bitcast.18), channel_id=1, source_target_pairs={{0,12},{2,6},{4,0},{6,10},{8,4},{10,14},{12,8},{14,2},{16,28},{18,... | collective-permute-start | bytes 1179656 | tf_op jit(solution)/shard_map/ppermute | solution.py:269
  42.6 17.3 %collective-permute-start.3 = (bf16[8,2,16,768]{3,2,1,0:T(8,128)(2,1)S(1)}, bf16[8,2,16,768]{3,2,1,0:T(8,128)(2,1)S(1)}, u32[]{:S(2)}, u32[]{:S(2)}) collective-permute-start(bf16[8,2,16,768]{3,2,1,0:T(8,128)(2,1)S(1)} %bitcast.19), channel_id=1, source_target_pairs={{0,2},{2,0},{4,6},{6,4},{8,10},{10,8},{12,14},{14,12},{16,18},{18,... | collective-permute-start | bytes 1179656 | tf_op jit(solution)/shard_map/ppermute | solution.py:269
  45.0 21.7 %collective-permute-start.4 = (bf16[8,2,16,768]{3,2,1,0:T(8,128)(2,1)S(1)}, bf16[8,2,16,768]{3,2,1,0:T(8,128)(2,1)S(1)}, u32[]{:S(2)}, u32[]{:S(2)}) collective-permute-start(bf16[8,2,16,768]{3,2,1,0:T(8,128)(2,1)S(1)} %bitcast.20), channel_id=1, source_target_pairs={{0,14},{2,4},{4,2},{6,8},{8,6},{10,12},{12,10},{14,0},{16,30},{18,... | collective-permute-start | bytes 1179656 | tf_op jit(solution)/shard_map/ppermute | solution.py:269
  49.3 17.4 %collective-permute-start.7 = (bf16[8,2,16,768]{3,2,1,0:T(8,128)(2,1)S(1)}, bf16[8,2,16,768]{3,2,1,0:T(8,128)(2,1)S(1)}, u32[]{:S(2)}, u32[]{:S(2)}) collective-permute-start(bf16[8,2,16,768]{3,2,1,0:T(8,128)(2,1)S(1)} %collective-permute-done.1), channel_id=1, source_target_pairs={{0,4},{2,14},{4,8},{6,2},{8,12},{10,6},{12,0},{14,10},{16,20},{18,... | collective-permute-start | bytes 1179656 | tf_op jit(solution)/shard_map/ppermute | solution.py:269
  53.1 13.6 %collective-permute-start.5 = (bf16[8,2,16,768]{3,2,1,0:T(8,128)(2,1)S(1)}, bf16[8,2,16,768]{3,2,1,0:T(8,128)(2,1)S(1)}, u32[]{:S(2)}, u32[]{:S(2)}) collective-permute-start(bf16[8,2,16,768]{3,2,1,0:T(8,128)(2,1)S(1)} %collective-permute-done.1), channel_id=1, source_target_pairs={{0,2},{2,0},{4,6},{6,4},{8,10},{10,8},{12,14},{14,12},{16,18},{18,... | collective-permute-start | bytes 1179656 | tf_op jit(solution)/shard_map/ppermute | solution.py:269
  58.0 9.7 %collective-permute-start.6 = (bf16[8,2,16,768]{3,2,1,0:T(8,128)(2,1)S(1)}, bf16[8,2,16,768]{3,2,1,0:T(8,128)(2,1)S(1)}, u32[]{:S(2)}, u32[]{:S(2)}) collective-permute-start(bf16[8,2,16,768]{3,2,1,0:T(8,128)(2,1)S(1)} %collective-permute-done.2), channel_id=1, source_target_pairs={{0,14},{2,4},{4,2},{6,8},{8,6},{10,12},{12,10},{14,0},{16,30},{18,... | collective-permute-start | bytes 1179656 | tf_op jit(solution)/shard_map/ppermute | solution.py:269
  60.1 14.7 %collective-permute-start.9 = (bf16[4,8,2,16,768]{4,3,2,1,0:T(8,128)(2,1)S(1)}, bf16[4,8,2,16,768]{4,3,2,1,0:T(8,128)(2,1)S(1)}, u32[]{:S(2)}, u32[]{:S(2)}) collective-permute-start(bf16[4,8,2,16,768]{4,3,2,1,0:T(8,128)(2,1)S(1)} %pad_maximum_fusion.refs_0_), channel_id=1, source_target_pairs={{0,1},{1,0},{2,3},{3,2},{4,5},{5,4},{6,7},{7,6},{8,9},{9,8},{10,11... | collective-permute-start | bytes 4718600 | tf_op jit(solution)/shard_map/ppermute | solution.py:273
  67.9 9.9 %collective-permute-start.8 = (bf16[4,8,2,16,768]{4,3,2,1,0:T(8,128)(2,1)S(1)}, bf16[4,8,2,16,768]{4,3,2,1,0:T(8,128)(2,1)S(1)}, u32[]{:S(2)}, u32[]{:S(2)}) collective-permute-start(bf16[4,8,2,16,768]{4,3,2,1,0:T(8,128)(2,1)S(1)} %pad_maximum_fusion.1.refs_1_), channel_id=1, source_target_pairs={{0,1},{1,0},{2,3},{3,2},{4,5},{5,4},{6,7},{7,6},{8,9},{9,8},{10,11... | collective-permute-start | bytes 4718600 | tf_op jit(solution)/shard_map/ppermute | solution.py:273

commit v11 on v10

--- a/solution.py
+++ b/solution.py
@@ -14,7 +14,7 @@
 AXES = ("y", "x", "z", "c")
 HALF = 384
 ROWS = 48
-OFFSETS = (0, -2, 2, 1, -1, 3, -3, 4)
+OFFSETS = (0, -2, 2, 4, 1, -1, 3, -3)
 PARTS = ((0, 4), (4, 8))
 STEPS = 14
 VMEM = pl.BlockSpec(memory_space=pltpu.VMEM)

time: 106 us -> 109 us (1.028)
  waiting for transfers between devices: 3.66 us -> 6.29 us
    ppermute x7, waiting for transfers between devices: 1.01 us -> 3.64 us  [per_device(): move = lambda value, step: lax.ppermute(value, AXES, along('z', 'y', step))]
    ppermute x7, starting transfers between devices: 25.7 us -> 27.7 us  [per_device(): move = lambda value, step: lax.ppermute(value, AXES, along('z', 'y', step))]
    ppermute x2, starting transfers between devices: 13.5 us -> 11.6 us  [per_device(): other = [lax.ppermute(part, 'c', swap).reshape(-1, wide) for part in own]]
  transfers between devices with their start and end apart: 10 -> 10, of which waited for: 3 -> 4; matrix products, arithmetic and copies ran while one was open for 0% -> 0% of each run, Pallas kernels for 1% -> 1%
where the time goes in v11:
time: 109 us; the launch traced here: 108 us
  starting transfers between devices  55.4 us (51%)
  blocking collectives  39.3 us (36%)
  waiting for transfers between devices  6.29 us (6%)
  Pallas kernels  4.37 us (4%)
  local copies, waits for them, and re-layouts  1.6 us (1%)
  other arithmetic  1.21 us (1%)
    ppermute x7, starting transfers between devices, per_device(): move = lambda value, step: lax.ppermute(value, AXES, along('z', 'y', step))  27.7 us
    all_to_all x1, blocking collectives, per_device(): parts = lax.all_to_all(messages, 'x', 0, 0, tiled=True)  25 us
    ppermute x1, starting transfers between devices, per_device(): lax.ppermute(send, 'c', swap)  16.1 us
    all_to_all x1, blocking collectives, exchange(): lax.all_to_all(blocks, AXES, 0, 0, tiled=True, axis_index_groups=groups(f...  14.3 us
    ppermute x2, starting transfers between devices, per_device(): other = [lax.ppermute(part, 'c', swap).reshape(-1, wide) for part in own]  11.6 us
    ppermute x7, waiting for transfers between devices, per_device(): move = lambda value, step: lax.ppermute(value, AXES, along('z', 'y', step))  3.64 us
  transfers between devices with their start and end apart: 10, of which 4 were waited for; matrix products, arithmetic and copies ran while one was open for 0% of the time, Pallas kernels for 1%

profile of v11, /device:TPU:1, one launch (start us, length us, event | category | flops | bytes accessed | tf_op | source)
XLA Modules:
  0.0 108.4 jit_solution(3859929631423523292)
XLA Ops:
  0.0 0.8 multiply_bitcast_fusion.limits_ref
  0.8 0.0 copy-start
  0.8 0.9 copy-done
  1.7 0.0 copy-start.1
  1.7 0.7 copy-done.1
  2.4 0.3 shard_map.46
  2.7 16.1 %collective-permute-start = (bf16[8,16,768]{2,1,0:T(8,128)(2,1)S(1)}, bf16[8,16,768]{2,1,0:T(8,128)(2,1)S(1)}, u32[]{:S(2)}, u32[]{:S(2)}) collective-permute-start(bf16[8,16,768]{2,1,0:T(8,128)(2,1)S(1)} %get-tuple-element.8), channel_id=1, source_target_pairs={{0,1},{1,0},{2,3},{3,2},{4,5},{5,4},{6,7},{7,6},{8,9},{9,8},{10,11... | collective-permute-start | bytes 589832 | tf_op jit(solution)/shard_map/ppermute | solution.py:266
  18.7 1.0 collective-permute-done
  19.8 14.3 %all_to_all.10 = bf16[8,32,768]{2,1,0:T(8,128)(2,1)S(1)} all-to-all(bf16[8,32,768]{2,1,0:T(8,128)(2,1)S(1)} %constant_dynamic-update-slice_fusion), channel_id=1, replica_groups={{0,128,256,384,512,640,768,896},{2,130,258,386,514,642,770,898},{4,132,..., dimensions={0} | all-to-all | bytes 786432 | tf_op jit(solution)/shard_map/all_to_all | solution.py:39
  34.1 4.4 %collective-permute-start.1 = (bf16[8,2,16,768]{3,2,1,0:T(8,128)(2,1)S(1)}, bf16[8,2,16,768]{3,2,1,0:T(8,128)(2,1)S(1)}, u32[]{:S(2)}, u32[]{:S(2)}) collective-permute-start(bf16[8,2,16,768]{3,2,1,0:T(8,128)(2,1)S(1)} %bitcast.17), channel_id=1, source_target_pairs={{0,4},{2,14},{4,8},{6,2},{8,12},{10,6},{12,0},{14,10},{16,20},{18,... | collective-permute-start | bytes 1179656 | tf_op jit(solution)/shard_map/ppermute | solution.py:269
  38.5 4.0 %collective-permute-start.2 = (bf16[8,2,16,768]{3,2,1,0:T(8,128)(2,1)S(1)}, bf16[8,2,16,768]{3,2,1,0:T(8,128)(2,1)S(1)}, u32[]{:S(2)}, u32[]{:S(2)}) collective-permute-start(bf16[8,2,16,768]{3,2,1,0:T(8,128)(2,1)S(1)} %bitcast.18), channel_id=1, source_target_pairs={{0,12},{2,6},{4,0},{6,10},{8,4},{10,14},{12,8},{14,2},{16,28},{18,... | collective-permute-start | bytes 1179656 | tf_op jit(solution)/shard_map/ppermute | solution.py:269
  42.6 3.5 %collective-permute-done.1 = bf16[8,2,16,768]{3,2,1,0:T(8,128)(2,1)S(1)} collective-permute-done((bf16[8,2,16,768]{3,2,1,0:T(8,128)(2,1)S(1)}, bf16[8,2,16,768]{3,2,1,0:T(8,128)(2,1)S(1)}, u32[]{:S(2)}, u32[]{:S(2)}) %collective-permute-start.1) | collective-permute-done | bytes 393248 | tf_op jit(solution)/shard_map/ppermute | solution.py:269
  46.1 7.0 %collective-permute-start.3 = (bf16[8,2,16,768]{3,2,1,0:T(8,128)(2,1)S(1)}, bf16[8,2,16,768]{3,2,1,0:T(8,128)(2,1)S(1)}, u32[]{:S(2)}, u32[]{:S(2)}) collective-permute-start(bf16[8,2,16,768]{3,2,1,0:T(8,128)(2,1)S(1)} %collective-permute-done.1), channel_id=1, source_target_pairs={{0,4},{2,14},{4,8},{6,2},{8,12},{10,6},{12,0},{14,10},{16,20},{18,... | collective-permute-start | bytes 1179656 | tf_op jit(solution)/shard_map/ppermute | solution.py:269
  53.1 3.6 %collective-permute-start.5 = (bf16[8,2,16,768]{3,2,1,0:T(8,128)(2,1)S(1)}, bf16[8,2,16,768]{3,2,1,0:T(8,128)(2,1)S(1)}, u32[]{:S(2)}, u32[]{:S(2)}) collective-permute-start(bf16[8,2,16,768]{3,2,1,0:T(8,128)(2,1)S(1)} %bitcast.19), channel_id=1, source_target_pairs={{0,14},{2,4},{4,2},{6,8},{8,6},{10,12},{12,10},{14,0},{16,30},{18,... | collective-permute-start | bytes 1179656 | tf_op jit(solution)/shard_map/ppermute | solution.py:269
  56.8 4.5 %collective-permute-start.4 = (bf16[8,2,16,768]{3,2,1,0:T(8,128)(2,1)S(1)}, bf16[8,2,16,768]{3,2,1,0:T(8,128)(2,1)S(1)}, u32[]{:S(2)}, u32[]{:S(2)}) collective-permute-start(bf16[8,2,16,768]{3,2,1,0:T(8,128)(2,1)S(1)} %bitcast.20), channel_id=1, source_target_pairs={{0,2},{2,0},{4,6},{6,4},{8,10},{10,8},{12,14},{14,12},{16,18},{18,... | collective-permute-start | bytes 1179656 | tf_op jit(solution)/shard_map/ppermute | solution.py:269
  61.3 0.0 collective-permute-done.2
  61.3 1.9 %collective-permute-start.7 = (bf16[8,2,16,768]{3,2,1,0:T(8,128)(2,1)S(1)}, bf16[8,2,16,768]{3,2,1,0:T(8,128)(2,1)S(1)}, u32[]{:S(2)}, u32[]{:S(2)}) collective-permute-start(bf16[8,2,16,768]{3,2,1,0:T(8,128)(2,1)S(1)} %collective-permute-done.2), channel_id=1, source_target_pairs={{0,14},{2,4},{4,2},{6,8},{8,6},{10,12},{12,10},{14,0},{16,30},{18,... | collective-permute-start | bytes 1179656 | tf_op jit(solution)/shard_map/ppermute | solution.py:269
  63.2 2.2 %collective-permute-start.6 = (bf16[8,2,16,768]{3,2,1,0:T(8,128)(2,1)S(1)}, bf16[8,2,16,768]{3,2,1,0:T(8,128)(2,1)S(1)}, u32[]{:S(2)}, u32[]{:S(2)}) collective-permute-start(bf16[8,2,16,768]{3,2,1,0:T(8,128)(2,1)S(1)} %collective-permute-done.1), channel_id=1, source_target_pairs={{0,2},{2,0},{4,6},{6,4},{8,10},{10,8},{12,14},{14,12},{16,18},{18,... | collective-permute-start | bytes 1179656 | tf_op jit(solution)/shard_map/ppermute | solution.py:269
  65.4 0.0 collective-permute-done.3
  65.4 0.2 pad_maximum_fusion.refs_0_
  65.6 6.2 %collective-permute-start.9 = (bf16[4,8,2,16,768]{4,3,2,1,0:T(8,128)(2,1)S(1)}, bf16[4,8,2,16,768]{4,3,2,1,0:T(8,128)(2,1)S(1)}, u32[]{:S(2)}, u32[]{:S(2)}) collective-permute-start(bf16[4,8,2,16,768]{4,3,2,1,0:T(8,128)(2,1)S(1)} %pad_maximum_fusion.refs_0_), channel_id=1, source_target_pairs={{0,1},{1,0},{2,3},{3,2},{4,5},{5,4},{6,7},{7,6},{8,9},{9,8},{10,11... | collective-permute-start | bytes 4718600 | tf_op jit(solution)/shard_map/ppermute | solution.py:273
  71.9 0.0 collective-permute-done.5
  71.9 0.0 collective-permute-done.4
  71.9 0.0 collective-permute-done.7
  71.9 0.1 collective-permute-done.6
  72.0 0.2 pad_maximum_fusion.1.refs_1_
  72.2 5.4 %collective-permute-start.8 = (bf16[4,8,2,16,768]{4,3,2,1,0:T(8,128)(2,1)S(1)}, bf16[4,8,2,16,768]{4,3,2,1,0:T(8,128)(2,1)S(1)}, u32[]{:S(2)}, u32[]{:S(2)}) collective-permute-start(bf16[4,8,2,16,768]{4,3,2,1,0:T(8,128)(2,1)S(1)} %pad_maximum_fusion.1.refs_1_), channel_id=1, source_target_pairs={{0,1},{1,0},{2,3},{3,2},{4,5},{5,4},{6,7},{7,6},{8,9},{9,8},{10,11... | collective-permute-start | bytes 4718600 | tf_op jit(solution)/shard_map/ppermute | solution.py:273
  77.6 0.0 collective-permute-done.9
  77.6 1.4 %shard_map.47.refs_3_ = f32[384,768]{1,0:T(8,128)S(1)} custom-call(bf16[4,8,2,16,768]{4,3,2,1,0:T(8,128)(2,1)S(1)} %pad_maximum_fusion.refs_0_, bf16[4,8,2,16,768]{4,3,2,1,0:T(8,128)(2,1)S(1)} %pad_maximum_fusion.1.refs_1_, bf16[1024,768]{1,0:T(8,128)(2,1)S(1)} %bitcast.14), custom_call_target="tpu_custom_call" | custom-call | flops 603979776 | bytes 6291456 | tf_op jit(solution)/shard_map/pallas_call | solution.py:234
  79.0 1.6 %collective-permute-done.8 = bf16[4,8,2,16,768]{4,3,2,1,0:T(8,128)(2,1)S(1)} collective-permute-done((bf16[4,8,2,16,768]{4,3,2,1,0:T(8,128)(2,1)S(1)}, bf16[4,8,2,16,768]{4,3,2,1,0:T(8,128)(2,1)S(1)}, u32[]{:S(2)}, u32[]{:S(2)}) %collective-permute-start.8) | collective-permute-done | bytes 1572896 | tf_op jit(solution)/shard_map/ppermute | solution.py:273
  80.6 1.9 %shard_map.48 = s16[8,304,128]{2,1,0:T(8,128)(2,1)S(1)} custom-call(bf16[4,8,2,16,768]{4,3,2,1,0:T(8,128)(2,1)S(1)} %pad_maximum_fusion.refs_0_, bf16[4,8,2,16,768]{4,3,2,1,0:T(8,128)(2,1)S(1)} %pad_maximum_fusion.1.refs_1_, bf16[1024,768]{1,0:T(8,128)(2,1)S(1)} %bitcast.15, f32[384,768]{1,0:T(8,128)S(1)} %shard_map.47.refs_3_), custom_call_target="tpu_custom_call" | custom-call | flops 603979776 | bytes 6291456 | tf_op jit(solution)/shard_map/pallas_call | solution.py:244
  82.5 25.0 %all_to_all.11.parts_ref = s16[8,304,128]{2,1,0:T(8,128)(2,1)S(1)} all-to-all(s16[8,304,128]{2,1,0:T(8,128)(2,1)S(1)} %shard_map.48), channel_id=1, replica_groups=mesh['y'=8,'x'=8,'z'=8,'c'=2] {'x'}, dimensions={0} | all-to-all | bytes 1245184 | tf_op jit(solution)/shard_map/all_to_all | solution.py:275
  107.5 0.8 shard_map.49
  (1 shorter events, 0.0 us)
Async XLA Ops:
  0.8 0.9 copy-start
  1.7 0.7 copy-start.1
  2.7 17.1 %collective-permute-start = (bf16[8,16,768]{2,1,0:T(8,128)(2,1)S(1)}, bf16[8,16,768]{2,1,0:T(8,128)(2,1)S(1)}, u32[]{:S(2)}, u32[]{:S(2)}) collective-permute-start(bf16[8,16,768]{2,1,0:T(8,128)(2,1)S(1)} %get-tuple-element.8), channel_id=1, source_target_pairs={{0,1},{1,0},{2,3},{3,2},{4,5},{5,4},{6,7},{7,6},{8,9},{9,8},{10,11... | collective-permute-start | bytes 589832 | tf_op jit(solution)/shard_map/ppermute | solution.py:266
  34.1 12.0 %collective-permute-start.1 = (bf16[8,2,16,768]{3,2,1,0:T(8,128)(2,1)S(1)}, bf16[8,2,16,768]{3,2,1,0:T(8,128)(2,1)S(1)}, u32[]{:S(2)}, u32[]{:S(2)}) collective-permute-start(bf16[8,2,16,768]{3,2,1,0:T(8,128)(2,1)S(1)} %bitcast.17), channel_id=1, source_target_pairs={{0,4},{2,14},{4,8},{6,2},{8,12},{10,6},{12,0},{14,10},{16,20},{18,... | collective-permute-start | bytes 1179656 | tf_op jit(solution)/shard_map/ppermute | solution.py:269
  38.5 22.7 %collective-permute-start.2 = (bf16[8,2,16,768]{3,2,1,0:T(8,128)(2,1)S(1)}, bf16[8,2,16,768]{3,2,1,0:T(8,128)(2,1)S(1)}, u32[]{:S(2)}, u32[]{:S(2)}) collective-permute-start(bf16[8,2,16,768]{3,2,1,0:T(8,128)(2,1)S(1)} %bitcast.18), channel_id=1, source_target_pairs={{0,12},{2,6},{4,0},{6,10},{8,4},{10,14},{12,8},{14,2},{16,28},{18,... | collective-permute-start | bytes 1179656 | tf_op jit(solution)/shard_map/ppermute | solution.py:269
  46.1 19.3 %collective-permute-start.3 = (bf16[8,2,16,768]{3,2,1,0:T(8,128)(2,1)S(1)}, bf16[8,2,16,768]{3,2,1,0:T(8,128)(2,1)S(1)}, u32[]{:S(2)}, u32[]{:S(2)}) collective-permute-start(bf16[8,2,16,768]{3,2,1,0:T(8,128)(2,1)S(1)} %collective-permute-done.1), channel_id=1, source_target_pairs={{0,4},{2,14},{4,8},{6,2},{8,12},{10,6},{12,0},{14,10},{16,20},{18,... | collective-permute-start | bytes 1179656 | tf_op jit(solution)/shard_map/ppermute | solution.py:269
  53.1 18.8 %collective-permute-start.5 = (bf16[8,2,16,768]{3,2,1,0:T(8,128)(2,1)S(1)}, bf16[8,2,16,768]{3,2,1,0:T(8,128)(2,1)S(1)}, u32[]{:S(2)}, u32[]{:S(2)}) collective-permute-start(bf16[8,2,16,768]{3,2,1,0:T(8,128)(2,1)S(1)} %bitcast.19), channel_id=1, source_target_pairs={{0,14},{2,4},{4,2},{6,8},{8,6},{10,12},{12,10},{14,0},{16,30},{18,... | collective-permute-start | bytes 1179656 | tf_op jit(solution)/shard_map/ppermute | solution.py:269
  56.8 15.1 %collective-permute-start.4 = (bf16[8,2,16,768]{3,2,1,0:T(8,128)(2,1)S(1)}, bf16[8,2,16,768]{3,2,1,0:T(8,128)(2,1)S(1)}, u32[]{:S(2)}, u32[]{:S(2)}) collective-permute-start(bf16[8,2,16,768]{3,2,1,0:T(8,128)(2,1)S(1)} %bitcast.20), channel_id=1, source_target_pairs={{0,2},{2,0},{4,6},{6,4},{8,10},{10,8},{12,14},{14,12},{16,18},{18,... | collective-permute-start | bytes 1179656 | tf_op jit(solution)/shard_map/ppermute | solution.py:269
  61.3 10.6 %collective-permute-start.7 = (bf16[8,2,16,768]{3,2,1,0:T(8,128)(2,1)S(1)}, bf16[8,2,16,768]{3,2,1,0:T(8,128)(2,1)S(1)}, u32[]{:S(2)}, u32[]{:S(2)}) collective-permute-start(bf16[8,2,16,768]{3,2,1,0:T(8,128)(2,1)S(1)} %collective-permute-done.2), channel_id=1, source_target_pairs={{0,14},{2,4},{4,2},{6,8},{8,6},{10,12},{12,10},{14,0},{16,30},{18,... | collective-permute-start | bytes 1179656 | tf_op jit(solution)/shard_map/ppermute | solution.py:269
  63.2 8.8 %collective-permute-start.6 = (bf16[8,2,16,768]{3,2,1,0:T(8,128)(2,1)S(1)}, bf16[8,2,16,768]{3,2,1,0:T(8,128)(2,1)S(1)}, u32[]{:S(2)}, u32[]{:S(2)}) collective-permute-start(bf16[8,2,16,768]{3,2,1,0:T(8,128)(2,1)S(1)} %collective-permute-done.1), channel_id=1, source_target_pairs={{0,2},{2,0},{4,6},{6,4},{8,10},{10,8},{12,14},{14,12},{16,18},{18,... | collective-permute-start | bytes 1179656 | tf_op jit(solution)/shard_map/ppermute | solution.py:269
  65.6 12.0 %collective-permute-start.9 = (bf16[4,8,2,16,768]{4,3,2,1,0:T(8,128)(2,1)S(1)}, bf16[4,8,2,16,768]{4,3,2,1,0:T(8,128)(2,1)S(1)}, u32[]{:S(2)}, u32[]{:S(2)}) collective-permute-start(bf16[4,8,2,16,768]{4,3,2,1,0:T(8,128)(2,1)S(1)} %pad_maximum_fusion.refs_0_), channel_id=1, source_target_pairs={{0,1},{1,0},{2,3},{3,2},{4,5},{5,4},{6,7},{7,6},{8,9},{9,8},{10,11... | collective-permute-start | bytes 4718600 | tf_op jit(solution)/shard_map/ppermute | solution.py:273
  72.2 8.4 %collective-permute-start.8 = (bf16[4,8,2,16,768]{4,3,2,1,0:T(8,128)(2,1)S(1)}, bf16[4,8,2,16,768]{4,3,2,1,0:T(8,128)(2,1)S(1)}, u32[]{:S(2)}, u32[]{:S(2)}) collective-permute-start(bf16[4,8,2,16,768]{4,3,2,1,0:T(8,128)(2,1)S(1)} %pad_maximum_fusion.1.refs_1_), channel_id=1, source_target_pairs={{0,1},{1,0},{2,3},{3,2},{4,5},{5,4},{6,7},{7,6},{8,9},{9,8},{10,11... | collective-permute-start | bytes 4718600 | tf_op jit(solution)/shard_map/ppermute | solution.py:273

commit v12 on v11

--- a/solution.py
+++ b/solution.py
@@ -14,7 +14,7 @@
 AXES = ("y", "x", "z", "c")
 HALF = 384
 ROWS = 48
-OFFSETS = (0, -2, 2, 4, 1, -1, 3, -3)
+OFFSETS = (0, -2, 1, -1, 2, 3, -3, 4)
 PARTS = ((0, 4), (4, 8))
 STEPS = 14
 VMEM = pl.BlockSpec(memory_space=pltpu.VMEM)
@@ -267,7 +267,8 @@
     wide = blocks.shape[2]
     blocks = exchange(blocks, "y", "z").reshape(N, 2, rows, wide)
     move = lambda value, step: lax.ppermute(value, AXES, along("z", "y", step))
-    slot = {0: blocks, -2: move(blocks, 2), 2: move(blocks, -2), 1: move(blocks, 1), -1: move(blocks, -1)}
+    slot = {0: blocks, -2: move(blocks, 2), -1: move(blocks, -1), 1: move(blocks, 1)}
+    slot[2] = move(slot[-1], 1)
     slot[4], slot[3], slot[-3] = move(slot[-2], 2), move(slot[-2], 1), move(slot[2], -1)
     own = [jnp.stack([slot[k] for k in OFFSETS[slice(*part)]]) for part in PARTS]
     other = [lax.ppermute(part, "c", swap).reshape(-1, wide) for part in own]

time: 109 us -> 113 us (1.037)
  waiting for transfers between devices: 6.29 us -> 10.5 us
    ppermute x7, starting transfers between devices: 27.7 us -> 23.4 us  [per_device(): move = lambda value, step: lax.ppermute(value, AXES, along('z', 'y', step))]
    ppermute x7, waiting for transfers between devices: 3.64 us -> 7.85 us  [per_device(): move = lambda value, step: lax.ppermute(value, AXES, along('z', 'y', step))]
    ppermute x2, starting transfers between devices: 11.6 us -> 15.7 us  [per_device(): other = [lax.ppermute(part, 'c', swap).reshape(-1, wide) for part in own]]
where the time goes in v12:
time: 113 us; the launch traced here: 112 us
  starting transfers between devices  55.1 us (49%)
  blocking collectives  39.3 us (35%)
  waiting for transfers between devices  10.5 us (9%)
  Pallas kernels  4.37 us (4%)
  local copies, waits for them, and re-layouts  1.6 us (1%)
  other arithmetic  1.21 us (1%)
    all_to_all x1, blocking collectives, per_device(): parts = lax.all_to_all(messages, 'x', 0, 0, tiled=True)  25 us
    ppermute x7, starting transfers between devices, per_device(): move = lambda value, step: lax.ppermute(value, AXES, along('z', 'y', step))  23.4 us
    ppermute x1, starting transfers between devices, per_device(): lax.ppermute(send, 'c', swap)  16.1 us
    ppermute x2, starting transfers between devices, per_device(): other = [lax.ppermute(part, 'c', swap).reshape(-1, wide) for part in own]  15.7 us
    all_to_all x1, blocking collectives, exchange(): lax.all_to_all(blocks, AXES, 0, 0, tiled=True, axis_index_groups=groups(f...  14.3 us
    ppermute x7, waiting for transfers between devices, per_device(): move = lambda value, step: lax.ppermute(value, AXES, along('z', 'y', step))  7.85 us
  transfers between devices with their start and end apart: 10, of which 4 were waited for; matrix products, arithmetic and copies ran while one was open for 0% of the time, Pallas kernels for 1%

profile of v12, /device:TPU:1, one launch (start us, length us, event | category | flops | bytes accessed | tf_op | source)
XLA Modules:
  0.0 112.3 jit_solution(7703393499143716456)
XLA Ops:
  0.0 0.8 multiply_bitcast_fusion.limits_ref
  0.8 0.0 copy-start
  0.8 0.9 copy-done
  1.7 0.0 copy-start.1
  1.7 0.7 copy-done.1
  2.4 0.3 shard_map.46
  2.7 16.1 %collective-permute-start = (bf16[8,16,768]{2,1,0:T(8,128)(2,1)S(1)}, bf16[8,16,768]{2,1,0:T(8,128)(2,1)S(1)}, u32[]{:S(2)}, u32[]{:S(2)}) collective-permute-start(bf16[8,16,768]{2,1,0:T(8,128)(2,1)S(1)} %get-tuple-element.8), channel_id=1, source_target_pairs={{0,1},{1,0},{2,3},{3,2},{4,5},{5,4},{6,7},{7,6},{8,9},{9,8},{10,11... | collective-permute-start | bytes 589832 | tf_op jit(solution)/shard_map/ppermute | solution.py:266
  18.7 1.0 collective-permute-done
  19.8 14.3 %all_to_all.10 = bf16[8,32,768]{2,1,0:T(8,128)(2,1)S(1)} all-to-all(bf16[8,32,768]{2,1,0:T(8,128)(2,1)S(1)} %constant_dynamic-update-slice_fusion), channel_id=1, replica_groups={{0,128,256,384,512,640,768,896},{2,130,258,386,514,642,770,898},{4,132,..., dimensions={0} | all-to-all | bytes 786432 | tf_op jit(solution)/shard_map/all_to_all | solution.py:39
  34.1 5.9 %collective-permute-start.3 = (bf16[8,2,16,768]{3,2,1,0:T(8,128)(2,1)S(1)}, bf16[8,2,16,768]{3,2,1,0:T(8,128)(2,1)S(1)}, u32[]{:S(2)}, u32[]{:S(2)}) collective-permute-start(bf16[8,2,16,768]{3,2,1,0:T(8,128)(2,1)S(1)} %bitcast.17), channel_id=1, source_target_pairs={{0,14},{2,4},{4,2},{6,8},{8,6},{10,12},{12,10},{14,0},{16,30},{18,... | collective-permute-start | bytes 1179656 | tf_op jit(solution)/shard_map/ppermute | solution.py:269
  40.0 1.9 %collective-permute-start.1 = (bf16[8,2,16,768]{3,2,1,0:T(8,128)(2,1)S(1)}, bf16[8,2,16,768]{3,2,1,0:T(8,128)(2,1)S(1)}, u32[]{:S(2)}, u32[]{:S(2)}) collective-permute-start(bf16[8,2,16,768]{3,2,1,0:T(8,128)(2,1)S(1)} %bitcast.18), channel_id=1, source_target_pairs={{0,4},{2,14},{4,8},{6,2},{8,12},{10,6},{12,0},{14,10},{16,20},{18,... | collective-permute-start | bytes 1179656 | tf_op jit(solution)/shard_map/ppermute | solution.py:269
  41.9 7.0 %collective-permute-done.3 = bf16[8,2,16,768]{3,2,1,0:T(8,128)(2,1)S(1)} collective-permute-done((bf16[8,2,16,768]{3,2,1,0:T(8,128)(2,1)S(1)}, bf16[8,2,16,768]{3,2,1,0:T(8,128)(2,1)S(1)}, u32[]{:S(2)}, u32[]{:S(2)}) %collective-permute-start.3) | collective-permute-done | bytes 393248 | tf_op jit(solution)/shard_map/ppermute | solution.py:269
  48.9 1.9 %collective-permute-start.4 = (bf16[8,2,16,768]{3,2,1,0:T(8,128)(2,1)S(1)}, bf16[8,2,16,768]{3,2,1,0:T(8,128)(2,1)S(1)}, u32[]{:S(2)}, u32[]{:S(2)}) collective-permute-start(bf16[8,2,16,768]{3,2,1,0:T(8,128)(2,1)S(1)} %collective-permute-done.3), channel_id=1, source_target_pairs={{0,2},{2,0},{4,6},{6,4},{8,10},{10,8},{12,14},{14,12},{16,18},{18,... | collective-permute-start | bytes 1179656 | tf_op jit(solution)/shard_map/ppermute | solution.py:269
  50.8 3.4 %collective-permute-start.2 = (bf16[8,2,16,768]{3,2,1,0:T(8,128)(2,1)S(1)}, bf16[8,2,16,768]{3,2,1,0:T(8,128)(2,1)S(1)}, u32[]{:S(2)}, u32[]{:S(2)}) collective-permute-start(bf16[8,2,16,768]{3,2,1,0:T(8,128)(2,1)S(1)} %bitcast.19), channel_id=1, source_target_pairs={{0,2},{2,0},{4,6},{6,4},{8,10},{10,8},{12,14},{14,12},{16,18},{18,... | collective-permute-start | bytes 1179656 | tf_op jit(solution)/shard_map/ppermute | solution.py:269
  54.2 0.0 collective-permute-done.1
  54.2 3.0 %collective-permute-start.7 = (bf16[8,2,16,768]{3,2,1,0:T(8,128)(2,1)S(1)}, bf16[8,2,16,768]{3,2,1,0:T(8,128)(2,1)S(1)}, u32[]{:S(2)}, u32[]{:S(2)}) collective-permute-start(bf16[8,2,16,768]{3,2,1,0:T(8,128)(2,1)S(1)} %collective-permute-done.1), channel_id=1, source_target_pairs={{0,4},{2,14},{4,8},{6,2},{8,12},{10,6},{12,0},{14,10},{16,20},{18,... | collective-permute-start | bytes 1179656 | tf_op jit(solution)/shard_map/ppermute | solution.py:269
  57.2 5.4 %collective-permute-start.5 = (bf16[8,2,16,768]{3,2,1,0:T(8,128)(2,1)S(1)}, bf16[8,2,16,768]{3,2,1,0:T(8,128)(2,1)S(1)}, u32[]{:S(2)}, u32[]{:S(2)}) collective-permute-start(bf16[8,2,16,768]{3,2,1,0:T(8,128)(2,1)S(1)} %collective-permute-done.1), channel_id=1, source_target_pairs={{0,2},{2,0},{4,6},{6,4},{8,10},{10,8},{12,14},{14,12},{16,18},{18,... | collective-permute-start | bytes 1179656 | tf_op jit(solution)/shard_map/ppermute | solution.py:269
  62.6 0.0 collective-permute-done.4
  62.6 1.9 %collective-permute-start.6 = (bf16[8,2,16,768]{3,2,1,0:T(8,128)(2,1)S(1)}, bf16[8,2,16,768]{3,2,1,0:T(8,128)(2,1)S(1)}, u32[]{:S(2)}, u32[]{:S(2)}) collective-permute-start(bf16[8,2,16,768]{3,2,1,0:T(8,128)(2,1)S(1)} %collective-permute-done.4), channel_id=1, source_target_pairs={{0,14},{2,4},{4,2},{6,8},{8,6},{10,12},{12,10},{14,0},{16,30},{18,... | collective-permute-start | bytes 1179656 | tf_op jit(solution)/shard_map/ppermute | solution.py:269
  64.6 0.0 collective-permute-done.2
  64.6 0.2 pad_maximum_fusion.refs_0_
  64.8 7.8 %collective-permute-start.9 = (bf16[4,8,2,16,768]{4,3,2,1,0:T(8,128)(2,1)S(1)}, bf16[4,8,2,16,768]{4,3,2,1,0:T(8,128)(2,1)S(1)}, u32[]{:S(2)}, u32[]{:S(2)}) collective-permute-start(bf16[4,8,2,16,768]{4,3,2,1,0:T(8,128)(2,1)S(1)} %pad_maximum_fusion.refs_0_), channel_id=1, source_target_pairs={{0,1},{1,0},{2,3},{3,2},{4,5},{5,4},{6,7},{7,6},{8,9},{9,8},{10,11... | collective-permute-start | bytes 4718600 | tf_op jit(solution)/shard_map/ppermute | solution.py:274
  72.6 0.0 collective-permute-done.7
  72.6 0.0 collective-permute-done.5
  72.6 0.9 collective-permute-done.6
  73.5 0.2 pad_maximum_fusion.1.refs_1_
  73.7 7.9 %collective-permute-start.8 = (bf16[4,8,2,16,768]{4,3,2,1,0:T(8,128)(2,1)S(1)}, bf16[4,8,2,16,768]{4,3,2,1,0:T(8,128)(2,1)S(1)}, u32[]{:S(2)}, u32[]{:S(2)}) collective-permute-start(bf16[4,8,2,16,768]{4,3,2,1,0:T(8,128)(2,1)S(1)} %pad_maximum_fusion.1.refs_1_), channel_id=1, source_target_pairs={{0,1},{1,0},{2,3},{3,2},{4,5},{5,4},{6,7},{7,6},{8,9},{9,8},{10,11... | collective-permute-start | bytes 4718600 | tf_op jit(solution)/shard_map/ppermute | solution.py:274
  81.5 0.0 collective-permute-done.9
  81.5 1.4 %shard_map.47.refs_3_ = f32[384,768]{1,0:T(8,128)S(1)} custom-call(bf16[4,8,2,16,768]{4,3,2,1,0:T(8,128)(2,1)S(1)} %pad_maximum_fusion.refs_0_, bf16[4,8,2,16,768]{4,3,2,1,0:T(8,128)(2,1)S(1)} %pad_maximum_fusion.1.refs_1_, bf16[1024,768]{1,0:T(8,128)(2,1)S(1)} %bitcast.14), custom_call_target="tpu_custom_call" | custom-call | flops 603979776 | bytes 6291456 | tf_op jit(solution)/shard_map/pallas_call | solution.py:234
  83.0 1.6 %collective-permute-done.8 = bf16[4,8,2,16,768]{4,3,2,1,0:T(8,128)(2,1)S(1)} collective-permute-done((bf16[4,8,2,16,768]{4,3,2,1,0:T(8,128)(2,1)S(1)}, bf16[4,8,2,16,768]{4,3,2,1,0:T(8,128)(2,1)S(1)}, u32[]{:S(2)}, u32[]{:S(2)}) %collective-permute-start.8) | collective-permute-done | bytes 1572896 | tf_op jit(solution)/shard_map/ppermute | solution.py:274
  84.6 1.9 %shard_map.48 = s16[8,304,128]{2,1,0:T(8,128)(2,1)S(1)} custom-call(bf16[4,8,2,16,768]{4,3,2,1,0:T(8,128)(2,1)S(1)} %pad_maximum_fusion.refs_0_, bf16[4,8,2,16,768]{4,3,2,1,0:T(8,128)(2,1)S(1)} %pad_maximum_fusion.1.refs_1_, bf16[1024,768]{1,0:T(8,128)(2,1)S(1)} %bitcast.15, f32[384,768]{1,0:T(8,128)S(1)} %shard_map.47.refs_3_), custom_call_target="tpu_custom_call" | custom-call | flops 603979776 | bytes 6291456 | tf_op jit(solution)/shard_map/pallas_call | solution.py:244
  86.4 25.0 %all_to_all.11.parts_ref = s16[8,304,128]{2,1,0:T(8,128)(2,1)S(1)} all-to-all(s16[8,304,128]{2,1,0:T(8,128)(2,1)S(1)} %shard_map.48), channel_id=1, replica_groups=mesh['y'=8,'x'=8,'z'=8,'c'=2] {'x'}, dimensions={0} | all-to-all | bytes 1245184 | tf_op jit(solution)/shard_map/all_to_all | solution.py:276
  111.5 0.8 shard_map.49
  (1 shorter events, 0.0 us)
Async XLA Ops:
  0.8 0.9 copy-start
  1.7 0.7 copy-start.1
  2.7 17.1 %collective-permute-start = (bf16[8,16,768]{2,1,0:T(8,128)(2,1)S(1)}, bf16[8,16,768]{2,1,0:T(8,128)(2,1)S(1)}, u32[]{:S(2)}, u32[]{:S(2)}) collective-permute-start(bf16[8,16,768]{2,1,0:T(8,128)(2,1)S(1)} %get-tuple-element.8), channel_id=1, source_target_pairs={{0,1},{1,0},{2,3},{3,2},{4,5},{5,4},{6,7},{7,6},{8,9},{9,8},{10,11... | collective-permute-start | bytes 589832 | tf_op jit(solution)/shard_map/ppermute | solution.py:266
  34.1 14.8 %collective-permute-start.3 = (bf16[8,2,16,768]{3,2,1,0:T(8,128)(2,1)S(1)}, bf16[8,2,16,768]{3,2,1,0:T(8,128)(2,1)S(1)}, u32[]{:S(2)}, u32[]{:S(2)}) collective-permute-start(bf16[8,2,16,768]{3,2,1,0:T(8,128)(2,1)S(1)} %bitcast.17), channel_id=1, source_target_pairs={{0,14},{2,4},{4,2},{6,8},{8,6},{10,12},{12,10},{14,0},{16,30},{18,... | collective-permute-start | bytes 1179656 | tf_op jit(solution)/shard_map/ppermute | solution.py:269
  40.0 14.2 %collective-permute-start.1 = (bf16[8,2,16,768]{3,2,1,0:T(8,128)(2,1)S(1)}, bf16[8,2,16,768]{3,2,1,0:T(8,128)(2,1)S(1)}, u32[]{:S(2)}, u32[]{:S(2)}) collective-permute-start(bf16[8,2,16,768]{3,2,1,0:T(8,128)(2,1)S(1)} %bitcast.18), channel_id=1, source_target_pairs={{0,4},{2,14},{4,8},{6,2},{8,12},{10,6},{12,0},{14,10},{16,20},{18,... | collective-permute-start | bytes 1179656 | tf_op jit(solution)/shard_map/ppermute | solution.py:269
  48.9 13.7 %collective-permute-start.4 = (bf16[8,2,16,768]{3,2,1,0:T(8,128)(2,1)S(1)}, bf16[8,2,16,768]{3,2,1,0:T(8,128)(2,1)S(1)}, u32[]{:S(2)}, u32[]{:S(2)}) collective-permute-start(bf16[8,2,16,768]{3,2,1,0:T(8,128)(2,1)S(1)} %collective-permute-done.3), channel_id=1, source_target_pairs={{0,2},{2,0},{4,6},{6,4},{8,10},{10,8},{12,14},{14,12},{16,18},{18,... | collective-permute-start | bytes 1179656 | tf_op jit(solution)/shard_map/ppermute | solution.py:269
  50.8 13.7 %collective-permute-start.2 = (bf16[8,2,16,768]{3,2,1,0:T(8,128)(2,1)S(1)}, bf16[8,2,16,768]{3,2,1,0:T(8,128)(2,1)S(1)}, u32[]{:S(2)}, u32[]{:S(2)}) collective-permute-start(bf16[8,2,16,768]{3,2,1,0:T(8,128)(2,1)S(1)} %bitcast.19), channel_id=1, source_target_pairs={{0,2},{2,0},{4,6},{6,4},{8,10},{10,8},{12,14},{14,12},{16,18},{18,... | collective-permute-start | bytes 1179656 | tf_op jit(solution)/shard_map/ppermute | solution.py:269
  54.2 18.4 %collective-permute-start.7 = (bf16[8,2,16,768]{3,2,1,0:T(8,128)(2,1)S(1)}, bf16[8,2,16,768]{3,2,1,0:T(8,128)(2,1)S(1)}, u32[]{:S(2)}, u32[]{:S(2)}) collective-permute-start(bf16[8,2,16,768]{3,2,1,0:T(8,128)(2,1)S(1)} %collective-permute-done.1), channel_id=1, source_target_pairs={{0,4},{2,14},{4,8},{6,2},{8,12},{10,6},{12,0},{14,10},{16,20},{18,... | collective-permute-start | bytes 1179656 | tf_op jit(solution)/shard_map/ppermute | solution.py:269
  57.2 15.4 %collective-permute-start.5 = (bf16[8,2,16,768]{3,2,1,0:T(8,128)(2,1)S(1)}, bf16[8,2,16,768]{3,2,1,0:T(8,128)(2,1)S(1)}, u32[]{:S(2)}, u32[]{:S(2)}) collective-permute-start(bf16[8,2,16,768]{3,2,1,0:T(8,128)(2,1)S(1)} %collective-permute-done.1), channel_id=1, source_target_pairs={{0,2},{2,0},{4,6},{6,4},{8,10},{10,8},{12,14},{14,12},{16,18},{18,... | collective-permute-start | bytes 1179656 | tf_op jit(solution)/shard_map/ppermute | solution.py:269
  62.6 10.8 %collective-permute-start.6 = (bf16[8,2,16,768]{3,2,1,0:T(8,128)(2,1)S(1)}, bf16[8,2,16,768]{3,2,1,0:T(8,128)(2,1)S(1)}, u32[]{:S(2)}, u32[]{:S(2)}) collective-permute-start(bf16[8,2,16,768]{3,2,1,0:T(8,128)(2,1)S(1)} %collective-permute-done.4), channel_id=1, source_target_pairs={{0,14},{2,4},{4,2},{6,8},{8,6},{10,12},{12,10},{14,0},{16,30},{18,... | collective-permute-start | bytes 1179656 | tf_op jit(solution)/shard_map/ppermute | solution.py:269
  64.8 16.8 %collective-permute-start.9 = (bf16[4,8,2,16,768]{4,3,2,1,0:T(8,128)(2,1)S(1)}, bf16[4,8,2,16,768]{4,3,2,1,0:T(8,128)(2,1)S(1)}, u32[]{:S(2)}, u32[]{:S(2)}) collective-permute-start(bf16[4,8,2,16,768]{4,3,2,1,0:T(8,128)(2,1)S(1)} %pad_maximum_fusion.refs_0_), channel_id=1, source_target_pairs={{0,1},{1,0},{2,3},{3,2},{4,5},{5,4},{6,7},{7,6},{8,9},{9,8},{10,11... | collective-permute-start | bytes 4718600 | tf_op jit(solution)/shard_map/ppermute | solution.py:274
  73.7 10.9 %collective-permute-start.8 = (bf16[4,8,2,16,768]{4,3,2,1,0:T(8,128)(2,1)S(1)}, bf16[4,8,2,16,768]{4,3,2,1,0:T(8,128)(2,1)S(1)}, u32[]{:S(2)}, u32[]{:S(2)}) collective-permute-start(bf16[4,8,2,16,768]{4,3,2,1,0:T(8,128)(2,1)S(1)} %pad_maximum_fusion.1.refs_1_), channel_id=1, source_target_pairs={{0,1},{1,0},{2,3},{3,2},{4,5},{5,4},{6,7},{7,6},{8,9},{9,8},{10,11... | collective-permute-start | bytes 4718600 | tf_op jit(solution)/shard_map/ppermute | solution.py:274

commit v13 on v11

--- a/solution.py
+++ b/solution.py
@@ -14,8 +14,8 @@
 AXES = ("y", "x", "z", "c")
 HALF = 384
 ROWS = 48
-OFFSETS = (0, -2, 2, 4, 1, -1, 3, -3)
-PARTS = ((0, 4), (4, 8))
+OFFSETS = (0, -2, 2, 1, -1, 4, 3, -3)
+PARTS = ((0, 3), (3, 6), (6, 8))
 STEPS = 14
 VMEM = pl.BlockSpec(memory_space=pltpu.VMEM)
 SMALL = pltpu.CompilerParams(vmem_limit_bytes=8 * 2**20)
@@ -175,9 +175,10 @@
         sum_ref = out_ref
 
 
-def first_parts_kernel(parts, *refs):
-    own, other, (out_ref, gathered) = refs[: len(PARTS)], refs[len(PARTS) : -2], refs[-2:]
-    contract_parts(parts, own, other, None, out_ref, gathered)
+def early_part_kernel(parts, *refs):
+    *refs, out_ref, gathered = refs
+    own, other, before = refs[: len(PARTS)], refs[len(PARTS) :][: len(parts)], refs[len(PARTS) + len(parts) :]
+    contract_parts(parts, own, other, before[0] if before else None, out_ref, gathered)
 
 
 def last_part_kernel(parts, *refs):
@@ -231,15 +232,19 @@
         transcendentals=0,
     )
     params = pltpu.CompilerParams(vmem_limit_bytes=32 * 2**20)
-    first = pl.pallas_call(
-        functools.partial(first_parts_kernel, early),
-        out_shape=jax.ShapeDtypeStruct((HALF, wide), jnp.float32),
-        in_specs=[VMEM] * (len(PARTS) + len(early)),
-        out_specs=VMEM,
-        scratch_shapes=[gathered(early)],
-        compiler_params=params,
-        cost_estimate=cost(early),
-    )(*own, *[other[p] for p in early])
+    first = []
+    for part in early:
+        first = [
+            pl.pallas_call(
+                functools.partial(early_part_kernel, [part]),
+                out_shape=jax.ShapeDtypeStruct((HALF, wide), jnp.float32),
+                in_specs=[VMEM] * (len(PARTS) + 1 + len(first)),
+                out_specs=VMEM,
+                scratch_shapes=[gathered([part])],
+                compiler_params=params,
+                cost_estimate=cost([part]),
+            )(*own, other[part], *first)
+        ]
     lanes = 128
     return pl.pallas_call(
         functools.partial(last_part_kernel, [last]),
@@ -249,7 +254,7 @@
         scratch_shapes=[gathered([last]), pltpu.VMEM((HALF, wide), jnp.float32)],
         compiler_params=params,
         cost_estimate=cost([last]),
-    )(*own, other[last], first)
+    )(*own, other[last], *first)
 
 
 def along(first, second, step):

time: 109 us -> 109 us (level)
  waiting for transfers between devices: 6.29 us -> 2.58 us
  blocking collectives: 39.3 us -> 40.6 us
  starting transfers between devices: 55.4 us -> 56.7 us
    ppermute x2 -> x3, starting transfers between devices: 11.6 us -> 17.7 us  [per_device(): other = [lax.ppermute(part, 'c', swap).reshape(-1, wide) for part in own]]
    ppermute x7, starting transfers between devices: 27.7 us -> 23 us  [per_device(): move = lambda value, step: lax.ppermute(value, AXES, along('z', 'y', step))]
    ppermute x7, waiting for transfers between devices: 3.64 us -> 1.53 us  [per_device(): move = lambda value, step: lax.ppermute(value, AXES, along('z', 'y', step))]
    ppermute x2 -> x3, waiting for transfers between devices: 1.6 us -> 0.01 us  [per_device(): other = [lax.ppermute(part, 'c', swap).reshape(-1, wide) for part in own]]
    all_to_all x1, blocking collectives: 25 us -> 26.4 us  [per_device(): parts = lax.all_to_all(messages, 'x', 0, 0, tiled=True)]
    pallas_call x1 -> x2, Pallas kernels: 1.4 us -> 2.43 us  [contract(): pl.pallas_call(functools.partial(early_part_kernel, [part]), out_shape=ja...]
  transfers between devices with their start and end apart: 10 -> 11, of which waited for: 4 -> 2; matrix products, arithmetic and copies ran while one was open for 0% -> 0% of each run, Pallas kernels for 1% -> 2%
where the time goes in v13:
time: 109 us; the launch traced here: 108 us
  starting transfers between devices  56.7 us (52%)
  blocking collectives  40.6 us (37%)
  Pallas kernels  5.08 us (5%)
  waiting for transfers between devices  2.58 us (2%)
  local copies, waits for them, and re-layouts  1.6 us (1%)
  other arithmetic  1.15 us (1%)
    all_to_all x1, blocking collectives, per_device(): parts = lax.all_to_all(messages, 'x', 0, 0, tiled=True)  26.4 us
    ppermute x7, starting transfers between devices, per_device(): move = lambda value, step: lax.ppermute(value, AXES, along('z', 'y', step))  23 us
    ppermute x3, starting transfers between devices, per_device(): other = [lax.ppermute(part, 'c', swap).reshape(-1, wide) for part in own]  17.7 us
    ppermute x1, starting transfers between devices, per_device(): lax.ppermute(send, 'c', swap)  16.1 us
    all_to_all x1, blocking collectives, exchange(): lax.all_to_all(blocks, AXES, 0, 0, tiled=True, axis_index_groups=groups(f...  14.3 us
    pallas_call x2, Pallas kernels, contract(): pl.pallas_call(functools.partial(early_part_kernel, [part]), out_shape=ja...  2.43 us
  transfers between devices with their start and end apart: 11, of which 2 were waited for; matrix products, arithmetic and copies ran while one was open for 0% of the time, Pallas kernels for 2%

profile of v13, /device:TPU:1, one launch (start us, length us, event | category | flops | bytes accessed | tf_op | source)
XLA Modules:
  0.0 108.0 jit_solution(2441643530483769532)
XLA Ops:
  0.0 0.8 multiply_bitcast_fusion.limits_ref
  0.8 0.0 copy-start
  0.8 0.9 copy-done
  1.7 0.0 copy-start.1
  1.7 0.7 copy-done.1
  2.4 0.3 shard_map.46
  2.7 16.1 %collective-permute-start = (bf16[8,16,768]{2,1,0:T(8,128)(2,1)S(1)}, bf16[8,16,768]{2,1,0:T(8,128)(2,1)S(1)}, u32[]{:S(2)}, u32[]{:S(2)}) collective-permute-start(bf16[8,16,768]{2,1,0:T(8,128)(2,1)S(1)} %get-tuple-element.8), channel_id=1, source_target_pairs={{0,1},{1,0},{2,3},{3,2},{4,5},{5,4},{6,7},{7,6},{8,9},{9,8},{10,11... | collective-permute-start | bytes 589832 | tf_op jit(solution)/shard_map/ppermute | solution.py:271
  18.7 1.0 collective-permute-done
  19.8 14.3 %all_to_all.10 = bf16[8,32,768]{2,1,0:T(8,128)(2,1)S(1)} all-to-all(bf16[8,32,768]{2,1,0:T(8,128)(2,1)S(1)} %constant_dynamic-update-slice_fusion), channel_id=1, replica_groups={{0,128,256,384,512,640,768,896},{2,130,258,386,514,642,770,898},{4,132,..., dimensions={0} | all-to-all | bytes 786432 | tf_op jit(solution)/shard_map/all_to_all | solution.py:39
  34.1 4.4 %collective-permute-start.1 = (bf16[8,2,16,768]{3,2,1,0:T(8,128)(2,1)S(1)}, bf16[8,2,16,768]{3,2,1,0:T(8,128)(2,1)S(1)}, u32[]{:S(2)}, u32[]{:S(2)}) collective-permute-start(bf16[8,2,16,768]{3,2,1,0:T(8,128)(2,1)S(1)} %bitcast.19), channel_id=1, source_target_pairs={{0,4},{2,14},{4,8},{6,2},{8,12},{10,6},{12,0},{14,10},{16,20},{18,... | collective-permute-start | bytes 1179656 | tf_op jit(solution)/shard_map/ppermute | solution.py:274
  38.5 4.0 %collective-permute-start.2 = (bf16[8,2,16,768]{3,2,1,0:T(8,128)(2,1)S(1)}, bf16[8,2,16,768]{3,2,1,0:T(8,128)(2,1)S(1)}, u32[]{:S(2)}, u32[]{:S(2)}) collective-permute-start(bf16[8,2,16,768]{3,2,1,0:T(8,128)(2,1)S(1)} %bitcast.20), channel_id=1, source_target_pairs={{0,12},{2,6},{4,0},{6,10},{8,4},{10,14},{12,8},{14,2},{16,28},{18,... | collective-permute-start | bytes 1179656 | tf_op jit(solution)/shard_map/ppermute | solution.py:274
  42.6 2.4 %collective-permute-start.3 = (bf16[8,2,16,768]{3,2,1,0:T(8,128)(2,1)S(1)}, bf16[8,2,16,768]{3,2,1,0:T(8,128)(2,1)S(1)}, u32[]{:S(2)}, u32[]{:S(2)}) collective-permute-start(bf16[8,2,16,768]{3,2,1,0:T(8,128)(2,1)S(1)} %bitcast.21), channel_id=1, source_target_pairs={{0,2},{2,0},{4,6},{6,4},{8,10},{10,8},{12,14},{14,12},{16,18},{18,... | collective-permute-start | bytes 1179656 | tf_op jit(solution)/shard_map/ppermute | solution.py:274
  45.0 4.3 %collective-permute-start.4 = (bf16[8,2,16,768]{3,2,1,0:T(8,128)(2,1)S(1)}, bf16[8,2,16,768]{3,2,1,0:T(8,128)(2,1)S(1)}, u32[]{:S(2)}, u32[]{:S(2)}) collective-permute-start(bf16[8,2,16,768]{3,2,1,0:T(8,128)(2,1)S(1)} %bitcast.22), channel_id=1, source_target_pairs={{0,14},{2,4},{4,2},{6,8},{8,6},{10,12},{12,10},{14,0},{16,30},{18,... | collective-permute-start | bytes 1179656 | tf_op jit(solution)/shard_map/ppermute | solution.py:274
  49.3 0.0 collective-permute-done.1
  49.3 3.8 %collective-permute-start.5 = (bf16[8,2,16,768]{3,2,1,0:T(8,128)(2,1)S(1)}, bf16[8,2,16,768]{3,2,1,0:T(8,128)(2,1)S(1)}, u32[]{:S(2)}, u32[]{:S(2)}) collective-permute-start(bf16[8,2,16,768]{3,2,1,0:T(8,128)(2,1)S(1)} %collective-permute-done.1), channel_id=1, source_target_pairs={{0,4},{2,14},{4,8},{6,2},{8,12},{10,6},{12,0},{14,10},{16,20},{18,... | collective-permute-start | bytes 1179656 | tf_op jit(solution)/shard_map/ppermute | solution.py:274
  53.1 0.0 collective-permute-done.2
  53.1 0.1 pad_maximum_fusion.refs_0_
  53.3 4.8 %collective-permute-start.10 = (bf16[3,8,2,16,768]{4,3,2,1,0:T(8,128)(2,1)S(1)}, bf16[3,8,2,16,768]{4,3,2,1,0:T(8,128)(2,1)S(1)}, u32[]{:S(2)}, u32[]{:S(2)}) collective-permute-start(bf16[3,8,2,16,768]{4,3,2,1,0:T(8,128)(2,1)S(1)} %pad_maximum_fusion.refs_0_), channel_id=1, source_target_pairs={{0,1},{1,0},{2,3},{3,2},{4,5},{5,4},{6,7},{7,6},{8,9},{9,8},{10,11... | collective-permute-start | bytes 3538952 | tf_op jit(solution)/shard_map/ppermute | solution.py:278
  58.1 2.1 %collective-permute-start.6 = (bf16[8,2,16,768]{3,2,1,0:T(8,128)(2,1)S(1)}, bf16[8,2,16,768]{3,2,1,0:T(8,128)(2,1)S(1)}, u32[]{:S(2)}, u32[]{:S(2)}) collective-permute-start(bf16[8,2,16,768]{3,2,1,0:T(8,128)(2,1)S(1)} %collective-permute-done.1), channel_id=1, source_target_pairs={{0,2},{2,0},{4,6},{6,4},{8,10},{10,8},{12,14},{14,12},{16,18},{18,... | collective-permute-start | bytes 1179656 | tf_op jit(solution)/shard_map/ppermute | solution.py:274
  60.2 0.0 collective-permute-done.3
  60.2 1.9 %collective-permute-start.7 = (bf16[8,2,16,768]{3,2,1,0:T(8,128)(2,1)S(1)}, bf16[8,2,16,768]{3,2,1,0:T(8,128)(2,1)S(1)}, u32[]{:S(2)}, u32[]{:S(2)}) collective-permute-start(bf16[8,2,16,768]{3,2,1,0:T(8,128)(2,1)S(1)} %collective-permute-done.2), channel_id=1, source_target_pairs={{0,14},{2,4},{4,2},{6,8},{8,6},{10,12},{12,10},{14,0},{16,30},{18,... | collective-permute-start | bytes 1179656 | tf_op jit(solution)/shard_map/ppermute | solution.py:274
  62.1 0.0 collective-permute-done.4
  62.1 0.0 collective-permute-done.5
  62.2 0.1 pad_maximum_fusion.1.refs_1_
  62.3 6.4 %collective-permute-start.9 = (bf16[3,8,2,16,768]{4,3,2,1,0:T(8,128)(2,1)S(1)}, bf16[3,8,2,16,768]{4,3,2,1,0:T(8,128)(2,1)S(1)}, u32[]{:S(2)}, u32[]{:S(2)}) collective-permute-start(bf16[3,8,2,16,768]{4,3,2,1,0:T(8,128)(2,1)S(1)} %pad_maximum_fusion.1.refs_1_), channel_id=1, source_target_pairs={{0,1},{1,0},{2,3},{3,2},{4,5},{5,4},{6,7},{7,6},{8,9},{9,8},{10,11... | collective-permute-start | bytes 3538952 | tf_op jit(solution)/shard_map/ppermute | solution.py:278
  68.7 0.0 collective-permute-done.6
  68.7 1.5 %collective-permute-done.7 = bf16[8,2,16,768]{3,2,1,0:T(8,128)(2,1)S(1)} collective-permute-done((bf16[8,2,16,768]{3,2,1,0:T(8,128)(2,1)S(1)}, bf16[8,2,16,768]{3,2,1,0:T(8,128)(2,1)S(1)}, u32[]{:S(2)}, u32[]{:S(2)}) %collective-permute-start.7) | collective-permute-done | bytes 393248 | tf_op jit(solution)/shard_map/ppermute | solution.py:274
  70.2 0.1 pad_maximum_fusion.2.refs_2_
  70.3 6.5 %collective-permute-start.8 = (bf16[2,8,2,16,768]{4,3,2,1,0:T(8,128)(2,1)S(1)}, bf16[2,8,2,16,768]{4,3,2,1,0:T(8,128)(2,1)S(1)}, u32[]{:S(2)}, u32[]{:S(2)}) collective-permute-start(bf16[2,8,2,16,768]{4,3,2,1,0:T(8,128)(2,1)S(1)} %pad_maximum_fusion.2.refs_2_), channel_id=1, source_target_pairs={{0,1},{1,0},{2,3},{3,2},{4,5},{5,4},{6,7},{7,6},{8,9},{9,8},{10,11... | collective-permute-start | bytes 2359304 | tf_op jit(solution)/shard_map/ppermute | solution.py:278
  76.8 0.0 collective-permute-done.10
  76.8 1.2 %shard_map.47.refs_4_ = f32[384,768]{1,0:T(8,128)S(1)} custom-call(bf16[3,8,2,16,768]{4,3,2,1,0:T(8,128)(2,1)S(1)} %pad_maximum_fusion.refs_0_, bf16[3,8,2,16,768]{4,3,2,1,0:T(8,128)(2,1)S(1)} %pad_maximum_fusion.1.refs_1_, bf16[2,8,2,16,768]{4,3,2,1,0:T(8,128)(2,1)S(1)} %pad_maximum_fusion.2.refs_2_, bf16[768,768]{1,0:T(8,128)(2,1)S(1)} %bitcast.16), custom_call_target="tpu_custom_call" | custom-call | flops 452984832 | bytes 4718592 | tf_op jit(solution)/shard_map/pallas_call | solution.py:238
  78.0 0.0 collective-permute-done.9
  78.0 1.2 %shard_map.48.refs_4_ = f32[384,768]{1,0:T(8,128)S(1)} custom-call(bf16[3,8,2,16,768]{4,3,2,1,0:T(8,128)(2,1)S(1)} %pad_maximum_fusion.refs_0_, bf16[3,8,2,16,768]{4,3,2,1,0:T(8,128)(2,1)S(1)} %pad_maximum_fusion.1.refs_1_, bf16[2,8,2,16,768]{4,3,2,1,0:T(8,128)(2,1)S(1)} %pad_maximum_fusion.2.refs_2_, bf16[768,768]{1,0:T(8,128)(2,1)S(1)} %bitcast.15, ...), custom_call_target="tpu_custom_call" | custom-call | flops 452984832 | bytes 4718592 | tf_op jit(solution)/shard_map/pallas_call | solution.py:238
  79.3 0.0 collective-permute-done.8
  79.3 1.5 %shard_map.49 = s16[8,304,128]{2,1,0:T(8,128)(2,1)S(1)} custom-call(bf16[3,8,2,16,768]{4,3,2,1,0:T(8,128)(2,1)S(1)} %pad_maximum_fusion.refs_0_, bf16[3,8,2,16,768]{4,3,2,1,0:T(8,128)(2,1)S(1)} %pad_maximum_fusion.1.refs_1_, bf16[2,8,2,16,768]{4,3,2,1,0:T(8,128)(2,1)S(1)} %pad_maximum_fusion.2.refs_2_, bf16[512,768]{1,0:T(8,128)(2,1)S(1)} %bitcast.17, ...), custom_call_target="tpu_custom_call" | custom-call | flops 301989888 | bytes 3145728 | tf_op jit(solution)/shard_map/pallas_call | solution.py:249
  80.8 26.4 %all_to_all.11.parts_ref = s16[8,304,128]{2,1,0:T(8,128)(2,1)S(1)} all-to-all(s16[8,304,128]{2,1,0:T(8,128)(2,1)S(1)} %shard_map.49), channel_id=1, replica_groups=mesh['y'=8,'x'=8,'z'=8,'c'=2] {'x'}, dimensions={0} | all-to-all | bytes 1245184 | tf_op jit(solution)/shard_map/all_to_all | solution.py:280
  107.2 0.8 shard_map.50
  (1 shorter events, 0.0 us)
Async XLA Ops:
  0.8 0.9 copy-start
  1.7 0.7 copy-start.1
  2.7 17.1 %collective-permute-start = (bf16[8,16,768]{2,1,0:T(8,128)(2,1)S(1)}, bf16[8,16,768]{2,1,0:T(8,128)(2,1)S(1)}, u32[]{:S(2)}, u32[]{:S(2)}) collective-permute-start(bf16[8,16,768]{2,1,0:T(8,128)(2,1)S(1)} %get-tuple-element.8), channel_id=1, source_target_pairs={{0,1},{1,0},{2,3},{3,2},{4,5},{5,4},{6,7},{7,6},{8,9},{9,8},{10,11... | collective-permute-start | bytes 589832 | tf_op jit(solution)/shard_map/ppermute | solution.py:271
  34.1 15.2 %collective-permute-start.1 = (bf16[8,2,16,768]{3,2,1,0:T(8,128)(2,1)S(1)}, bf16[8,2,16,768]{3,2,1,0:T(8,128)(2,1)S(1)}, u32[]{:S(2)}, u32[]{:S(2)}) collective-permute-start(bf16[8,2,16,768]{3,2,1,0:T(8,128)(2,1)S(1)} %bitcast.19), channel_id=1, source_target_pairs={{0,4},{2,14},{4,8},{6,2},{8,12},{10,6},{12,0},{14,10},{16,20},{18,... | collective-permute-start | bytes 1179656 | tf_op jit(solution)/shard_map/ppermute | solution.py:274
  38.5 14.6 %collective-permute-start.2 = (bf16[8,2,16,768]{3,2,1,0:T(8,128)(2,1)S(1)}, bf16[8,2,16,768]{3,2,1,0:T(8,128)(2,1)S(1)}, u32[]{:S(2)}, u32[]{:S(2)}) collective-permute-start(bf16[8,2,16,768]{3,2,1,0:T(8,128)(2,1)S(1)} %bitcast.20), channel_id=1, source_target_pairs={{0,12},{2,6},{4,0},{6,10},{8,4},{10,14},{12,8},{14,2},{16,28},{18,... | collective-permute-start | bytes 1179656 | tf_op jit(solution)/shard_map/ppermute | solution.py:274
  42.6 17.6 %collective-permute-start.3 = (bf16[8,2,16,768]{3,2,1,0:T(8,128)(2,1)S(1)}, bf16[8,2,16,768]{3,2,1,0:T(8,128)(2,1)S(1)}, u32[]{:S(2)}, u32[]{:S(2)}) collective-permute-start(bf16[8,2,16,768]{3,2,1,0:T(8,128)(2,1)S(1)} %bitcast.21), channel_id=1, source_target_pairs={{0,2},{2,0},{4,6},{6,4},{8,10},{10,8},{12,14},{14,12},{16,18},{18,... | collective-permute-start | bytes 1179656 | tf_op jit(solution)/shard_map/ppermute | solution.py:274
  45.0 17.1 %collective-permute-start.4 = (bf16[8,2,16,768]{3,2,1,0:T(8,128)(2,1)S(1)}, bf16[8,2,16,768]{3,2,1,0:T(8,128)(2,1)S(1)}, u32[]{:S(2)}, u32[]{:S(2)}) collective-permute-start(bf16[8,2,16,768]{3,2,1,0:T(8,128)(2,1)S(1)} %bitcast.22), channel_id=1, source_target_pairs={{0,14},{2,4},{4,2},{6,8},{8,6},{10,12},{12,10},{14,0},{16,30},{18,... | collective-permute-start | bytes 1179656 | tf_op jit(solution)/shard_map/ppermute | solution.py:274
  49.3 12.8 %collective-permute-start.5 = (bf16[8,2,16,768]{3,2,1,0:T(8,128)(2,1)S(1)}, bf16[8,2,16,768]{3,2,1,0:T(8,128)(2,1)S(1)}, u32[]{:S(2)}, u32[]{:S(2)}) collective-permute-start(bf16[8,2,16,768]{3,2,1,0:T(8,128)(2,1)S(1)} %collective-permute-done.1), channel_id=1, source_target_pairs={{0,4},{2,14},{4,8},{6,2},{8,12},{10,6},{12,0},{14,10},{16,20},{18,... | collective-permute-start | bytes 1179656 | tf_op jit(solution)/shard_map/ppermute | solution.py:274
  53.3 23.5 %collective-permute-start.10 = (bf16[3,8,2,16,768]{4,3,2,1,0:T(8,128)(2,1)S(1)}, bf16[3,8,2,16,768]{4,3,2,1,0:T(8,128)(2,1)S(1)}, u32[]{:S(2)}, u32[]{:S(2)}) collective-permute-start(bf16[3,8,2,16,768]{4,3,2,1,0:T(8,128)(2,1)S(1)} %pad_maximum_fusion.refs_0_), channel_id=1, source_target_pairs={{0,1},{1,0},{2,3},{3,2},{4,5},{5,4},{6,7},{7,6},{8,9},{9,8},{10,11... | collective-permute-start | bytes 3538952 | tf_op jit(solution)/shard_map/ppermute | solution.py:278
  58.1 10.6 %collective-permute-start.6 = (bf16[8,2,16,768]{3,2,1,0:T(8,128)(2,1)S(1)}, bf16[8,2,16,768]{3,2,1,0:T(8,128)(2,1)S(1)}, u32[]{:S(2)}, u32[]{:S(2)}) collective-permute-start(bf16[8,2,16,768]{3,2,1,0:T(8,128)(2,1)S(1)} %collective-permute-done.1), channel_id=1, source_target_pairs={{0,2},{2,0},{4,6},{6,4},{8,10},{10,8},{12,14},{14,12},{16,18},{18,... | collective-permute-start | bytes 1179656 | tf_op jit(solution)/shard_map/ppermute | solution.py:274
  60.2 10.0 %collective-permute-start.7 = (bf16[8,2,16,768]{3,2,1,0:T(8,128)(2,1)S(1)}, bf16[8,2,16,768]{3,2,1,0:T(8,128)(2,1)S(1)}, u32[]{:S(2)}, u32[]{:S(2)}) collective-permute-start(bf16[8,2,16,768]{3,2,1,0:T(8,128)(2,1)S(1)} %collective-permute-done.2), channel_id=1, source_target_pairs={{0,14},{2,4},{4,2},{6,8},{8,6},{10,12},{12,10},{14,0},{16,30},{18,... | collective-permute-start | bytes 1179656 | tf_op jit(solution)/shard_map/ppermute | solution.py:274
  62.3 15.7 %collective-permute-start.9 = (bf16[3,8,2,16,768]{4,3,2,1,0:T(8,128)(2,1)S(1)}, bf16[3,8,2,16,768]{4,3,2,1,0:T(8,128)(2,1)S(1)}, u32[]{:S(2)}, u32[]{:S(2)}) collective-permute-start(bf16[3,8,2,16,768]{4,3,2,1,0:T(8,128)(2,1)S(1)} %pad_maximum_fusion.1.refs_1_), channel_id=1, source_target_pairs={{0,1},{1,0},{2,3},{3,2},{4,5},{5,4},{6,7},{7,6},{8,9},{9,8},{10,11... | collective-permute-start | bytes 3538952 | tf_op jit(solution)/shard_map/ppermute | solution.py:278
  70.3 9.0 %collective-permute-start.8 = (bf16[2,8,2,16,768]{4,3,2,1,0:T(8,128)(2,1)S(1)}, bf16[2,8,2,16,768]{4,3,2,1,0:T(8,128)(2,1)S(1)}, u32[]{:S(2)}, u32[]{:S(2)}) collective-permute-start(bf16[2,8,2,16,768]{4,3,2,1,0:T(8,128)(2,1)S(1)} %pad_maximum_fusion.2.refs_2_), channel_id=1, source_target_pairs={{0,1},{1,0},{2,3},{3,2},{4,5},{5,4},{6,7},{7,6},{8,9},{9,8},{10,11... | collective-permute-start | bytes 2359304 | tf_op jit(solution)/shard_map/ppermute | solution.py:278

commit v14 on v10

--- a/solution.py
+++ b/solution.py
@@ -118,12 +118,11 @@
     return lax.rem(place + (1 - 2 * lax.rem(place, 2)) * offset + N, N)
 
 
-def contract_part(own_refs, other_ref, gathered, part, write):
+def gather_part(own_refs, gathered, part):
     places, two, rows, wide = own_refs[0].shape[1:]
     core = lax.axis_index("c")
     mine = jnp.where(core == 0, lax.axis_index("z"), lax.axis_index("y"))
     theirs = jnp.where(core == 0, lax.axis_index("y"), lax.axis_index("z"))
-    tile = 256
 
     def gather(columns):
         for k, offset in enumerate(OFFSETS[slice(*PARTS[part])]):
@@ -135,7 +134,19 @@
                         at = pl.multiple_of(((k * places + place) * two + h) * rows, rows)
                         gathered[pl.ds(at, rows), columns] = own_ref[slot - first, inner, 1 - h, :, columns]
 
-    depth = other_ref.shape[0]
+    @pl.when(core == 0)
+    def _():
+        gather(slice(0, HALF))
+
+    @pl.when(core == 1)
+    def _():
+        gather(slice(0, wide))
+
+
+def contract_part(gathered, other_ref, write):
+    depth, wide = other_ref.shape
+    core = lax.axis_index("c")
+    tile = 256
 
     def run(left_ref, right_ref, columns):
         def column_tile(t, carry):
@@ -155,34 +166,29 @@
 
     @pl.when(core == 0)
     def _():
-        gather(slice(0, HALF))
         run(gathered, other_ref, slice(0, HALF))
 
     @pl.when(core == 1)
     def _():
-        gather(slice(0, wide))
         run(other_ref, gathered, slice(HALF, 2 * HALF))
 
 
-def contract_parts(parts, own_refs, other_refs, sum_ref, out_ref, gathered):
-    for part, other_ref in zip(parts, other_refs):
-
-        def write(start, value, before=sum_ref):
-            columns = pl.ds(start, value.shape[1])
-            out_ref[:, columns] = value if before is None else before[:, columns] + value
-
-        contract_part(own_refs, other_ref, gathered, part, write)
-        sum_ref = out_ref
-
-
-def first_parts_kernel(parts, *refs):
-    own, other, (out_ref, gathered) = refs[: len(PARTS)], refs[len(PARTS) : -2], refs[-2:]
-    contract_parts(parts, own, other, None, out_ref, gathered)
-
-
-def last_part_kernel(parts, *refs):
-    own, other, (first_ref, out_ref, gathered, total) = refs[: len(PARTS)], refs[len(PARTS) : -4], refs[-4:]
-    contract_parts(parts, own, other, first_ref, total, gathered)
+def first_part_kernel(own_0, own_1, other_ref, out_ref, ready_ref, gathered):
+    def write(start, value):
+        out_ref[:, pl.ds(start, value.shape[1])] = value
+
+    own_refs = (own_0, own_1)
+    gather_part(own_refs, gathered, 0)
+    contract_part(gathered, other_ref, write)
+    gather_part(own_refs, ready_ref, 1)
+
+
+def last_part_kernel(ready_ref, other_ref, first_ref, out_ref, total):
+    def write(start, value):
+        columns = pl.ds(start, value.shape[1])
+        total[:, columns] = first_ref[:, columns] + value
+
+    contract_part(ready_ref, other_ref, write)
 
     lanes = out_ref.shape[2]
     tiles = total.shape[1] // lanes
@@ -221,35 +227,31 @@
 
 
 def contract(own, other):
-    wide = own[0].shape[-1]
-    *early, last = range(len(PARTS))
-    depths = [o.shape[0] for o in other]
-    gathered = lambda parts: pltpu.VMEM((max(depths[p] for p in parts), wide), jnp.bfloat16)
-    cost = lambda parts: pl.CostEstimate(
-        flops=2 * sum(depths[p] for p in parts) * wide * HALF,
-        bytes_accessed=8 * sum(depths[p] for p in parts) * wide,
-        transcendentals=0,
-    )
+    depth, wide = other[0].shape
+    cost = pl.CostEstimate(flops=2 * depth * wide * HALF, bytes_accessed=8 * depth * wide, transcendentals=0)
     params = pltpu.CompilerParams(vmem_limit_bytes=32 * 2**20)
-    first = pl.pallas_call(
-        functools.partial(first_parts_kernel, early),
-        out_shape=jax.ShapeDtypeStruct((HALF, wide), jnp.float32),
-        in_specs=[VMEM] * (len(PARTS) + len(early)),
-        out_specs=VMEM,
-        scratch_shapes=[gathered(early)],
+    first, ready = pl.pallas_call(
+        first_part_kernel,
+        out_shape=[
+            jax.ShapeDtypeStruct((HALF, wide), jnp.float32),
+            jax.ShapeDtypeStruct(other[1].shape, jnp.bfloat16),
+        ],
+        in_specs=[VMEM] * 3,
+        out_specs=[VMEM] * 2,
+        scratch_shapes=[pltpu.VMEM((depth, wide), jnp.bfloat16)],
         compiler_params=params,
-        cost_estimate=cost(early),
-    )(*own, *[other[p] for p in early])
+        cost_estimate=cost,
+    )(*own, other[0])
     lanes = 128
     return pl.pallas_call(
-        functools.partial(last_part_kernel, [last]),
+        last_part_kernel,
         out_shape=jax.ShapeDtypeStruct((HALF // ROWS, wide // lanes * ROWS + 16, lanes), jnp.int16),
-        in_specs=[VMEM] * (len(PARTS) + 2),
+        in_specs=[VMEM] * 3,
         out_specs=VMEM,
-        scratch_shapes=[gathered([last]), pltpu.VMEM((HALF, wide), jnp.float32)],
+        scratch_shapes=[pltpu.VMEM((HALF, wide), jnp.float32)],
         compiler_params=params,
-        cost_estimate=cost([last]),
-    )(*own, other[last], first)
+        cost_estimate=cost,
+    )(ready, other[1], first)
 
 
 def along(first, second, step):

time: 106 us -> 106 us (level)
  no operation moved by 1% of the time
where the time goes in v14:
time: 106 us; the launch traced here: 105 us
  starting transfers between devices  55.3 us (52%)
  blocking collectives  39.3 us (37%)
  Pallas kernels  4.41 us (4%)
  waiting for transfers between devices  3.5 us (3%)
  local copies, waits for them, and re-layouts  1.6 us (2%)
  other arithmetic  1.21 us (1%)
    ppermute x7, starting transfers between devices, per_device(): move = lambda value, step: lax.ppermute(value, AXES, along('z', 'y', step))  25.7 us
    all_to_all x1, blocking collectives, per_device(): parts = lax.all_to_all(messages, 'x', 0, 0, tiled=True)  25 us
    ppermute x1, starting transfers between devices, per_device(): lax.ppermute(send, 'c', swap)  16.1 us
    all_to_all x1, blocking collectives, exchange(): lax.all_to_all(blocks, AXES, 0, 0, tiled=True, axis_index_groups=groups(f...  14.3 us
    ppermute x2, starting transfers between devices, per_device(): other = [lax.ppermute(part, 'c', swap).reshape(-1, wide) for part in own]  13.5 us
  transfers between devices with their start and end apart: 10, of which 3 were waited for; matrix products, arithmetic and copies ran while one was open for 0% of the time, Pallas kernels for 1%

profile of v14, /device:TPU:1, one launch (start us, length us, event | category | flops | bytes accessed | tf_op | source)
XLA Modules:
  0.0 105.5 jit_solution(6777428173522482167)
XLA Ops:
  0.0 0.8 multiply_bitcast_fusion.limits_ref
  0.8 0.0 copy-start
  0.8 0.9 copy-done
  1.7 0.0 copy-start.1
  1.7 0.7 copy-done.1
  2.4 0.3 shard_map.46
  2.7 16.1 %collective-permute-start = (bf16[8,16,768]{2,1,0:T(8,128)(2,1)S(1)}, bf16[8,16,768]{2,1,0:T(8,128)(2,1)S(1)}, u32[]{:S(2)}, u32[]{:S(2)}) collective-permute-start(bf16[8,16,768]{2,1,0:T(8,128)(2,1)S(1)} %get-tuple-element.10), channel_id=1, source_target_pairs={{0,1},{1,0},{2,3},{3,2},{4,5},{5,4},{6,7},{7,6},{8,9},{9,8},{10,11... | collective-permute-start | bytes 589832 | tf_op jit(solution)/shard_map/ppermute | solution.py:268
  18.7 1.0 collective-permute-done
  19.8 14.3 %all_to_all.10 = bf16[8,32,768]{2,1,0:T(8,128)(2,1)S(1)} all-to-all(bf16[8,32,768]{2,1,0:T(8,128)(2,1)S(1)} %constant_dynamic-update-slice_fusion), channel_id=1, replica_groups={{0,128,256,384,512,640,768,896},{2,130,258,386,514,642,770,898},{4,132,..., dimensions={0} | all-to-all | bytes 786432 | tf_op jit(solution)/shard_map/all_to_all | solution.py:39
  34.1 4.4 %collective-permute-start.1 = (bf16[8,2,16,768]{3,2,1,0:T(8,128)(2,1)S(1)}, bf16[8,2,16,768]{3,2,1,0:T(8,128)(2,1)S(1)}, u32[]{:S(2)}, u32[]{:S(2)}) collective-permute-start(bf16[8,2,16,768]{3,2,1,0:T(8,128)(2,1)S(1)} %bitcast.17), channel_id=1, source_target_pairs={{0,4},{2,14},{4,8},{6,2},{8,12},{10,6},{12,0},{14,10},{16,20},{18,... | collective-permute-start | bytes 1179656 | tf_op jit(solution)/shard_map/ppermute | solution.py:271
  38.5 4.0 %collective-permute-start.2 = (bf16[8,2,16,768]{3,2,1,0:T(8,128)(2,1)S(1)}, bf16[8,2,16,768]{3,2,1,0:T(8,128)(2,1)S(1)}, u32[]{:S(2)}, u32[]{:S(2)}) collective-permute-start(bf16[8,2,16,768]{3,2,1,0:T(8,128)(2,1)S(1)} %bitcast.18), channel_id=1, source_target_pairs={{0,12},{2,6},{4,0},{6,10},{8,4},{10,14},{12,8},{14,2},{16,28},{18,... | collective-permute-start | bytes 1179656 | tf_op jit(solution)/shard_map/ppermute | solution.py:271
  42.6 2.4 %collective-permute-start.3 = (bf16[8,2,16,768]{3,2,1,0:T(8,128)(2,1)S(1)}, bf16[8,2,16,768]{3,2,1,0:T(8,128)(2,1)S(1)}, u32[]{:S(2)}, u32[]{:S(2)}) collective-permute-start(bf16[8,2,16,768]{3,2,1,0:T(8,128)(2,1)S(1)} %bitcast.19), channel_id=1, source_target_pairs={{0,2},{2,0},{4,6},{6,4},{8,10},{10,8},{12,14},{14,12},{16,18},{18,... | collective-permute-start | bytes 1179656 | tf_op jit(solution)/shard_map/ppermute | solution.py:271
  45.0 4.3 %collective-permute-start.4 = (bf16[8,2,16,768]{3,2,1,0:T(8,128)(2,1)S(1)}, bf16[8,2,16,768]{3,2,1,0:T(8,128)(2,1)S(1)}, u32[]{:S(2)}, u32[]{:S(2)}) collective-permute-start(bf16[8,2,16,768]{3,2,1,0:T(8,128)(2,1)S(1)} %bitcast.20), channel_id=1, source_target_pairs={{0,14},{2,4},{4,2},{6,8},{8,6},{10,12},{12,10},{14,0},{16,30},{18,... | collective-permute-start | bytes 1179656 | tf_op jit(solution)/shard_map/ppermute | solution.py:271
  49.3 0.0 collective-permute-done.1
  49.3 3.8 %collective-permute-start.7 = (bf16[8,2,16,768]{3,2,1,0:T(8,128)(2,1)S(1)}, bf16[8,2,16,768]{3,2,1,0:T(8,128)(2,1)S(1)}, u32[]{:S(2)}, u32[]{:S(2)}) collective-permute-start(bf16[8,2,16,768]{3,2,1,0:T(8,128)(2,1)S(1)} %collective-permute-done.1), channel_id=1, source_target_pairs={{0,4},{2,14},{4,8},{6,2},{8,12},{10,6},{12,0},{14,10},{16,20},{18,... | collective-permute-start | bytes 1179656 | tf_op jit(solution)/shard_map/ppermute | solution.py:271
  53.1 4.8 %collective-permute-start.5 = (bf16[8,2,16,768]{3,2,1,0:T(8,128)(2,1)S(1)}, bf16[8,2,16,768]{3,2,1,0:T(8,128)(2,1)S(1)}, u32[]{:S(2)}, u32[]{:S(2)}) collective-permute-start(bf16[8,2,16,768]{3,2,1,0:T(8,128)(2,1)S(1)} %collective-permute-done.1), channel_id=1, source_target_pairs={{0,2},{2,0},{4,6},{6,4},{8,10},{10,8},{12,14},{14,12},{16,18},{18,... | collective-permute-start | bytes 1179656 | tf_op jit(solution)/shard_map/ppermute | solution.py:271
  58.0 0.0 collective-permute-done.2
  58.0 1.9 %collective-permute-start.6 = (bf16[8,2,16,768]{3,2,1,0:T(8,128)(2,1)S(1)}, bf16[8,2,16,768]{3,2,1,0:T(8,128)(2,1)S(1)}, u32[]{:S(2)}, u32[]{:S(2)}) collective-permute-start(bf16[8,2,16,768]{3,2,1,0:T(8,128)(2,1)S(1)} %collective-permute-done.2), channel_id=1, source_target_pairs={{0,14},{2,4},{4,2},{6,8},{8,6},{10,12},{12,10},{14,0},{16,30},{18,... | collective-permute-start | bytes 1179656 | tf_op jit(solution)/shard_map/ppermute | solution.py:271
  59.9 0.0 collective-permute-done.3
  59.9 0.2 pad_maximum_fusion.own_0
  60.1 6.6 %collective-permute-start.8 = (bf16[4,8,2,16,768]{4,3,2,1,0:T(8,128)(2,1)S(1)}, bf16[4,8,2,16,768]{4,3,2,1,0:T(8,128)(2,1)S(1)}, u32[]{:S(2)}, u32[]{:S(2)}) collective-permute-start(bf16[4,8,2,16,768]{4,3,2,1,0:T(8,128)(2,1)S(1)} %pad_maximum_fusion.own_0), channel_id=1, source_target_pairs={{0,1},{1,0},{2,3},{3,2},{4,5},{5,4},{6,7},{7,6},{8,9},{9,8},{10,11... | collective-permute-start | bytes 4718600 | tf_op jit(solution)/shard_map/ppermute | solution.py:275
  66.7 0.0 collective-permute-done.4
  66.7 0.0 collective-permute-done.7
  66.7 0.0 collective-permute-done.5
  66.7 1.0 collective-permute-done.6
  67.7 0.2 pad_maximum_fusion.1.own_1
  67.9 6.9 %collective-permute-start.9 = (bf16[4,8,2,16,768]{4,3,2,1,0:T(8,128)(2,1)S(1)}, bf16[4,8,2,16,768]{4,3,2,1,0:T(8,128)(2,1)S(1)}, u32[]{:S(2)}, u32[]{:S(2)}) collective-permute-start(bf16[4,8,2,16,768]{4,3,2,1,0:T(8,128)(2,1)S(1)} %pad_maximum_fusion.1.own_1), channel_id=1, source_target_pairs={{0,1},{1,0},{2,3},{3,2},{4,5},{5,4},{6,7},{7,6},{8,9},{9,8},{10,11... | collective-permute-start | bytes 4718600 | tf_op jit(solution)/shard_map/ppermute | solution.py:275
  74.8 0.0 collective-permute-done.8
  74.8 1.6 %shard_map.47 = (f32[384,768]{1,0:T(8,128)S(1)}, bf16[1024,768]{1,0:T(8,128)(2,1)S(1)}) custom-call(bf16[4,8,2,16,768]{4,3,2,1,0:T(8,128)(2,1)S(1)} %pad_maximum_fusion.own_0, bf16[4,8,2,16,768]{4,3,2,1,0:T(8,128)(2,1)S(1)} %pad_maximum_fusion.1.own_1, bf16[1024,768]{1,0:T(8,128)(2,1)S(1)} %bitcast.14), custom_call_target="tpu_custom_call" | custom-call | flops 603979776 | bytes 6291456 | tf_op jit(solution)/shard_map/pallas_call | solution.py:233
  76.4 1.4 %collective-permute-done.9 = bf16[4,8,2,16,768]{4,3,2,1,0:T(8,128)(2,1)S(1)} collective-permute-done((bf16[4,8,2,16,768]{4,3,2,1,0:T(8,128)(2,1)S(1)}, bf16[4,8,2,16,768]{4,3,2,1,0:T(8,128)(2,1)S(1)}, u32[]{:S(2)}, u32[]{:S(2)}) %collective-permute-start.9) | collective-permute-done | bytes 1572896 | tf_op jit(solution)/shard_map/ppermute | solution.py:275
  77.8 1.8 %shard_map.48 = s16[8,304,128]{2,1,0:T(8,128)(2,1)S(1)} custom-call(bf16[1024,768]{1,0:T(8,128)(2,1)S(1)} %get-tuple-element.11.ready_ref, bf16[1024,768]{1,0:T(8,128)(2,1)S(1)} %bitcast.15, f32[384,768]{1,0:T(8,128)S(1)} %get-tuple-element.12.first_ref), custom_call_target="tpu_custom_call" | custom-call | flops 603979776 | bytes 6291456 | tf_op jit(solution)/shard_map/pallas_call | solution.py:246
  79.6 25.0 %all_to_all.11.parts_ref = s16[8,304,128]{2,1,0:T(8,128)(2,1)S(1)} all-to-all(s16[8,304,128]{2,1,0:T(8,128)(2,1)S(1)} %shard_map.48), channel_id=1, replica_groups=mesh['y'=8,'x'=8,'z'=8,'c'=2] {'x'}, dimensions={0} | all-to-all | bytes 1245184 | tf_op jit(solution)/shard_map/all_to_all | solution.py:277
  104.7 0.8 shard_map.49
  (1 shorter events, 0.0 us)
Async XLA Ops:
  0.8 0.9 copy-start
  1.7 0.7 copy-start.1
  2.7 17.1 %collective-permute-start = (bf16[8,16,768]{2,1,0:T(8,128)(2,1)S(1)}, bf16[8,16,768]{2,1,0:T(8,128)(2,1)S(1)}, u32[]{:S(2)}, u32[]{:S(2)}) collective-permute-start(bf16[8,16,768]{2,1,0:T(8,128)(2,1)S(1)} %get-tuple-element.10), channel_id=1, source_target_pairs={{0,1},{1,0},{2,3},{3,2},{4,5},{5,4},{6,7},{7,6},{8,9},{9,8},{10,11... | collective-permute-start | bytes 589832 | tf_op jit(solution)/shard_map/ppermute | solution.py:268
  34.1 15.2 %collective-permute-start.1 = (bf16[8,2,16,768]{3,2,1,0:T(8,128)(2,1)S(1)}, bf16[8,2,16,768]{3,2,1,0:T(8,128)(2,1)S(1)}, u32[]{:S(2)}, u32[]{:S(2)}) collective-permute-start(bf16[8,2,16,768]{3,2,1,0:T(8,128)(2,1)S(1)} %bitcast.17), channel_id=1, source_target_pairs={{0,4},{2,14},{4,8},{6,2},{8,12},{10,6},{12,0},{14,10},{16,20},{18,... | collective-permute-start | bytes 1179656 | tf_op jit(solution)/shard_map/ppermute | solution.py:271
  38.5 19.4 %collective-permute-start.2 = (bf16[8,2,16,768]{3,2,1,0:T(8,128)(2,1)S(1)}, bf16[8,2,16,768]{3,2,1,0:T(8,128)(2,1)S(1)}, u32[]{:S(2)}, u32[]{:S(2)}) collective-permute-start(bf16[8,2,16,768]{3,2,1,0:T(8,128)(2,1)S(1)} %bitcast.18), channel_id=1, source_target_pairs={{0,12},{2,6},{4,0},{6,10},{8,4},{10,14},{12,8},{14,2},{16,28},{18,... | collective-permute-start | bytes 1179656 | tf_op jit(solution)/shard_map/ppermute | solution.py:271
  42.6 17.3 %collective-permute-start.3 = (bf16[8,2,16,768]{3,2,1,0:T(8,128)(2,1)S(1)}, bf16[8,2,16,768]{3,2,1,0:T(8,128)(2,1)S(1)}, u32[]{:S(2)}, u32[]{:S(2)}) collective-permute-start(bf16[8,2,16,768]{3,2,1,0:T(8,128)(2,1)S(1)} %bitcast.19), channel_id=1, source_target_pairs={{0,2},{2,0},{4,6},{6,4},{8,10},{10,8},{12,14},{14,12},{16,18},{18,... | collective-permute-start | bytes 1179656 | tf_op jit(solution)/shard_map/ppermute | solution.py:271
  45.0 21.7 %collective-permute-start.4 = (bf16[8,2,16,768]{3,2,1,0:T(8,128)(2,1)S(1)}, bf16[8,2,16,768]{3,2,1,0:T(8,128)(2,1)S(1)}, u32[]{:S(2)}, u32[]{:S(2)}) collective-permute-start(bf16[8,2,16,768]{3,2,1,0:T(8,128)(2,1)S(1)} %bitcast.20), channel_id=1, source_target_pairs={{0,14},{2,4},{4,2},{6,8},{8,6},{10,12},{12,10},{14,0},{16,30},{18,... | collective-permute-start | bytes 1179656 | tf_op jit(solution)/shard_map/ppermute | solution.py:271
  49.3 17.4 %collective-permute-start.7 = (bf16[8,2,16,768]{3,2,1,0:T(8,128)(2,1)S(1)}, bf16[8,2,16,768]{3,2,1,0:T(8,128)(2,1)S(1)}, u32[]{:S(2)}, u32[]{:S(2)}) collective-permute-start(bf16[8,2,16,768]{3,2,1,0:T(8,128)(2,1)S(1)} %collective-permute-done.1), channel_id=1, source_target_pairs={{0,4},{2,14},{4,8},{6,2},{8,12},{10,6},{12,0},{14,10},{16,20},{18,... | collective-permute-start | bytes 1179656 | tf_op jit(solution)/shard_map/ppermute | solution.py:271
  53.1 13.6 %collective-permute-start.5 = (bf16[8,2,16,768]{3,2,1,0:T(8,128)(2,1)S(1)}, bf16[8,2,16,768]{3,2,1,0:T(8,128)(2,1)S(1)}, u32[]{:S(2)}, u32[]{:S(2)}) collective-permute-start(bf16[8,2,16,768]{3,2,1,0:T(8,128)(2,1)S(1)} %collective-permute-done.1), channel_id=1, source_target_pairs={{0,2},{2,0},{4,6},{6,4},{8,10},{10,8},{12,14},{14,12},{16,18},{18,... | collective-permute-start | bytes 1179656 | tf_op jit(solution)/shard_map/ppermute | solution.py:271
  58.0 9.7 %collective-permute-start.6 = (bf16[8,2,16,768]{3,2,1,0:T(8,128)(2,1)S(1)}, bf16[8,2,16,768]{3,2,1,0:T(8,128)(2,1)S(1)}, u32[]{:S(2)}, u32[]{:S(2)}) collective-permute-start(bf16[8,2,16,768]{3,2,1,0:T(8,128)(2,1)S(1)} %collective-permute-done.2), channel_id=1, source_target_pairs={{0,14},{2,4},{4,2},{6,8},{8,6},{10,12},{12,10},{14,0},{16,30},{18,... | collective-permute-start | bytes 1179656 | tf_op jit(solution)/shard_map/ppermute | solution.py:271
  60.1 14.7 %collective-permute-start.8 = (bf16[4,8,2,16,768]{4,3,2,1,0:T(8,128)(2,1)S(1)}, bf16[4,8,2,16,768]{4,3,2,1,0:T(8,128)(2,1)S(1)}, u32[]{:S(2)}, u32[]{:S(2)}) collective-permute-start(bf16[4,8,2,16,768]{4,3,2,1,0:T(8,128)(2,1)S(1)} %pad_maximum_fusion.own_0), channel_id=1, source_target_pairs={{0,1},{1,0},{2,3},{3,2},{4,5},{5,4},{6,7},{7,6},{8,9},{9,8},{10,11... | collective-permute-start | bytes 4718600 | tf_op jit(solution)/shard_map/ppermute | solution.py:275
  67.9 9.9 %collective-permute-start.9 = (bf16[4,8,2,16,768]{4,3,2,1,0:T(8,128)(2,1)S(1)}, bf16[4,8,2,16,768]{4,3,2,1,0:T(8,128)(2,1)S(1)}, u32[]{:S(2)}, u32[]{:S(2)}) collective-permute-start(bf16[4,8,2,16,768]{4,3,2,1,0:T(8,128)(2,1)S(1)} %pad_maximum_fusion.1.own_1), channel_id=1, source_target_pairs={{0,1},{1,0},{2,3},{3,2},{4,5},{5,4},{6,7},{7,6},{8,9},{9,8},{10,11... | collective-permute-start | bytes 4718600 | tf_op jit(solution)/shard_map/ppermute | solution.py:275

commit v15 on v10

--- a/solution.py
+++ b/solution.py
@@ -203,7 +203,7 @@
         out_ref[d, tiles * ROWS :, :] = exponents.astype(jnp.int16)
         return carry
 
-    lax.fori_loop(0, out_ref.shape[0], message, 0)
+    lax.fori_loop(0, out_ref.shape[0], message, 0, unroll=True)
 
 
 def sum_kernel(parts_ref, out_ref):

time: 106 us -> 106 us (level)
  no operation moved by 1% of the time
where the time goes in v15:
time: 106 us; the launch traced here: 105 us
  starting transfers between devices  55.3 us (52%)
  blocking collectives  39.3 us (37%)
  Pallas kernels  4.26 us (4%)
  waiting for transfers between devices  3.66 us (3%)
  local copies, waits for them, and re-layouts  1.6 us (2%)
  other arithmetic  1.21 us (1%)
    ppermute x7, starting transfers between devices, per_device(): move = lambda value, step: lax.ppermute(value, AXES, along('z', 'y', step))  25.7 us
    all_to_all x1, blocking collectives, per_device(): parts = lax.all_to_all(messages, 'x', 0, 0, tiled=True)  25 us
    ppermute x1, starting transfers between devices, per_device(): lax.ppermute(send, 'c', swap)  16.1 us
    all_to_all x1, blocking collectives, exchange(): lax.all_to_all(blocks, AXES, 0, 0, tiled=True, axis_index_groups=groups(f...  14.3 us
    ppermute x2, starting transfers between devices, per_device(): other = [lax.ppermute(part, 'c', swap).reshape(-1, wide) for part in own]  13.5 us
  transfers between devices with their start and end apart: 10, of which 3 were waited for; matrix products, arithmetic and copies ran while one was open for 0% of the time, Pallas kernels for 1%

profile of v15, /device:TPU:1, one launch (start us, length us, event | category | flops | bytes accessed | tf_op | source)
XLA Modules:
  0.0 105.4 jit_solution(9167157133265203383)
XLA Ops:
  0.0 0.8 multiply_bitcast_fusion.limits_ref
  0.8 0.0 copy-start
  0.8 0.9 copy-done
  1.7 0.0 copy-start.1
  1.7 0.7 copy-done.1
  2.4 0.3 shard_map.46
  2.7 16.1 %collective-permute-start = (bf16[8,16,768]{2,1,0:T(8,128)(2,1)S(1)}, bf16[8,16,768]{2,1,0:T(8,128)(2,1)S(1)}, u32[]{:S(2)}, u32[]{:S(2)}) collective-permute-start(bf16[8,16,768]{2,1,0:T(8,128)(2,1)S(1)} %get-tuple-element.8), channel_id=1, source_target_pairs={{0,1},{1,0},{2,3},{3,2},{4,5},{5,4},{6,7},{7,6},{8,9},{9,8},{10,11... | collective-permute-start | bytes 589832 | tf_op jit(solution)/shard_map/ppermute | solution.py:266
  18.7 1.0 collective-permute-done
  19.8 14.3 %all_to_all.10 = bf16[8,32,768]{2,1,0:T(8,128)(2,1)S(1)} all-to-all(bf16[8,32,768]{2,1,0:T(8,128)(2,1)S(1)} %constant_dynamic-update-slice_fusion), channel_id=1, replica_groups={{0,128,256,384,512,640,768,896},{2,130,258,386,514,642,770,898},{4,132,..., dimensions={0} | all-to-all | bytes 786432 | tf_op jit(solution)/shard_map/all_to_all | solution.py:39
  34.1 4.4 %collective-permute-start.1 = (bf16[8,2,16,768]{3,2,1,0:T(8,128)(2,1)S(1)}, bf16[8,2,16,768]{3,2,1,0:T(8,128)(2,1)S(1)}, u32[]{:S(2)}, u32[]{:S(2)}) collective-permute-start(bf16[8,2,16,768]{3,2,1,0:T(8,128)(2,1)S(1)} %bitcast.17), channel_id=1, source_target_pairs={{0,4},{2,14},{4,8},{6,2},{8,12},{10,6},{12,0},{14,10},{16,20},{18,... | collective-permute-start | bytes 1179656 | tf_op jit(solution)/shard_map/ppermute | solution.py:269
  38.5 4.0 %collective-permute-start.2 = (bf16[8,2,16,768]{3,2,1,0:T(8,128)(2,1)S(1)}, bf16[8,2,16,768]{3,2,1,0:T(8,128)(2,1)S(1)}, u32[]{:S(2)}, u32[]{:S(2)}) collective-permute-start(bf16[8,2,16,768]{3,2,1,0:T(8,128)(2,1)S(1)} %bitcast.18), channel_id=1, source_target_pairs={{0,12},{2,6},{4,0},{6,10},{8,4},{10,14},{12,8},{14,2},{16,28},{18,... | collective-permute-start | bytes 1179656 | tf_op jit(solution)/shard_map/ppermute | solution.py:269
  42.6 2.4 %collective-permute-start.3 = (bf16[8,2,16,768]{3,2,1,0:T(8,128)(2,1)S(1)}, bf16[8,2,16,768]{3,2,1,0:T(8,128)(2,1)S(1)}, u32[]{:S(2)}, u32[]{:S(2)}) collective-permute-start(bf16[8,2,16,768]{3,2,1,0:T(8,128)(2,1)S(1)} %bitcast.19), channel_id=1, source_target_pairs={{0,2},{2,0},{4,6},{6,4},{8,10},{10,8},{12,14},{14,12},{16,18},{18,... | collective-permute-start | bytes 1179656 | tf_op jit(solution)/shard_map/ppermute | solution.py:269
  45.0 4.3 %collective-permute-start.4 = (bf16[8,2,16,768]{3,2,1,0:T(8,128)(2,1)S(1)}, bf16[8,2,16,768]{3,2,1,0:T(8,128)(2,1)S(1)}, u32[]{:S(2)}, u32[]{:S(2)}) collective-permute-start(bf16[8,2,16,768]{3,2,1,0:T(8,128)(2,1)S(1)} %bitcast.20), channel_id=1, source_target_pairs={{0,14},{2,4},{4,2},{6,8},{8,6},{10,12},{12,10},{14,0},{16,30},{18,... | collective-permute-start | bytes 1179656 | tf_op jit(solution)/shard_map/ppermute | solution.py:269
  49.3 0.0 collective-permute-done.1
  49.3 3.8 %collective-permute-start.7 = (bf16[8,2,16,768]{3,2,1,0:T(8,128)(2,1)S(1)}, bf16[8,2,16,768]{3,2,1,0:T(8,128)(2,1)S(1)}, u32[]{:S(2)}, u32[]{:S(2)}) collective-permute-start(bf16[8,2,16,768]{3,2,1,0:T(8,128)(2,1)S(1)} %collective-permute-done.1), channel_id=1, source_target_pairs={{0,4},{2,14},{4,8},{6,2},{8,12},{10,6},{12,0},{14,10},{16,20},{18,... | collective-permute-start | bytes 1179656 | tf_op jit(solution)/shard_map/ppermute | solution.py:269
  53.1 4.8 %collective-permute-start.5 = (bf16[8,2,16,768]{3,2,1,0:T(8,128)(2,1)S(1)}, bf16[8,2,16,768]{3,2,1,0:T(8,128)(2,1)S(1)}, u32[]{:S(2)}, u32[]{:S(2)}) collective-permute-start(bf16[8,2,16,768]{3,2,1,0:T(8,128)(2,1)S(1)} %collective-permute-done.1), channel_id=1, source_target_pairs={{0,2},{2,0},{4,6},{6,4},{8,10},{10,8},{12,14},{14,12},{16,18},{18,... | collective-permute-start | bytes 1179656 | tf_op jit(solution)/shard_map/ppermute | solution.py:269
  58.0 0.0 collective-permute-done.2
  58.0 1.9 %collective-permute-start.6 = (bf16[8,2,16,768]{3,2,1,0:T(8,128)(2,1)S(1)}, bf16[8,2,16,768]{3,2,1,0:T(8,128)(2,1)S(1)}, u32[]{:S(2)}, u32[]{:S(2)}) collective-permute-start(bf16[8,2,16,768]{3,2,1,0:T(8,128)(2,1)S(1)} %collective-permute-done.2), channel_id=1, source_target_pairs={{0,14},{2,4},{4,2},{6,8},{8,6},{10,12},{12,10},{14,0},{16,30},{18,... | collective-permute-start | bytes 1179656 | tf_op jit(solution)/shard_map/ppermute | solution.py:269
  59.9 0.0 collective-permute-done.3
  59.9 0.2 pad_maximum_fusion.refs_0_
  60.1 6.6 %collective-permute-start.9 = (bf16[4,8,2,16,768]{4,3,2,1,0:T(8,128)(2,1)S(1)}, bf16[4,8,2,16,768]{4,3,2,1,0:T(8,128)(2,1)S(1)}, u32[]{:S(2)}, u32[]{:S(2)}) collective-permute-start(bf16[4,8,2,16,768]{4,3,2,1,0:T(8,128)(2,1)S(1)} %pad_maximum_fusion.refs_0_), channel_id=1, source_target_pairs={{0,1},{1,0},{2,3},{3,2},{4,5},{5,4},{6,7},{7,6},{8,9},{9,8},{10,11... | collective-permute-start | bytes 4718600 | tf_op jit(solution)/shard_map/ppermute | solution.py:273
  66.7 0.0 collective-permute-done.4
  66.7 0.0 collective-permute-done.7
  66.7 0.0 collective-permute-done.5
  66.7 1.0 collective-permute-done.6
  67.7 0.2 pad_maximum_fusion.1.refs_1_
  67.9 6.9 %collective-permute-start.8 = (bf16[4,8,2,16,768]{4,3,2,1,0:T(8,128)(2,1)S(1)}, bf16[4,8,2,16,768]{4,3,2,1,0:T(8,128)(2,1)S(1)}, u32[]{:S(2)}, u32[]{:S(2)}) collective-permute-start(bf16[4,8,2,16,768]{4,3,2,1,0:T(8,128)(2,1)S(1)} %pad_maximum_fusion.1.refs_1_), channel_id=1, source_target_pairs={{0,1},{1,0},{2,3},{3,2},{4,5},{5,4},{6,7},{7,6},{8,9},{9,8},{10,11... | collective-permute-start | bytes 4718600 | tf_op jit(solution)/shard_map/ppermute | solution.py:273
  74.8 0.0 collective-permute-done.9
  74.8 1.4 %shard_map.47.refs_3_ = f32[384,768]{1,0:T(8,128)S(1)} custom-call(bf16[4,8,2,16,768]{4,3,2,1,0:T(8,128)(2,1)S(1)} %pad_maximum_fusion.refs_0_, bf16[4,8,2,16,768]{4,3,2,1,0:T(8,128)(2,1)S(1)} %pad_maximum_fusion.1.refs_1_, bf16[1024,768]{1,0:T(8,128)(2,1)S(1)} %bitcast.14), custom_call_target="tpu_custom_call" | custom-call | flops 603979776 | bytes 6291456 | tf_op jit(solution)/shard_map/pallas_call | solution.py:234
  76.2 1.6 %collective-permute-done.8 = bf16[4,8,2,16,768]{4,3,2,1,0:T(8,128)(2,1)S(1)} collective-permute-done((bf16[4,8,2,16,768]{4,3,2,1,0:T(8,128)(2,1)S(1)}, bf16[4,8,2,16,768]{4,3,2,1,0:T(8,128)(2,1)S(1)}, u32[]{:S(2)}, u32[]{:S(2)}) %collective-permute-start.8) | collective-permute-done | bytes 1572896 | tf_op jit(solution)/shard_map/ppermute | solution.py:273
  77.8 1.8 %shard_map.48 = s16[8,304,128]{2,1,0:T(8,128)(2,1)S(1)} custom-call(bf16[4,8,2,16,768]{4,3,2,1,0:T(8,128)(2,1)S(1)} %pad_maximum_fusion.refs_0_, bf16[4,8,2,16,768]{4,3,2,1,0:T(8,128)(2,1)S(1)} %pad_maximum_fusion.1.refs_1_, bf16[1024,768]{1,0:T(8,128)(2,1)S(1)} %bitcast.15, f32[384,768]{1,0:T(8,128)S(1)} %shard_map.47.refs_3_), custom_call_target="tpu_custom_call" | custom-call | flops 603979776 | bytes 6291456 | tf_op jit(solution)/shard_map/pallas_call | solution.py:244
  79.6 25.0 %all_to_all.11.parts_ref = s16[8,304,128]{2,1,0:T(8,128)(2,1)S(1)} all-to-all(s16[8,304,128]{2,1,0:T(8,128)(2,1)S(1)} %shard_map.48), channel_id=1, replica_groups=mesh['y'=8,'x'=8,'z'=8,'c'=2] {'x'}, dimensions={0} | all-to-all | bytes 1245184 | tf_op jit(solution)/shard_map/all_to_all | solution.py:275
  104.6 0.8 shard_map.49
  (1 shorter events, 0.0 us)
Async XLA Ops:
  0.8 0.9 copy-start
  1.7 0.7 copy-start.1
  2.7 17.1 %collective-permute-start = (bf16[8,16,768]{2,1,0:T(8,128)(2,1)S(1)}, bf16[8,16,768]{2,1,0:T(8,128)(2,1)S(1)}, u32[]{:S(2)}, u32[]{:S(2)}) collective-permute-start(bf16[8,16,768]{2,1,0:T(8,128)(2,1)S(1)} %get-tuple-element.8), channel_id=1, source_target_pairs={{0,1},{1,0},{2,3},{3,2},{4,5},{5,4},{6,7},{7,6},{8,9},{9,8},{10,11... | collective-permute-start | bytes 589832 | tf_op jit(solution)/shard_map/ppermute | solution.py:266
  34.1 15.2 %collective-permute-start.1 = (bf16[8,2,16,768]{3,2,1,0:T(8,128)(2,1)S(1)}, bf16[8,2,16,768]{3,2,1,0:T(8,128)(2,1)S(1)}, u32[]{:S(2)}, u32[]{:S(2)}) collective-permute-start(bf16[8,2,16,768]{3,2,1,0:T(8,128)(2,1)S(1)} %bitcast.17), channel_id=1, source_target_pairs={{0,4},{2,14},{4,8},{6,2},{8,12},{10,6},{12,0},{14,10},{16,20},{18,... | collective-permute-start | bytes 1179656 | tf_op jit(solution)/shard_map/ppermute | solution.py:269
  38.5 19.4 %collective-permute-start.2 = (bf16[8,2,16,768]{3,2,1,0:T(8,128)(2,1)S(1)}, bf16[8,2,16,768]{3,2,1,0:T(8,128)(2,1)S(1)}, u32[]{:S(2)}, u32[]{:S(2)}) collective-permute-start(bf16[8,2,16,768]{3,2,1,0:T(8,128)(2,1)S(1)} %bitcast.18), channel_id=1, source_target_pairs={{0,12},{2,6},{4,0},{6,10},{8,4},{10,14},{12,8},{14,2},{16,28},{18,... | collective-permute-start | bytes 1179656 | tf_op jit(solution)/shard_map/ppermute | solution.py:269
  42.6 17.3 %collective-permute-start.3 = (bf16[8,2,16,768]{3,2,1,0:T(8,128)(2,1)S(1)}, bf16[8,2,16,768]{3,2,1,0:T(8,128)(2,1)S(1)}, u32[]{:S(2)}, u32[]{:S(2)}) collective-permute-start(bf16[8,2,16,768]{3,2,1,0:T(8,128)(2,1)S(1)} %bitcast.19), channel_id=1, source_target_pairs={{0,2},{2,0},{4,6},{6,4},{8,10},{10,8},{12,14},{14,12},{16,18},{18,... | collective-permute-start | bytes 1179656 | tf_op jit(solution)/shard_map/ppermute | solution.py:269
  45.0 21.7 %collective-permute-start.4 = (bf16[8,2,16,768]{3,2,1,0:T(8,128)(2,1)S(1)}, bf16[8,2,16,768]{3,2,1,0:T(8,128)(2,1)S(1)}, u32[]{:S(2)}, u32[]{:S(2)}) collective-permute-start(bf16[8,2,16,768]{3,2,1,0:T(8,128)(2,1)S(1)} %bitcast.20), channel_id=1, source_target_pairs={{0,14},{2,4},{4,2},{6,8},{8,6},{10,12},{12,10},{14,0},{16,30},{18,... | collective-permute-start | bytes 1179656 | tf_op jit(solution)/shard_map/ppermute | solution.py:269
  49.3 17.4 %collective-permute-start.7 = (bf16[8,2,16,768]{3,2,1,0:T(8,128)(2,1)S(1)}, bf16[8,2,16,768]{3,2,1,0:T(8,128)(2,1)S(1)}, u32[]{:S(2)}, u32[]{:S(2)}) collective-permute-start(bf16[8,2,16,768]{3,2,1,0:T(8,128)(2,1)S(1)} %collective-permute-done.1), channel_id=1, source_target_pairs={{0,4},{2,14},{4,8},{6,2},{8,12},{10,6},{12,0},{14,10},{16,20},{18,... | collective-permute-start | bytes 1179656 | tf_op jit(solution)/shard_map/ppermute | solution.py:269
  53.1 13.6 %collective-permute-start.5 = (bf16[8,2,16,768]{3,2,1,0:T(8,128)(2,1)S(1)}, bf16[8,2,16,768]{3,2,1,0:T(8,128)(2,1)S(1)}, u32[]{:S(2)}, u32[]{:S(2)}) collective-permute-start(bf16[8,2,16,768]{3,2,1,0:T(8,128)(2,1)S(1)} %collective-permute-done.1), channel_id=1, source_target_pairs={{0,2},{2,0},{4,6},{6,4},{8,10},{10,8},{12,14},{14,12},{16,18},{18,... | collective-permute-start | bytes 1179656 | tf_op jit(solution)/shard_map/ppermute | solution.py:269
  58.0 9.7 %collective-permute-start.6 = (bf16[8,2,16,768]{3,2,1,0:T(8,128)(2,1)S(1)}, bf16[8,2,16,768]{3,2,1,0:T(8,128)(2,1)S(1)}, u32[]{:S(2)}, u32[]{:S(2)}) collective-permute-start(bf16[8,2,16,768]{3,2,1,0:T(8,128)(2,1)S(1)} %collective-permute-done.2), channel_id=1, source_target_pairs={{0,14},{2,4},{4,2},{6,8},{8,6},{10,12},{12,10},{14,0},{16,30},{18,... | collective-permute-start | bytes 1179656 | tf_op jit(solution)/shard_map/ppermute | solution.py:269
  60.1 14.7 %collective-permute-start.9 = (bf16[4,8,2,16,768]{4,3,2,1,0:T(8,128)(2,1)S(1)}, bf16[4,8,2,16,768]{4,3,2,1,0:T(8,128)(2,1)S(1)}, u32[]{:S(2)}, u32[]{:S(2)}) collective-permute-start(bf16[4,8,2,16,768]{4,3,2,1,0:T(8,128)(2,1)S(1)} %pad_maximum_fusion.refs_0_), channel_id=1, source_target_pairs={{0,1},{1,0},{2,3},{3,2},{4,5},{5,4},{6,7},{7,6},{8,9},{9,8},{10,11... | collective-permute-start | bytes 4718600 | tf_op jit(solution)/shard_map/ppermute | solution.py:273
  67.9 9.9 %collective-permute-start.8 = (bf16[4,8,2,16,768]{4,3,2,1,0:T(8,128)(2,1)S(1)}, bf16[4,8,2,16,768]{4,3,2,1,0:T(8,128)(2,1)S(1)}, u32[]{:S(2)}, u32[]{:S(2)}) collective-permute-start(bf16[4,8,2,16,768]{4,3,2,1,0:T(8,128)(2,1)S(1)} %pad_maximum_fusion.1.refs_1_), channel_id=1, source_target_pairs={{0,1},{1,0},{2,3},{3,2},{4,5},{5,4},{6,7},{7,6},{8,9},{9,8},{10,11... | collective-permute-start | bytes 4718600 | tf_op jit(solution)/shard_map/ppermute | solution.py:273
